TPU v7x, 32 devices: a whole 2x2x4 slice. The times are simulated.
32 devices in a mesh: groups: 2 (over y), tiles: 4 (over z), levels: 2 (over x), sub: 2 (over core).
Axes of the slice: x: 2, y: 2, z: 4, core: 2. Of those that a mesh axis runs over, the one named last changes fastest.
Arguments:
- final_adjoint: float32 [6, 18, 16, 720], P('groups', 'levels', 'tiles', 'sub'), parts along dimension 0, may hold values from -6 to 6
- lon_courant: float32 [36, 16, 720], P(('groups', 'levels'), 'tiles', 'sub'), parts along dimension 0, may hold values from 0.02 to 0.24
- lat_courant: float32 [36, 16, 720], P(('groups', 'levels'), 'tiles', 'sub'), parts along dimension 0, may hold values from 0.02 to 0.24
- upwind_flags: int32 [2, 36, 16, 720], P(None, ('groups', 'levels'), 'tiles', 'sub'), parts along dimension 1, may hold values 0 or 1
- vertical_mixing: float32 [36, 16, 720], P(('groups', 'levels'), 'tiles', 'sub'), parts along dimension 0, may hold values from 0.01 to 0.45
- level_profile: float32 [18], P('levels'), may hold values from 0.01 to 0.1
- sounding_owner: int32 [6144, 1], P(('groups', 'tiles', 'sub')), parts along dimension 0, may hold values from 0 to 7; in each aligned block of 384 rows (0 to 383, 384 to 767, ...) at most 128 rows name the same one
- sounding_target: int32 [6144], P(('groups', 'tiles', 'sub')), parts along dimension 0, may hold values from 0 to 8639
- misfit: float32 [3, 6144], P(None, ('groups', 'tiles', 'sub')), parts along dimension 1, may hold values from -6 to 6
- averaging_kernel: float32 [18, 6144], P('levels', ('groups', 'tiles', 'sub')), parts along dimension 1, may hold values from 0.2 to 1.5
Outputs:
- adjoint_state: float32 [6, 18, 16, 720], P('groups', 'levels', 'tiles', 'sub'), parts along dimension 0
- flux_gradient: float32 [6, 16, 720], P('groups', ('tiles', 'levels'), 'sub'), parts along dimension 0
There are 2 independent parts, one for each index of `groups`. A program takes and returns all parts, laid end to end along the dimension named above; an argument that names none is the same for every part. Nothing has to cross between parts.
Inputs may be any that keep to these rules, and one draw needn't show every extreme that they name: `sounding_owner`: in the rows of one device, at most 128 soundings name one owner, a bound that some block reaches of them.
All inputs are finite; a program needn't handle non-finite values. No bound on the sum of `upwind_flags` on one device may be relied on, other than what follows from the above.
Results may differ from a plain program's by a relative error of at most 0.0001.
Values sent between devices are 32-bit elements; how exact they have to be, the bound alone decides.
No kernel may reach another device: no remote copies, remote signals or barrier semaphores. Data moves between devices by JAX's collectives and lax.ppermute only.
A program may use at most 128 MiB of HBM per device.

v0:
```python
import jax
import jax.numpy as jnp
from jax import lax
from jax.sharding import PartitionSpec as P

STEPS = 6
CAP = 128


def shifted(value, axis, steps):
    count = lax.axis_size(axis)
    pairs = [(source, (source + steps) % count) for source in range(count)]
    return lax.ppermute(value, axis, pairs)


def shifted_2(value, axis, steps):
    count = lax.axis_size(axis)
    initial, last = (max(0, -steps), min(count, count - steps))
    return lax.ppermute(value, axis, [(source, source + steps) for source in range(initial, last)])


def with_halo(block, sides, width):
    for axis, dim in sides:
        count = lax.axis_size(axis)
        forward = [(i, i + 1) for i in range(count - 1)]
        forward.append((count - 1, 0))
        backward = [(target, source) for source, target in forward]
        low = lax.ppermute(
            lax.slice_in_dim(block, block.shape[dim] - width, None, axis=dim), axis, forward
        )
        high = lax.ppermute(lax.slice_in_dim(block, 0, width, axis=dim), axis, backward)
        block = jnp.concatenate([low, block, high], axis=dim)
    return block


def per_device(
    final_adjoint,
    lon_courant,
    lat_courant,
    upwind_flags,
    vertical_mixing,
    level_profile,
    sounding_owner,
    sounding_target,
    misfit,
    averaging_kernel,
):
    lev_dev, rows, columns = lon_courant.shape
    tiles_count = lax.axis_size("tiles")
    sub_count = lax.axis_size("sub")
    levels_count = lax.axis_size("levels")
    owners_count = tiles_count * sub_count
    flags = upwind_flags.astype(jnp.float32)
    row_ids = lax.axis_index("tiles") * rows + jnp.arange(rows, dtype=jnp.int32)
    row_open = (row_ids < rows * tiles_count - 1).astype(jnp.float32)[None, :, None]
    level_ids = lax.axis_index("levels") * lev_dev + jnp.arange(lev_dev, dtype=jnp.int32)
    level_open = (level_ids < lev_dev * levels_count - 1).astype(jnp.float32)[:, None, None]
    east = lon_courant * flags[0]
    north = lat_courant * flags[1] * row_open
    upward = vertical_mixing * level_open
    west_source = lon_courant * (1.0 - flags[0])
    south_source = lat_courant * (1.0 - flags[1]) * row_open
    west_edge = shifted(west_source[:, :, -1:], "sub", 1)
    west = jnp.concatenate([west_edge, west_source[:, :, :-1]], axis=2)
    south_edge = shifted_2(south_source[:, -1:, :], "tiles", 1)
    south = jnp.concatenate([south_edge, south_source[:, :-1, :]], axis=1)
    below_edge = shifted_2(upward[-1:], "levels", 1)
    downward = jnp.concatenate([below_edge, upward[:-1]], axis=0)
    owner = sounding_owner[:, 0]
    one_hot = (owner[:, None] == jnp.arange(owners_count, dtype=jnp.int32)[None, :]).astype(
        jnp.int32
    )
    before = jnp.cumsum(one_hot, axis=0) - one_hot
    rank = jnp.sum(before * one_hot, axis=1)
    slots = owner * CAP + rank
    payload = jnp.concatenate([misfit, averaging_kernel], axis=0)
    width = payload.shape[0]
    send_floats = jnp.zeros((width, owners_count * CAP), jnp.float32).at[:, slots].set(payload)
    send_ints = jnp.zeros((1, owners_count * CAP), jnp.int32).at[0, slots].set(sounding_target)
    got_floats, got_ints = (
        lax.all_to_all(
            send_floats.reshape(width, owners_count, CAP),
            ("tiles", "sub"),
            split_axis=1,
            concat_axis=1,
            tiled=True,
        ),
        lax.all_to_all(
            send_ints.reshape(1, owners_count, CAP),
            ("tiles", "sub"),
            split_axis=1,
            concat_axis=1,
            tiled=True,
        ),
    )
    got_floats = got_floats.reshape(width, owners_count * CAP)
    targets = got_ints.reshape(owners_count * CAP)
    tracers = misfit.shape[0]
    contrib = got_floats[:tracers][:, None, :] * got_floats[tracers:][None, :, :]
    cells = rows * columns
    forcing = (
        jnp.zeros((tracers, lev_dev, STEPS * cells), jnp.float32).at[:, :, targets].add(contrib)
    )
    forcing = forcing.reshape(tracers, lev_dev, STEPS, rows, columns)
    coeff_pad = with_halo(jnp.stack([upward, downward]), (("tiles", 2), ("sub", 3)), 1)
    adjoint = final_adjoint
    flux_gradient = jnp.zeros((tracers, rows // levels_count, columns), jnp.float32)
    for step_index in range(STEPS):
        padded = with_halo(adjoint, (("tiles", 2), ("levels", 1), ("sub", 3)), 1)
        centre = padded[:, 1:-1]
        mixed_pad = (
            centre
            + coeff_pad[0] * (padded[:, 2:] - centre)
            + coeff_pad[1] * (padded[:, :-2] - centre)
        )
        mixed = mixed_pad[:, :, 1:-1, 1:-1]
        east_vals = mixed_pad[:, :, 1:-1, 2:]
        west_vals = mixed_pad[:, :, 1:-1, :-2]
        north_vals = mixed_pad[:, :, 2:, 1:-1]
        south_vals = mixed_pad[:, :, :-2, 1:-1]
        moved = mixed + east * (east_vals - mixed) + west * (west_vals - mixed)
        moved = moved + north * (north_vals - mixed) + south * (south_vals - mixed)
        adjoint = moved + forcing[:, :, step_index]
        band_flux = jnp.sum(adjoint * level_profile[None, :, None, None], axis=1)
        flux_gradient = flux_gradient + lax.psum_scatter(
            band_flux, "levels", scatter_dimension=1, tiled=True
        )
    return (adjoint, flux_gradient)


def solution(mesh):
    return jax.shard_map(
        per_device,
        mesh=mesh,
        in_specs=(
            P("groups", "levels", "tiles", "sub"),
            P(("groups", "levels"), "tiles", "sub"),
            P(("groups", "levels"), "tiles", "sub"),
            P(None, ("groups", "levels"), "tiles", "sub"),
            P(("groups", "levels"), "tiles", "sub"),
            P("levels"),
            P(("groups", "tiles", "sub"), None),
            P(("groups", "tiles", "sub")),
            P(None, ("groups", "tiles", "sub")),
            P("levels", ("groups", "tiles", "sub")),
        ),
        out_specs=(P("groups", "levels", "tiles", "sub"), P("groups", ("tiles", "levels"), "sub")),
        check_vma=False,
    )
```

profile of v0, /device:TPU:0, one launch (start us, length us, event | category | flops | bytes accessed | tf_op | source)
XLA Modules:
  0.0 308.2 jit_solution(9869735308682378609)
XLA Ops:
  1.6 4.8 %collective-permute-start.6 = (f32[1,4,360]{2,1,0:T(4,128)S(1)}, f32[1,4,360]{2,1,0:T(4,128)S(1)}, u32[]{:S(2)}, u32[]{:S(2)}) collective-permute-start(f32[1,4,360]{2,1,0:T(4,128)S(1)} %slice.449), channel_id=1, source_target_pairs={{0,2},{1,3},{4,6},{5,7},{8,10},{9,11},{12,14},{13,15},{16,18},{17,... | collective-permute-start | bytes 17288 | tf_op jit(solution)/shard_map/ppermute | solution.py:19
  9.2 2.2 collective-permute-start.1
  14.0 3.6 %scatter_custom_fusion = s32[1024]{0:T(1024)} fusion(s32[384]{0:T(512)S(1)} %fusion.86, s32[384]{0:T(512)} %param.17, s32[]{:T(128)} %constant.10.clone.1), kind=kCustom, calls=%fused_computation.211 | custom fusion | bytes 4608 | tf_op jit(solution)/shard_map/scatter | solution.py:79
  17.7 3.3 %all-to-all-start = ((s32[1,8,128]{2,0,1:T(1,128)}), s32[1,8,128]{2,0,1:T(1,128)S(1)}, u32[]{:S(2)}, u32[]{:S(2)}) async-start(s32[1,8,128]{2,0,1:T(1,128)} %bitcast.10), calls=%async_computation | async-start | bytes 8192 | tf_op jit(solution)/shard_map/all_to_all | solution.py:88
  24.0 3.6 %collective-permute-start.12 = (f32[9,1,360]{2,1,0:T(1,128)S(1)}, f32[9,1,360]{2,1,0:T(1,128)S(1)}, u32[]{:S(2)}, u32[]{:S(2)}) collective-permute-start(f32[9,1,360]{2,1,0:T(1,128)S(1)} %slice.463), channel_id=1, source_target_pairs={{0,4},{4,8},{8,12},{1,5},{5,9},{9,13},{2,6},{6,10},{10,14},{3,7},{... | collective-permute-start | bytes 38888 | tf_op jit(solution)/shard_map/ppermute | solution.py:19
  33.5 2.3 collective-permute-start.8
  35.9 3.4 %all-to-all-start.1 = ((f32[12,8,128]{2,0,1:T(8,128)}), f32[12,8,128]{2,0,1:T(8,128)S(1)}, u32[]{:S(2)}, u32[]{:S(2)}) async-start(f32[12,8,128]{2,0,1:T(8,128)} %copy.35), calls=%async_computation.1 | async-start | bytes 131072 | tf_op jit(solution)/shard_map/all_to_all | solution.py:81
  49.0 4.8 %multiply_bitcast_fusion = f32[1024,3,9]{2,1,0:T(4,128)S(1)} fusion(f32[9,1024]{0,1:T(8,128)S(1)} %bitcast.63, f32[3,1024]{0,1:T(8,128)} %copy.36), kind=kLoop, calls=%fused_computation.3 | loop fusion | flops 27648 | bytes 159744 | tf_op jit(solution)/shard_map/mul | solution.py:99
  53.8 6.4 %broadcast_in_dim.6 = f32[3,9,8640]{1,0,2:T(4,128)} broadcast(f32[]{:T(128)} %constant.9.clone.1), dimensions={} | broadcast | bytes 933124 | tf_op jit(solution)/shard_map/broadcast_in_dim | solution.py:102
  60.2 122.9 %scatter_fusion = f32[3,9,8640]{1,0,2:T(4,128)} fusion(f32[3,9,8640]{1,0,2:T(4,128)} %broadcast_in_dim.6, s32[1024]{0:T(1024)S(1)} %bitcast.67, f32[1024,3,9]{2,1,0:T(4,128)S(1)} %multiply_bitcast_fusion), kind=kCustom, calls=%fused_computation.2 | custom fusion | flops 27648 | bytes 335872 | tf_op jit(solution)/shard_map/scatter-add | solution.py:102
  183.1 12.4 %fusion.88 = (f32[3,9,1,4,360]{1,0,4,3,2:T(4,128)S(1)}, f32[3,9,1,4,360]{1,0,4,3,2:T(4,128)}, f32[3,9,1,4,360]{1,0,4,3,2:T(4,128)}, f32[3,9,1,4,360]{1,0,4,3,2:T...) fusion(f32[3,9,6,4,360]{1,0,4,3,2:T(4,128)} %bitcast.61), kind=kLoop, calls=%fused_computation.217 | loop fusion | bytes 1866240 | tf_op jit(solution)/shard_map/slice | solution.py:123
  195.5 3.6 %copy.49 = f32[3,9,1,4,360]{4,3,1,0,2:T(4,128)} copy(f32[3,9,1,4,360]{1,0,4,3,2:T(4,128)} %get-tuple-element.14) | data formatting | bytes 311040
  199.0 2.3 fusion.73
  201.4 3.8 %collective-permute-start.14 = (f32[3,9,1,360]{3,2,1,0:T(1,128)S(1)}, f32[3,9,1,360]{3,2,1,0:T(1,128)S(1)}, u32[]{:S(2)}, u32[]{:S(2)}) collective-permute-start(f32[3,9,1,360]{3,2,1,0:T(1,128)S(1)} %get-tuple-element.52), channel_id=1, source_target_pairs={{4,0},{8,4},{12,8},{0,12},{5,1},{9,5},{13,9},{1,13},{6,2},{10,6},{... | collective-permute-start | bytes 116648 | tf_op jit(solution)/shard_map/ppermute | solution.py:31
  215.7 3.6 %copy.50 = f32[3,9,1,4,360]{4,3,1,0,2:T(4,128)} copy(f32[3,9,1,4,360]{1,0,4,3,2:T(4,128)} %get-tuple-element.13) | data formatting | bytes 311040
  234.4 3.6 %copy.51 = f32[3,9,1,4,360]{4,3,1,0,2:T(4,128)} copy(f32[3,9,1,4,360]{1,0,4,3,2:T(4,128)} %get-tuple-element.12) | data formatting | bytes 311040
  241.4 3.4 %collective-permute-start.26 = (f32[3,9,1,360]{3,2,1,0:T(1,128)S(1)}, f32[3,9,1,360]{3,2,1,0:T(1,128)S(1)}, u32[]{:S(2)}, u32[]{:S(2)}) collective-permute-start(f32[3,9,1,360]{3,2,1,0:T(1,128)S(1)} %get-tuple-element.48), channel_id=1, source_target_pairs={{4,0},{8,4},{12,8},{0,12},{5,1},{9,5},{13,9},{1,13},{6,2},{10,6},{... | collective-permute-start | bytes 116648 | tf_op jit(solution)/shard_map/ppermute | solution.py:31
  254.0 3.6 %copy.52 = f32[3,9,1,4,360]{4,3,1,0,2:T(4,128)} copy(f32[3,9,1,4,360]{1,0,4,3,2:T(4,128)} %get-tuple-element.11) | data formatting | bytes 311040
  261.6 3.0 collective-permute-start.32
  272.4 3.6 %copy.53 = f32[3,9,1,4,360]{4,3,1,0,2:T(4,128)} copy(f32[3,9,1,4,360]{1,0,4,3,2:T(4,128)} %get-tuple-element.10) | data formatting | bytes 311040
  280.2 2.7 collective-permute-start.38
  294.1 2.3 copy.54
  298.0 2.4 multiply_reduce_fusion.4
  300.4 7.2 %all-reduce.1 = f32[3,4,360]{2,1,0:T(4,128)S(1)} all-reduce(f32[3,4,360]{2,1,0:T(4,128)S(1)} %add_add_fusion), channel_id=7, replica_groups=mesh['groups'=2,'tiles'=4,'levels'=2,'sub'=2] {'levels'}, use_global_device_ids=true, to_apply=%region_7.8.clone | all-reduce | flops 4320 | bytes 34560
  (190 shorter events, 91.7 us)
Async XLA Ops:
  1.6 30.3 %collective-permute-start.6 = (f32[1,4,360]{2,1,0:T(4,128)S(1)}, f32[1,4,360]{2,1,0:T(4,128)S(1)}, u32[]{:S(2)}, u32[]{:S(2)}) collective-permute-start(f32[1,4,360]{2,1,0:T(4,128)S(1)} %slice.449), channel_id=1, source_target_pairs={{0,2},{1,3},{4,6},{5,7},{8,10},{9,11},{12,14},{13,15},{16,18},{17,... | collective-permute-start | bytes 17288 | tf_op jit(solution)/shard_map/ppermute | solution.py:19
  7.5 32.5 %collective-permute-start = (f32[3,9,1,360]{3,2,1,0:T(1,128)S(1)}, f32[3,9,1,360]{3,2,1,0:T(1,128)S(1)}, u32[]{:S(2)}, u32[]{:S(2)}) collective-permute-start(f32[3,9,1,360]{3,2,1,0:T(1,128)S(1)} %get-tuple-element.57), channel_id=1, source_target_pairs={{0,4},{4,8},{8,12},{12,0},{1,5},{5,9},{9,13},{13,1},{2,6},{6,10},{... | collective-permute-start | bytes 116648 | tf_op jit(solution)/shard_map/ppermute | solution.py:28
  9.2 30.9 %collective-permute-start.1 = (f32[3,9,1,360]{3,2,1,0:T(1,128)S(1)}, f32[3,9,1,360]{3,2,1,0:T(1,128)S(1)}, u32[]{:S(2)}, u32[]{:S(2)}) collective-permute-start(f32[3,9,1,360]{3,2,1,0:T(1,128)S(1)} %get-tuple-element.58), channel_id=1, source_target_pairs={{4,0},{8,4},{12,8},{0,12},{5,1},{9,5},{13,9},{1,13},{6,2},{10,6},{... | collective-permute-start | bytes 116648 | tf_op jit(solution)/shard_map/ppermute | solution.py:31
  17.7 18.2 %all-to-all-start = ((s32[1,8,128]{2,0,1:T(1,128)}), s32[1,8,128]{2,0,1:T(1,128)S(1)}, u32[]{:S(2)}, u32[]{:S(2)}) async-start(s32[1,8,128]{2,0,1:T(1,128)} %bitcast.10), calls=%async_computation | async-start | bytes 8192 | tf_op jit(solution)/shard_map/all_to_all | solution.py:88
  23.6 8.2 %collective-permute-start.11 = (f32[9,4,1]{2,1,0:T(4,128)S(1)}, f32[9,4,1]{2,1,0:T(4,128)S(1)}, u32[]{:S(2)}, u32[]{:S(2)}) collective-permute-start(f32[9,4,1]{2,1,0:T(4,128)S(1)} %slice.458), channel_id=1, source_target_pairs={{0,1},{1,0},{2,3},{3,2},{4,5},{5,4},{6,7},{7,6},{8,9},{9,8},{10,11... | collective-permute-start | bytes 440 | tf_op jit(solution)/shard_map/ppermute | solution.py:13
  24.0 15.3 %collective-permute-start.12 = (f32[9,1,360]{2,1,0:T(1,128)S(1)}, f32[9,1,360]{2,1,0:T(1,128)S(1)}, u32[]{:S(2)}, u32[]{:S(2)}) collective-permute-start(f32[9,1,360]{2,1,0:T(1,128)S(1)} %slice.463), channel_id=1, source_target_pairs={{0,4},{4,8},{8,12},{1,5},{5,9},{9,13},{2,6},{6,10},{10,14},{3,7},{... | collective-permute-start | bytes 38888 | tf_op jit(solution)/shard_map/ppermute | solution.py:19
  32.0 7.3 %collective-permute-start.7 = (f32[2,9,1,360]{3,2,1,0:T(1,128)S(1)}, f32[2,9,1,360]{3,2,1,0:T(1,128)S(1)}, u32[]{:S(2)}, u32[]{:S(2)}) collective-permute-start(f32[2,9,1,360]{3,2,1,0:T(1,128)S(1)} %get-tuple-element.61), channel_id=1, source_target_pairs={{0,4},{4,8},{8,12},{12,0},{1,5},{5,9},{9,13},{13,1},{2,6},{6,10},{... | collective-permute-start | bytes 77768 | tf_op jit(solution)/shard_map/ppermute | solution.py:28
  33.5 5.8 %collective-permute-start.8 = (f32[2,9,1,360]{3,2,1,0:T(1,128)S(1)}, f32[2,9,1,360]{3,2,1,0:T(1,128)S(1)}, u32[]{:S(2)}, u32[]{:S(2)}) collective-permute-start(f32[2,9,1,360]{3,2,1,0:T(1,128)S(1)} %get-tuple-element.62), channel_id=1, source_target_pairs={{4,0},{8,4},{12,8},{0,12},{5,1},{9,5},{13,9},{1,13},{6,2},{10,6},{... | collective-permute-start | bytes 77768 | tf_op jit(solution)/shard_map/ppermute | solution.py:31
  35.9 11.9 %all-to-all-start.1 = ((f32[12,8,128]{2,0,1:T(8,128)}), f32[12,8,128]{2,0,1:T(8,128)S(1)}, u32[]{:S(2)}, u32[]{:S(2)}) async-start(f32[12,8,128]{2,0,1:T(8,128)} %copy.35), calls=%async_computation.1 | async-start | bytes 131072 | tf_op jit(solution)/shard_map/all_to_all | solution.py:81
  40.1 4.3 %collective-permute-start.2 = (f32[3,1,6,360]{3,2,1,0:T(8,128)S(1)}, f32[3,1,6,360]{3,2,1,0:T(8,128)S(1)}, u32[]{:S(2)}, u32[]{:S(2)}) collective-permute-start(f32[3,1,6,360]{3,2,1,0:T(8,128)S(1)} %get-tuple-element.37), channel_id=1, source_target_pairs={{0,2},{2,0},{1,3},{3,1},{4,6},{6,4},{5,7},{7,5},{8,10},{10,8},{9,1... | collective-permute-start | bytes 77768 | tf_op jit(solution)/shard_map/ppermute | solution.py:28
  40.2 4.6 %collective-permute-start.3 = (f32[3,1,6,360]{3,2,1,0:T(8,128)S(1)}, f32[3,1,6,360]{3,2,1,0:T(8,128)S(1)}, u32[]{:S(2)}, u32[]{:S(2)}) collective-permute-start(f32[3,1,6,360]{3,2,1,0:T(8,128)S(1)} %get-tuple-element.38), channel_id=1, source_target_pairs={{2,0},{0,2},{3,1},{1,3},{6,4},{4,6},{7,5},{5,7},{10,8},{8,10},{11,... | collective-permute-start | bytes 77768 | tf_op jit(solution)/shard_map/ppermute | solution.py:31
  201.4 5.9 %collective-permute-start.13 = (f32[3,9,1,360]{3,2,1,0:T(1,128)S(1)}, f32[3,9,1,360]{3,2,1,0:T(1,128)S(1)}, u32[]{:S(2)}, u32[]{:S(2)}) collective-permute-start(f32[3,9,1,360]{3,2,1,0:T(1,128)S(1)} %get-tuple-element.51), channel_id=1, source_target_pairs={{0,4},{4,8},{8,12},{12,0},{1,5},{5,9},{9,13},{13,1},{2,6},{6,10},{... | collective-permute-start | bytes 116648 | tf_op jit(solution)/shard_map/ppermute | solution.py:28
  201.4 7.5 %collective-permute-start.14 = (f32[3,9,1,360]{3,2,1,0:T(1,128)S(1)}, f32[3,9,1,360]{3,2,1,0:T(1,128)S(1)}, u32[]{:S(2)}, u32[]{:S(2)}) collective-permute-start(f32[3,9,1,360]{3,2,1,0:T(1,128)S(1)} %get-tuple-element.52), channel_id=1, source_target_pairs={{4,0},{8,4},{12,8},{0,12},{5,1},{9,5},{13,9},{1,13},{6,2},{10,6},{... | collective-permute-start | bytes 116648 | tf_op jit(solution)/shard_map/ppermute | solution.py:31
  222.2 6.0 %collective-permute-start.19 = (f32[3,9,1,360]{3,2,1,0:T(1,128)S(1)}, f32[3,9,1,360]{3,2,1,0:T(1,128)S(1)}, u32[]{:S(2)}, u32[]{:S(2)}) collective-permute-start(f32[3,9,1,360]{3,2,1,0:T(1,128)S(1)} %get-tuple-element.49), channel_id=1, source_target_pairs={{0,4},{4,8},{8,12},{12,0},{1,5},{5,9},{9,13},{13,1},{2,6},{6,10},{... | collective-permute-start | bytes 116648 | tf_op jit(solution)/shard_map/ppermute | solution.py:28
  224.1 4.4 %collective-permute-start.20 = (f32[3,9,1,360]{3,2,1,0:T(1,128)S(1)}, f32[3,9,1,360]{3,2,1,0:T(1,128)S(1)}, u32[]{:S(2)}, u32[]{:S(2)}) collective-permute-start(f32[3,9,1,360]{3,2,1,0:T(1,128)S(1)} %get-tuple-element.50), channel_id=1, source_target_pairs={{4,0},{8,4},{12,8},{0,12},{5,1},{9,5},{13,9},{1,13},{6,2},{10,6},{... | collective-permute-start | bytes 116648 | tf_op jit(solution)/shard_map/ppermute | solution.py:31
  240.9 5.9 %collective-permute-start.25 = (f32[3,9,1,360]{3,2,1,0:T(1,128)S(1)}, f32[3,9,1,360]{3,2,1,0:T(1,128)S(1)}, u32[]{:S(2)}, u32[]{:S(2)}) collective-permute-start(f32[3,9,1,360]{3,2,1,0:T(1,128)S(1)} %get-tuple-element.47), channel_id=1, source_target_pairs={{0,4},{4,8},{8,12},{12,0},{1,5},{5,9},{9,13},{13,1},{2,6},{6,10},{... | collective-permute-start | bytes 116648 | tf_op jit(solution)/shard_map/ppermute | solution.py:28
  241.4 5.4 %collective-permute-start.26 = (f32[3,9,1,360]{3,2,1,0:T(1,128)S(1)}, f32[3,9,1,360]{3,2,1,0:T(1,128)S(1)}, u32[]{:S(2)}, u32[]{:S(2)}) collective-permute-start(f32[3,9,1,360]{3,2,1,0:T(1,128)S(1)} %get-tuple-element.48), channel_id=1, source_target_pairs={{4,0},{8,4},{12,8},{0,12},{5,1},{9,5},{13,9},{1,13},{6,2},{10,6},{... | collective-permute-start | bytes 116648 | tf_op jit(solution)/shard_map/ppermute | solution.py:31
  253.5 4.1 %collective-permute-start.29 = (f32[3,11,6,1]{3,2,1,0:T(8,128)}, f32[3,11,6,1]{3,2,1,0:T(8,128)}, u32[]{:S(2)}, u32[]{:S(2)}) collective-permute-start(f32[3,11,6,1]{3,2,1,0:T(8,128)} %get-tuple-element.19), channel_id=1, source_target_pairs={{0,1},{1,0},{2,3},{3,2},{4,5},{5,4},{6,7},{7,6},{8,9},{9,8},{10,11... | collective-permute-start | bytes 2384 | tf_op jit(solution)/shard_map/ppermute | solution.py:28
  260.7 5.9 %collective-permute-start.31 = (f32[3,9,1,360]{3,2,1,0:T(1,128)S(1)}, f32[3,9,1,360]{3,2,1,0:T(1,128)S(1)}, u32[]{:S(2)}, u32[]{:S(2)}) collective-permute-start(f32[3,9,1,360]{3,2,1,0:T(1,128)S(1)} %get-tuple-element.45), channel_id=1, source_target_pairs={{0,4},{4,8},{8,12},{12,0},{1,5},{5,9},{9,13},{13,1},{2,6},{6,10},{... | collective-permute-start | bytes 116648 | tf_op jit(solution)/shard_map/ppermute | solution.py:28
  261.6 5.0 %collective-permute-start.32 = (f32[3,9,1,360]{3,2,1,0:T(1,128)S(1)}, f32[3,9,1,360]{3,2,1,0:T(1,128)S(1)}, u32[]{:S(2)}, u32[]{:S(2)}) collective-permute-start(f32[3,9,1,360]{3,2,1,0:T(1,128)S(1)} %get-tuple-element.46), channel_id=1, source_target_pairs={{4,0},{8,4},{12,8},{0,12},{5,1},{9,5},{13,9},{1,13},{6,2},{10,6},{... | collective-permute-start | bytes 116648 | tf_op jit(solution)/shard_map/ppermute | solution.py:31
  279.0 5.9 %collective-permute-start.37 = (f32[3,9,1,360]{3,2,1,0:T(1,128)S(1)}, f32[3,9,1,360]{3,2,1,0:T(1,128)S(1)}, u32[]{:S(2)}, u32[]{:S(2)}) collective-permute-start(f32[3,9,1,360]{3,2,1,0:T(1,128)S(1)} %get-tuple-element.43), channel_id=1, source_target_pairs={{0,4},{4,8},{8,12},{12,0},{1,5},{5,9},{9,13},{13,1},{2,6},{6,10},{... | collective-permute-start | bytes 116648 | tf_op jit(solution)/shard_map/ppermute | solution.py:28
  280.2 4.9 %collective-permute-start.38 = (f32[3,9,1,360]{3,2,1,0:T(1,128)S(1)}, f32[3,9,1,360]{3,2,1,0:T(1,128)S(1)}, u32[]{:S(2)}, u32[]{:S(2)}) collective-permute-start(f32[3,9,1,360]{3,2,1,0:T(1,128)S(1)} %get-tuple-element.44), channel_id=1, source_target_pairs={{4,0},{8,4},{12,8},{0,12},{5,1},{9,5},{13,9},{1,13},{6,2},{10,6},{... | collective-permute-start | bytes 116648 | tf_op jit(solution)/shard_map/ppermute | solution.py:31
  291.6 4.7 %collective-permute-start.41 = (f32[3,11,6,1]{3,2,1,0:T(8,128)}, f32[3,11,6,1]{3,2,1,0:T(8,128)}, u32[]{:S(2)}, u32[]{:S(2)}) collective-permute-start(f32[3,11,6,1]{3,2,1,0:T(8,128)} %get-tuple-element.15), channel_id=1, source_target_pairs={{0,1},{1,0},{2,3},{3,2},{4,5},{5,4},{6,7},{7,6},{8,9},{9,8},{10,11... | collective-permute-start | bytes 2384 | tf_op jit(solution)/shard_map/ppermute | solution.py:28
  291.7 4.7 %collective-permute-start.42 = (f32[3,11,6,1]{3,2,1,0:T(8,128)}, f32[3,11,6,1]{3,2,1,0:T(8,128)}, u32[]{:S(2)}, u32[]{:S(2)}) collective-permute-start(f32[3,11,6,1]{3,2,1,0:T(8,128)} %get-tuple-element.16), channel_id=1, source_target_pairs={{1,0},{0,1},{3,2},{2,3},{5,4},{4,5},{7,6},{6,7},{9,8},{8,9},{11,10... | collective-permute-start | bytes 2384 | tf_op jit(solution)/shard_map/ppermute | solution.py:31
  (41 other events, 692.5 us)
where the time goes:
time: 312 us; the launch traced here: 308 us
  other arithmetic  159 us (51%)
  starting transfers between devices  58.9 us (19%)
  local copies, waits for them, and re-layouts  49.9 us (16%)
  waiting for transfers between devices  30.9 us (10%)
  blocking collectives  7.18 us (2%)
    scatter-add x1, other arithmetic, per_device(): jnp.zeros((tracers, lev_dev, STEPS * cells), jnp.float32).at[:, :, targets]  123 us
    ppermute x20, starting transfers between devices, with_halo(): lax.ppermute(lax.slice_in_dim(block, 0, width, axis=dim), axis, backward)  29.5 us
    ppermute x20, waiting for transfers between devices, with_halo(): lax.ppermute(lax.slice_in_dim(block, block.shape[dim] - width, None, axis...  22.6 us
    unnamed x48, local copies, waits for them, and re-layouts  22 us
    ppermute x20, starting transfers between devices, with_halo(): lax.ppermute(lax.slice_in_dim(block, block.shape[dim] - width, None, axis...  13.9 us
    slice x1, local copies, waits for them, and re-layouts, per_device(): adjoint = moved + forcing[:, :, step_index]  12.4 us
    ppermute x2, starting transfers between devices, shifted_2(): lax.ppermute(value, axis, [(source, source + steps) for source in range(i...  8.43 us
    ppermute x20, waiting for transfers between devices, with_halo(): lax.ppermute(lax.slice_in_dim(block, 0, width, axis=dim), axis, backward)  8.26 us
  transfers between devices with their start and end apart: 45, of which 22 were waited for; matrix products, arithmetic and copies ran while one was open for 11% of the time, Pallas kernels for 0%

commit v1 on v0

v1 whole, which is shorter than its diff:
```python
import functools

import jax
import jax.numpy as jnp
from jax import lax
from jax.experimental import pallas as pl
from jax.experimental.pallas import tpu as pltpu
from jax.sharding import PartitionSpec as P

STEPS = 6
WIDTH = 2
ROUNDS = STEPS // WIDTH
LANES = 128
CHUNK = 3072
F32 = jnp.float32
BF16 = jnp.bfloat16
VMEM = pl.BlockSpec(memory_space=pltpu.VMEM)
SMEM = pl.BlockSpec(memory_space=pltpu.SMEM)
PARAMS = pltpu.CompilerParams(vmem_limit_bytes=48 * 1024 * 1024)


def window(margin, levels):
    count = lax.axis_size("levels")
    if count == 1:
        return 0, levels
    if count == 2:
        return lax.axis_index("levels") * (STEPS - margin), levels + margin
    return STEPS - margin, levels + 2 * margin


def level_moves(levels):
    count = lax.axis_size("levels")
    band = lax.axis_index("levels")
    if count == 1:
        return []
    if count == 2:
        return [([(0, 1), (1, 0)], (levels - STEPS) * (1 - band), levels * (1 - band))]
    up = [(i, i + 1) for i in range(count - 1)]
    down = [(i + 1, i) for i in range(count - 1)]
    return [(up, levels - STEPS, 0), (down, 0, STEPS + levels)]


def move(value, tile_step, level_pairs=None):
    tiles, bands = lax.axis_size("tiles"), lax.axis_size("levels")
    if level_pairs is None:
        level_pairs = [(i, i) for i in range(bands)]
    pairs = [
        (tile * bands + source, (tile + tile_step) * bands + target)
        for tile in range(tiles)
        for source, target in level_pairs
        if 0 <= tile + tile_step < tiles
    ]
    return lax.ppermute(value, ("tiles", "levels"), pairs)


def own_planes(adj, lon, lat, flags, mix):
    tracers, levels, rows, _ = adj.shape
    last_band = lax.axis_index("levels") == lax.axis_size("levels") - 1
    last_tile = lax.axis_index("tiles") == lax.axis_size("tiles") - 1
    shape = lon.shape
    level_ids = lax.broadcasted_iota(jnp.int32, shape, 0)
    row_ids = lax.broadcasted_iota(jnp.int32, shape, 1)
    top = (level_ids == levels - 1) & last_band
    shut = (row_ids == rows - 1) & last_tile
    first = flags[0].astype(F32)
    second = flags[1].astype(F32)
    lat_open = jnp.where(shut, 0.0, lat[...])
    planes = [adj[t] for t in range(tracers)]
    planes.append(jnp.where(top, 0.0, mix[...]))
    planes.append(lon[...] * first)
    planes.append(lon[...] * (1.0 - first))
    planes.append(lat_open * second)
    planes.append(lat_open * (1.0 - second))
    return planes


def edges_kernel(adj, lon, lat, flags, mix, misfit, kernel, owner, target, edge_out, pay_out, buf):
    tracers, levels, rows, columns = adj.shape
    width = edge_out.shape[-1]
    tail = columns // LANES * LANES
    buf[...] = jnp.zeros_like(buf)
    for p, plane in enumerate(own_planes(adj, lon, lat, flags, mix)):
        buf[0, p, :, 0:rows, :] = plane[:, :, 0:LANES]
        buf[1, p, :, 0:rows, 0 : columns - tail] = plane[:, :, tail:]
    lane = lax.broadcasted_iota(jnp.int32, (8, LANES), 1)
    gap = columns - tail
    for p in range(buf.shape[1]):
        for l in range(levels):
            start = pltpu.roll(buf[0, p, l], gap, 1)
            end = pltpu.roll(buf[1, p, l], width - gap, 1)
            both = jnp.where(
                lane >= width - STEPS,
                end,
                jnp.where((lane >= gap) & (lane < gap + STEPS), start, 0.0),
            )
            edge_out[p, l] = both[0:rows]
    pay_out[...] = jnp.zeros_like(pay_out)
    pay_out[0:tracers] = misfit[...]
    pay_out[tracers : tracers + levels] = kernel[...]
    pay_out[tracers + levels : tracers + levels + 1] = owner[...].astype(F32)
    pay_out[tracers + levels + 1 : tracers + levels + 2] = target[...].astype(F32)


def pack_kernel(moves, adj, lon, lat, flags, mix, edge, own_out, north_out, south_out, *rest):
    tracers, levels, rows, columns = adj.shape
    tail = columns // LANES * LANES
    gap = columns - tail
    buf = rest[-1]
    outs = rest[:-1]
    buf[...] = jnp.zeros_like(buf)
    lane = lax.broadcasted_iota(jnp.int32, (levels, rows, LANES), 2)
    for p, plane in enumerate(own_planes(adj, lon, lat, flags, mix)):
        buf[p, :, 0:rows, 0:columns] = plane
        last = buf[p, :, 0:rows, tail : tail + LANES]
        buf[p, :, 0:rows, tail : tail + LANES] = jnp.where(lane < gap, last, edge[p])
    mixing, east, west, north, south = range(tracers, tracers + 5)
    own_out[...] = buf[:, :, 0:rows, :]

    def rows_of(out, first, row, single, with_south, start, count):
        pick = pl.ds(start, count)
        entry = 0
        planes = list(range(tracers)) + [mixing, north] + ([south] if with_south else [])
        for p in planes:
            out[entry] = buf[p, pick, first : first + WIDTH, :]
            entry += 1
        out[entry, :, 0:1, :] = buf[east, pick, single : single + 1, :]
        out[entry, :, 1:2, :] = buf[west, pick, single : single + 1, :]

    rows_of(north_out, rows - WIDTH, rows, rows - 1, True, 0, levels)
    rows_of(south_out, 0, rows, 0, False, 0, levels)
    for i, (_, start, _) in enumerate(moves()):
        level_out, north_far, south_far = outs[3 * i : 3 * i + 3]
        level_out[...] = buf[:, pl.ds(start, STEPS), 0:rows, :]
        rows_of(north_far, rows - WIDTH, rows, rows - 1, True, start, STEPS)
        rows_of(south_far, 0, rows, 0, False, start, STEPS)


def advance(step, src, dst, coef, forcing, index, profile, flux, levels):
    tracers = src.shape[0]
    first, count = window(STEPS - 1 - step, levels)
    own, _ = window(0, levels)
    lanes = src.shape[-1]
    total = [flux[t] for t in range(tracers)]
    for i in range(count):
        at = first + i
        up, down = coef[0, at + 1], coef[0, at]
        east, west, north, south = (coef[c, at + 1] for c in range(1, 5))
        own_id = at - own
        inside = (own_id >= 0) & (own_id < levels)
        weight = jnp.where(inside, profile[jnp.clip(own_id, 0, levels - 1)], 0.0)
        for t in range(tracers):
            a = src[t, at + 1]
            b = a + up * (src[t, at + 2] - a) + down * (src[t, at] - a)
            moved = b + east * (pltpu.roll(b, lanes - 1, 1) - b) + west * (pltpu.roll(b, 1, 1) - b)
            moved = moved + north * (pltpu.roll(b, 7, 0) - b) + south * (pltpu.roll(b, 1, 0) - b)
            new = moved + forcing[index, t, at]
            dst[t, at + 1] = new
            total[t] = total[t] + weight * new
    for t in range(tracers):
        flux[t] = total[t]


def clear_pads(ref):
    levels = ref.shape[1]
    ref[:, 0:1] = jnp.zeros((ref.shape[0], 1) + ref.shape[2:], F32)
    ref[:, levels - 1 : levels] = jnp.zeros((ref.shape[0], 1) + ref.shape[2:], F32)


def run_steps(number, work, other, coef, forcing, profile, flux, levels):
    refs = [work, other]
    for i in range(WIDTH):
        advance(number * WIDTH + i, refs[i % 2], refs[(i + 1) % 2], coef, forcing, i, profile, flux, levels)
    return refs[WIDTH % 2]


def send_rows(number, state, north_out, south_out, rows, levels):
    start, count = window(STEPS - (number + 1) * WIDTH, levels)
    north_out[...] = state[:, pl.ds(start + 1, count), rows - WIDTH : rows, :]
    south_out[...] = state[:, pl.ds(start + 1, count), 0:WIDTH, :]


def first_kernel(moves, *refs):
    number = len(moves())
    own, from_south, from_north = refs[:3]
    far = refs[3 : 3 + 3 * number]
    forcing, profile, state_out, coef_out, flux, north_out, south_out, work, other, raw = refs[3 + 3 * number :]
    planes, levels, rows, lanes = own.shape
    tracers = planes - 5
    mixing, east, west, north, south = range(tracers, tracers + 5)
    raw[...] = jnp.zeros_like(raw)
    flux[...] = jnp.zeros_like(flux)
    clear_pads(work)
    clear_pads(other)

    def place(start, count, body, below, above):
        pick = pl.ds(start + 1, count)
        lo, hi = slice(6, 6 + WIDTH), slice(rows, rows + WIDTH)
        for p in range(planes):
            ref, plane = (work, p) if p < tracers else (raw, p - tracers)
            ref[plane, pick, 0:rows, :] = body[p]
        for entry, p in enumerate(list(range(tracers)) + [mixing, north, south]):
            ref, plane = (work, p) if p < tracers else (raw, p - tracers)
            ref[plane, pick, lo, :] = below[entry]
            if p != south:
                ref[plane, pick, hi, :] = above[entry]
        for k, p in enumerate((east, west)):
            raw[p - tracers, pick, 7:8, :] = below[tracers + 3, :, k : k + 1, :]
            raw[p - tracers, pick, rows : rows + 1, :] = above[tracers + 2, :, k : k + 1, :]

    own_start, _ = window(0, levels)
    place(own_start, levels, own, from_south, from_north)
    for i, (_, _, slot) in enumerate(moves()):
        place(slot, STEPS, *far[3 * i : 3 * i + 3])
    coef_out[0] = raw[0]
    coef_out[1] = raw[1]
    coef_out[3] = raw[3]
    for l in range(raw.shape[1]):
        coef_out[2, l] = pltpu.roll(raw[2, l], 1, 1)
        coef_out[4, l] = pltpu.roll(raw[4, l], 1, 0)
    last = run_steps(0, work, other, coef_out, forcing, profile, flux, levels)
    state_out[...] = last[...]
    send_rows(0, state_out, north_out, south_out, rows, levels)


def next_kernel(number, levels, rows, state, coef, from_south, from_north, forcing, profile, flux_in, *refs):
    work, other = refs[-2:]
    start, count = window(STEPS - number * WIDTH, levels)
    pick = pl.ds(start + 1, count)
    work[...] = state[...]
    work[:, pick, rows : rows + WIDTH, :] = from_north[...]
    work[:, pick, 6 : 6 + WIDTH, :] = from_south[...]
    clear_pads(other)
    if number < ROUNDS - 1:
        state_out, flux, north_out, south_out = refs[:-2]
        flux[...] = flux_in[...]
        last = run_steps(number, work, other, coef, forcing, profile, flux, levels)
        state_out[...] = last[...]
        send_rows(number, state_out, north_out, south_out, rows, levels)
        return
    adjoint, keep, give, flux = refs[:-2]
    flux[...] = flux_in[...]
    last = run_steps(number, work, other, coef, forcing, profile, flux, levels)
    own, _ = window(0, levels)
    columns = adjoint.shape[-1]
    adjoint[...] = last[:, pl.ds(own + 1, levels), 0:rows, 0:columns]
    if lax.axis_size("levels") == 2:
        half = rows // 2
        upper = lax.axis_index("levels") == 1
        low, high = flux[:, 0:half, 0:columns], flux[:, half:rows, 0:columns]
        keep[...] = jnp.where(upper, high, low)
        give[...] = jnp.where(upper, low, high)
    else:
        keep[...] = flux[:, 0:rows, 0:columns]
        give[...] = jnp.zeros_like(give)


def forcing_kernel(tracers, levels, rows, columns, got, out, left, right, terms, keys, kern):
    bands, sources, _, held = got.shape
    lanes = out.shape[-1]
    wide = out.shape[2]
    subs = lax.axis_size("sub")
    band, tile, sub = (lax.axis_index(name) for name in ("levels", "tiles", "sub"))
    own, _ = window(0, levels)
    for s in range(sources):
        cols = slice(s * held, (s + 1) * held)
        owner = got[band, s, tracers + levels : tracers + levels + 1, :]
        target = got[band, s, tracers + levels + 1 : tracers + levels + 2, :]
        cells = rows * columns
        step = jnp.floor((target + 0.5) * (1.0 / cells))
        cell = target - step * cells
        row = jnp.floor((cell + 0.5) * (1.0 / columns))
        col = cell - row * columns
        owner_tile = jnp.floor((owner + 0.5) * (1.0 / subs))
        owner_sub = owner - owner_tile * subs
        row = row + (owner_tile - tile.astype(F32)) * rows
        shift = owner_sub - sub.astype(F32)
        col = col + jnp.where(shift < 0, shift + subs, shift) * columns
        near = (row >= -2) & (row <= rows + 1)
        east_side = col < columns + STEPS
        west_side = col >= subs * columns - STEPS
        lane = jnp.where(east_side, col, jnp.where(west_side, col - subs * columns + lanes, -1.0))
        key = jnp.where(near, step * 8 + jnp.where(row < 0, row + 8, row), -1.0)
        keys[:, cols] = jnp.broadcast_to(key, (8, held))
        ids = lax.broadcasted_iota(jnp.int32, (lanes, held), 0).astype(F32)
        right[:, cols] = jnp.where(ids == lane, 1.0, 0.0).astype(BF16)
        for l in range(wide):
            level = band * levels + l - own
            source_band = jnp.clip(level // levels, 0, bands - 1)
            source_level = level - (level // levels) * levels
            kern[l, :, cols] = got[source_band, s, pl.ds(tracers + source_level, 1), :]
    for l in range(wide):
        for t in range(tracers):
            weights = [got[band, s, t : t + 1, :] for s in range(sources)]
            value = kern[l] * (jnp.concatenate(weights, axis=1) if sources > 1 else weights[0])
            high = value.astype(BF16).astype(F32)
            low = value - high
            both = [jnp.broadcast_to(x, (8, x.shape[1])) for x in (high, low)]
            terms[l * tracers + t] = jnp.concatenate(both, axis=0).astype(BF16)
    ids = lax.broadcasted_iota(jnp.int32, (8, keys.shape[1]), 0).astype(F32)
    for pair in range(STEPS // 2):
        first, count = window(STEPS - 1 - 2 * pair, levels)

        def one_step(odd, carry, pair=pair, first=first, count=count):
            step = 2 * pair + odd
            hit = jnp.where(keys[...] == ids + (step * 8).astype(F32), 1.0, 0.0)
            mask = jnp.concatenate([hit, hit], axis=0).astype(BF16)

            def fill(i, carry):
                left[pl.ds(pl.multiple_of(i * 16, 16), 16), :] = terms[first * tracers + i] * mask
                return carry

            lax.fori_loop(0, count * tracers, fill, 0)
            size = count * tracers * 16
            product = lax.dot_general(
                left[0:size, :], right[...], (((1,), (1,)), ((), ())), preferred_element_type=F32
            )
            for i in range(count):
                for t in range(tracers):
                    base = (i * tracers + t) * 16
                    value = product[base : base + 8] + product[base + 8 : base + 16]
                    place = (step, t, first + i)
                    if pl.num_programs(0) == 1:
                        out[place] = value
                    else:
                        old = jnp.where(pl.program_id(0) == 0, 0.0, out[place])
                        out[place] = old + value
            return carry

        lax.fori_loop(0, 2, one_step, 0)


def per_device(
    final_adjoint,
    lon_courant,
    lat_courant,
    upwind_flags,
    vertical_mixing,
    level_profile,
    sounding_owner,
    sounding_target,
    misfit,
    averaging_kernel,
):
    tracers, levels, rows, columns = final_adjoint.shape
    held = misfit.shape[1]
    bands, subs, tiles = (lax.axis_size(name) for name in ("levels", "sub", "tiles"))
    planes = tracers + 5
    lanes = -(-(columns + 2 * STEPS) // LANES) * LANES
    wide = window(STEPS, levels)[1]
    moves = functools.partial(level_moves, levels)
    shape = lambda *dims: jax.ShapeDtypeStruct(dims, F32)
    call = functools.partial(pl.pallas_call, compiler_params=PARAMS)
    fields = (final_adjoint, lon_courant, lat_courant, upwind_flags, vertical_mixing)

    pay_rows = -(-(tracers + levels + 2) // 8) * 8
    edge, payload = call(
        edges_kernel,
        out_shape=(shape(planes, levels, rows, LANES), shape(pay_rows, held)),
        in_specs=[VMEM] * 9,
        out_specs=(VMEM, VMEM),
        scratch_shapes=[pltpu.VMEM((2, planes, levels, 8, LANES), F32)],
        name="edges",
    )(*fields, misfit, averaging_kernel, sounding_owner.reshape(1, held), sounding_target.reshape(1, held))
    edge = lax.ppermute(edge, "sub", [(i, (i + 1) % subs) for i in range(subs)])
    gathered = lax.all_gather(payload, ("levels", "tiles", "sub"))
    gathered = gathered.reshape(bands, tiles * subs, pay_rows, held)

    sizes = []
    for count in [levels] + [STEPS] * len(moves()):
        if count != levels or sizes:
            sizes.append(shape(planes, count, rows, lanes))
        sizes.append(shape(tracers + 4, count, WIDTH, lanes))
        sizes.append(shape(tracers + 3, count, WIDTH, lanes))
    packed = call(
        functools.partial(pack_kernel, moves),
        out_shape=(shape(planes, levels, rows, lanes), *sizes),
        in_specs=[VMEM] * 6,
        out_specs=[VMEM] * (1 + len(sizes)),
        scratch_shapes=[pltpu.VMEM((planes, levels, 8, lanes), F32)],
        name="pack",
    )(*fields, edge)
    own = packed[0]
    received = [move(packed[1], 1), move(packed[2], -1)]
    for i, (pairs, _, _) in enumerate(moves()):
        level_part, north_part, south_part = packed[3 + 3 * i : 6 + 3 * i]
        received += [move(level_part, 0, pairs), move(north_part, 1, pairs), move(south_part, -1, pairs)]

    sources = max(1, min(tiles * subs, CHUNK // held))
    batch = sources * held
    chunks = tiles * subs // sources
    forcing = call(
        functools.partial(forcing_kernel, tracers, levels, rows, columns),
        out_shape=shape(STEPS, tracers, wide, 8, lanes),
        grid=(chunks,),
        in_specs=[pl.BlockSpec((bands, sources, pay_rows, held), lambda i: (0, i, 0, 0))],
        out_specs=pl.BlockSpec((STEPS, tracers, wide, 8, lanes), lambda i: (0, 0, 0, 0, 0)),
        scratch_shapes=[
            pltpu.VMEM((wide * tracers * 16, batch), BF16),
            pltpu.VMEM((lanes, batch), BF16),
            pltpu.VMEM((wide * tracers, 16, batch), BF16),
            pltpu.VMEM((8, batch), F32),
            pltpu.VMEM((wide, 1, batch), F32),
        ],
        name="forcing",
    )(gathered)

    def force_spec(number):
        return pl.BlockSpec((WIDTH, tracers, wide, 8, lanes), lambda i: (number, 0, 0, 0, 0))

    state_shape = (tracers, wide + 2, 8, lanes)
    coef_shape = (5, wide + 2, 8, lanes)
    flux_shape = (tracers, 8, lanes)

    def whole(dims):
        return pl.BlockSpec(dims, lambda i: (0,) * len(dims))

    def messages(number):
        count = window(STEPS - number * WIDTH, levels)[1]
        return shape(tracers, count, WIDTH, lanes)

    scratch = [pltpu.VMEM(state_shape, F32)] * 2
    inputs = [own, *received]
    outs = (shape(*state_shape), shape(*coef_shape), shape(*flux_shape), messages(1), messages(1))
    state, coef, flux, north, south = call(
        functools.partial(first_kernel, moves),
        out_shape=outs,
        grid=(1,),
        in_specs=[whole(x.shape) for x in inputs] + [force_spec(0), SMEM],
        out_specs=[whole(x.shape) for x in outs],
        scratch_shapes=scratch + [pltpu.VMEM(coef_shape, F32)],
        name="round0",
    )(*inputs, forcing, level_profile)
    half = rows // 2 if bands == 2 else rows
    for number in range(1, ROUNDS):
        inputs = [state, coef, move(north, 1), move(south, -1)]
        if number < ROUNDS - 1:
            outs = (shape(*state_shape), shape(*flux_shape), messages(number + 1), messages(number + 1))
            extra = []
        else:
            part = shape(tracers, half, columns)
            outs = (shape(tracers, levels, rows, columns), part, part)
            extra = [pltpu.VMEM(flux_shape, F32)]
        results = call(
            functools.partial(next_kernel, number, levels, rows),
            out_shape=outs,
            grid=(1,),
            in_specs=[whole(x.shape) for x in inputs] + [force_spec(number), SMEM, whole(flux_shape)],
            out_specs=[whole(x.shape) for x in outs],
            scratch_shapes=extra + scratch,
            name="round" + str(number),
        )(*inputs, forcing, level_profile, flux)
        if number < ROUNDS - 1:
            state, flux, north, south = results
    adjoint, keep, give = results
    if bands == 2:
        flux_gradient = keep + lax.ppermute(give, "levels", [(0, 1), (1, 0)])
    else:
        flux_gradient = lax.psum_scatter(keep, "levels", scatter_dimension=1, tiled=True)
    return adjoint, flux_gradient


def solution(mesh):
    return jax.shard_map(
        per_device,
        mesh=mesh,
        in_specs=(
            P("groups", "levels", "tiles", "sub"),
            P(("groups", "levels"), "tiles", "sub"),
            P(("groups", "levels"), "tiles", "sub"),
            P(None, ("groups", "levels"), "tiles", "sub"),
            P(("groups", "levels"), "tiles", "sub"),
            P("levels"),
            P(("groups", "tiles", "sub"), None),
            P(("groups", "tiles", "sub")),
            P(None, ("groups", "tiles", "sub")),
            P("levels", ("groups", "tiles", "sub")),
        ),
        out_specs=(P("groups", "levels", "tiles", "sub"), P("groups", ("tiles", "levels"), "sub")),
        check_vma=False,
    )
```

time: 312 us -> 94.8 us (0.30); the launches traced: 308 us -> 94.2 us
  other arithmetic: 159 us -> 0.6 us
  local copies, waits for them, and re-layouts: 49.9 us -> 8.73 us
  starting transfers between devices: 58.9 us -> 21.8 us
  Pallas kernels: 0 us -> 24.4 us
  waiting for transfers between devices: 30.9 us -> 14.5 us
  blocking collectives: 7.18 us -> 23.3 us
    scatter-add x1 -> x0, other arithmetic: 123 us -> none  [per_device(): jnp.zeros((tracers, lev_dev, STEPS * cells), jnp.float32).at[:, :, targets]]
    ppermute x43 -> x11, starting transfers between devices: 52.2 us -> 21.8 us  [the longest x9 19.8 us: move(): return lax.ppermute(value, ('tiles', 'levels'), pairs)]
    pallas_call x0 -> x6, Pallas kernels: none -> 24.4 us  [the longest x1 17.1 us: per_device(): call(functools.partial(forcing_kernel, tracers, levels, rows, columns), o...]
    all_gather x0 -> x1, blocking collectives: none -> 23.3 us  [per_device(): gathered = lax.all_gather(payload, ('levels', 'tiles', 'sub'))]
    ppermute x43 -> x11, waiting for transfers between devices: 30.9 us -> 14.5 us  [the longest x9 11.4 us: move(): return lax.ppermute(value, ('tiles', 'levels'), pairs)]
    slice x13 -> x0, local copies, waits for them, and re-layouts: 14.1 us -> none  [the longest x1 12.4 us: per_device(): adjoint = moved + forcing[:, :, step_index]]
    unnamed x48 -> x22, local copies, waits for them, and re-layouts: 22 us -> 8.04 us
    concatenate x10 -> x0, other arithmetic: 8.82 us -> none  [the longest x7 7.95 us: with_halo(): block = jnp.concatenate([low, block, high], axis=dim)]
  transfers between devices with their start and end apart: 45 -> 11, of which waited for: 22 -> 6; matrix products, arithmetic and copies ran while one was open for 11% -> 0% of each run, Pallas kernels for 0% -> 18%
where the time goes in v1:
time: 94.8 us; the launch traced here: 94.2 us
  Pallas kernels  24.4 us (26%)
  blocking collectives  23.3 us (25%)
  starting transfers between devices  21.8 us (23%)
  waiting for transfers between devices  14.5 us (15%)
  local copies, waits for them, and re-layouts  8.73 us (9%)
    all_gather x1, blocking collectives, per_device(): gathered = lax.all_gather(payload, ('levels', 'tiles', 'sub'))  23.3 us
    ppermute x9, starting transfers between devices, move(): return lax.ppermute(value, ('tiles', 'levels'), pairs)  19.8 us
    pallas_call x1, Pallas kernels, per_device(): call(functools.partial(forcing_kernel, tracers, levels, rows, columns), o...  17.1 us
    ppermute x9, waiting for transfers between devices, move(): return lax.ppermute(value, ('tiles', 'levels'), pairs)  11.4 us
    unnamed x22, local copies, waits for them, and re-layouts  8.04 us
    pallas_call x2, Pallas kernels, per_device(): call(functools.partial(next_kernel, number, levels, rows), out_shape=outs...  3.63 us
    pallas_call x1, Pallas kernels, per_device(): call(functools.partial(first_kernel, moves), out_shape=outs, grid=(1,), i...  2.98 us
    ppermute x1, waiting for transfers between devices, per_device(): flux_gradient = keep + lax.ppermute(give, 'levels', [(0, 1), (1, 0)])  2.14 us
  transfers between devices with their start and end apart: 11, of which 6 were waited for; matrix products, arithmetic and copies ran while one was open for 0% of the time, Pallas kernels for 18%

profile of v1, /device:TPU:0, one launch (start us, length us, event | category | flops | bytes accessed | tf_op | source)
XLA Modules:
  0.0 94.2 jit_solution(1522656641318163437)
XLA Ops:
  1.3 0.9 copy-done.2
  2.2 0.9 copy-done.3
  8.5 1.0 %collective-permute-done.edge = f32[8,9,4,128]{3,2,1,0:T(4,128)S(1)} collective-permute-done((f32[8,9,4,128]{3,2,1,0:T(4,128)S(1)}, f32[8,9,4,128]{3,2,1,0:T(4,128)S(1)}, u32[]{:S(2)}, u32[]{:S(2)}) %collective-permute-start) | collective-permute-done | bytes 147488 | tf_op jit(solution)/shard_map/ppermute | solution.py:364
  9.9 2.9 %collective-permute-start.3 = (f32[8,6,4,384]{3,2,1,0:T(4,128)S(1)}, f32[8,6,4,384]{3,2,1,0:T(4,128)S(1)}, u32[]{:S(2)}, u32[]{:S(2)}) collective-permute-start(f32[8,6,4,384]{3,2,1,0:T(4,128)S(1)} %get-tuple-element.26), channel_id=1, source_target_pairs={{0,2},{2,0},{4,6},{6,4},{8,10},{10,8},{12,14},{14,12},{1,3},{3,1},... | collective-permute-start | bytes 884744 | tf_op jit(solution)/shard_map/ppermute | solution.py:53
  12.9 3.5 %collective-permute-start.1 = (f32[7,9,2,384]{3,2,1,0:T(2,128)S(1)}, f32[7,9,2,384]{3,2,1,0:T(2,128)S(1)}, u32[]{:S(2)}, u32[]{:S(2)}) collective-permute-start(f32[7,9,2,384]{3,2,1,0:T(2,128)S(1)} %get-tuple-element.24), channel_id=1, source_target_pairs={{0,4},{2,6},{4,8},{6,10},{8,12},{10,14},{1,5},{3,7},{5,9},{7,11},{... | collective-permute-start | bytes 580616 | tf_op jit(solution)/shard_map/ppermute | solution.py:53
  16.3 1.3 %collective-permute-start.5 = (f32[6,6,2,384]{3,2,1,0:T(2,128)S(1)}, f32[6,6,2,384]{3,2,1,0:T(2,128)S(1)}, u32[]{:S(2)}, u32[]{:S(2)}) collective-permute-start(f32[6,6,2,384]{3,2,1,0:T(2,128)S(1)} %get-tuple-element.28), channel_id=1, source_target_pairs={{4,2},{6,0},{8,6},{10,4},{12,10},{14,8},{5,3},{7,1},{9,7},{11,5},{... | collective-permute-start | bytes 331784 | tf_op jit(solution)/shard_map/ppermute | solution.py:53
  17.6 5.5 %collective-permute-start.4 = (f32[7,6,2,384]{3,2,1,0:T(2,128)S(1)}, f32[7,6,2,384]{3,2,1,0:T(2,128)S(1)}, u32[]{:S(2)}, u32[]{:S(2)}) collective-permute-start(f32[7,6,2,384]{3,2,1,0:T(2,128)S(1)} %get-tuple-element.27), channel_id=1, source_target_pairs={{0,6},{2,4},{4,10},{6,8},{8,14},{10,12},{1,7},{3,5},{5,11},{7,9},{... | collective-permute-start | bytes 387080 | tf_op jit(solution)/shard_map/ppermute | solution.py:53
  23.1 1.3 %collective-permute-start.2 = (f32[6,9,2,384]{3,2,1,0:T(2,128)S(1)}, f32[6,9,2,384]{3,2,1,0:T(2,128)S(1)}, u32[]{:S(2)}, u32[]{:S(2)}) collective-permute-start(f32[6,9,2,384]{3,2,1,0:T(2,128)S(1)} %get-tuple-element.25), channel_id=1, source_target_pairs={{4,0},{6,2},{8,4},{10,6},{12,8},{14,10},{5,1},{7,3},{9,5},{11,7},{... | collective-permute-start | bytes 497672 | tf_op jit(solution)/shard_map/ppermute | solution.py:53
  24.4 23.3 %all-gather = f32[256,384]{1,0:T(8,128)S(1)} all-gather(f32[16,384]{1,0:T(8,128)S(1)} %get-tuple-element.29), channel_id=2, replica_groups=mesh['groups'=2,'tiles'=4,'levels'=2,'sub'=2] {'levels','tiles','sub'}, dimensions={0}, use_global_device_ids=true | all-gather | bytes 417792 | tf_op jit(solution)/shard_map/all_gather | solution.py:365
  47.7 17.1 %forcing.1.refs_6_ = f32[6,3,15,8,384]{4,3,2,1,0:T(8,128)S(1)} custom-call(f32[2,8,16,384]{3,2,1,0:T(8,128)S(1)} %bitcast.2), custom_call_target="tpu_custom_call" | custom-call | tf_op jit(solution)/shard_map/forcing/pallas_call | solution.py:391
  64.9 1.7 %copy-done = f32[6,3,15,8,384]{4,3,2,1,0:T(8,128)} copy-done((f32[6,3,15,8,384]{4,3,2,1,0:T(8,128)}, f32[6,3,15,8,384]{4,3,2,1,0:T(8,128)S(1)}, u32[]{:S(2)}) %copy-start) | copy-done | bytes 3317784
  66.6 3.0 %round0.1 = (f32[3,17,8,384]{3,2,1,0:T(8,128)S(1)}, f32[5,17,8,384]{3,2,1,0:T(8,128)S(1)}, f32[3,8,384]{2,1,0:T(8,128)S(1)}, f32[3,13,2,384]{3,2,1,0:T(2,128)S(1)}, f32[3,13,2,384]{3,2,1,0:T(2,128)S(1)}) custom-call(f32[8,9,4,384]{3,2,1,0:T(4,128)S(1)} %get-tuple-element.23.refs_0_, f32[7,9,2,384]{3,2,1,0:T(2,128)S(1)} %collective-permute-done.1.refs_1_, ...), custom_call_target="tpu_custom_call" | custom-call | tf_op jit(solution)/shard_map/round0/pallas_call | solution.py:424
  69.6 1.3 %collective-permute-start.6 = (f32[3,13,2,384]{3,2,1,0:T(2,128)S(1)}, f32[3,13,2,384]{3,2,1,0:T(2,128)S(1)}, u32[]{:S(2)}, u32[]{:S(2)}) collective-permute-start(f32[3,13,2,384]{3,2,1,0:T(2,128)S(1)} %get-tuple-element.32), channel_id=1, source_target_pairs={{0,4},{2,6},{4,8},{6,10},{8,12},{10,14},{1,5},{3,7},{5,9},{7,11},{... | collective-permute-start | bytes 359432 | tf_op jit(solution)/shard_map/ppermute | solution.py:53
  70.9 1.3 %collective-permute-start.7 = (f32[3,13,2,384]{3,2,1,0:T(2,128)S(1)}, f32[3,13,2,384]{3,2,1,0:T(2,128)S(1)}, u32[]{:S(2)}, u32[]{:S(2)}) collective-permute-start(f32[3,13,2,384]{3,2,1,0:T(2,128)S(1)} %get-tuple-element.33), channel_id=1, source_target_pairs={{4,0},{6,2},{8,4},{10,6},{12,8},{14,10},{5,1},{7,3},{9,5},{11,7},{... | collective-permute-start | bytes 359432 | tf_op jit(solution)/shard_map/ppermute | solution.py:53
  72.2 2.0 %collective-permute-done.6.from_south = f32[3,13,2,384]{3,2,1,0:T(2,128)S(1)} collective-permute-done((f32[3,13,2,384]{3,2,1,0:T(2,128)S(1)}, f32[3,13,2,384]{3,2,1,0:T(2,128)S(1)}, u32[]{:S(2)}, u32[]{:S(2)}) %collective-permute-start.6) | collective-permute-done | bytes 119840 | tf_op jit(solution)/shard_map/ppermute | solution.py:53
  74.2 4.1 %collective-permute-done.7.from_north = f32[3,13,2,384]{3,2,1,0:T(2,128)S(1)} collective-permute-done((f32[3,13,2,384]{3,2,1,0:T(2,128)S(1)}, f32[3,13,2,384]{3,2,1,0:T(2,128)S(1)}, u32[]{:S(2)}, u32[]{:S(2)}) %collective-permute-start.7) | collective-permute-done | bytes 119840 | tf_op jit(solution)/shard_map/ppermute | solution.py:53
  78.3 1.6 %round1.1 = (f32[3,17,8,384]{3,2,1,0:T(8,128)S(1)}, f32[3,8,384]{2,1,0:T(8,128)S(1)}, f32[3,11,2,384]{3,2,1,0:T(2,128)S(1)}, f32[3,11,2,384]{3,2,1,0:T(2,128)S(1)}) custom-call(f32[3,17,8,384]{3,2,1,0:T(8,128)S(1)} %get-tuple-element.30.state, f32[5,17,8,384]{3,2,1,0:T(8,128)S(1)} %get-tuple-element.31.coef, ...), custom_call_target="tpu_custom_call" | custom-call | tf_op jit(solution)/shard_map/round1/pallas_call | solution.py:443
  79.9 1.5 %collective-permute-start.8 = (f32[3,11,2,384]{3,2,1,0:T(2,128)S(1)}, f32[3,11,2,384]{3,2,1,0:T(2,128)S(1)}, u32[]{:S(2)}, u32[]{:S(2)}) collective-permute-start(f32[3,11,2,384]{3,2,1,0:T(2,128)S(1)} %get-tuple-element.36), channel_id=1, source_target_pairs={{0,4},{2,6},{4,8},{6,10},{8,12},{10,14},{1,5},{3,7},{5,9},{7,11},{... | collective-permute-start | bytes 304136 | tf_op jit(solution)/shard_map/ppermute | solution.py:53
  81.3 1.3 %collective-permute-start.9 = (f32[3,11,2,384]{3,2,1,0:T(2,128)S(1)}, f32[3,11,2,384]{3,2,1,0:T(2,128)S(1)}, u32[]{:S(2)}, u32[]{:S(2)}) collective-permute-start(f32[3,11,2,384]{3,2,1,0:T(2,128)S(1)} %get-tuple-element.37), channel_id=1, source_target_pairs={{4,0},{6,2},{8,4},{10,6},{12,8},{14,10},{5,1},{7,3},{9,5},{11,7},{... | collective-permute-start | bytes 304136 | tf_op jit(solution)/shard_map/ppermute | solution.py:53
  82.6 0.9 collective-permute-done.8.from_south
  83.6 4.3 %collective-permute-done.9.from_north = f32[3,11,2,384]{3,2,1,0:T(2,128)S(1)} collective-permute-done((f32[3,11,2,384]{3,2,1,0:T(2,128)S(1)}, f32[3,11,2,384]{3,2,1,0:T(2,128)S(1)}, u32[]{:S(2)}, u32[]{:S(2)}) %collective-permute-start.9) | collective-permute-done | bytes 101408 | tf_op jit(solution)/shard_map/ppermute | solution.py:53
  87.9 2.0 %round2.1 = (f32[3,9,4,360]{3,2,1,0:T(4,128)}, f32[3,2,360]{2,1,0:T(2,128)S(1)}, f32[3,2,360]{2,1,0:T(2,128)S(1)}) custom-call(f32[3,17,8,384]{3,2,1,0:T(8,128)S(1)} %get-tuple-element.35.state, f32[5,17,8,384]{3,2,1,0:T(8,128)S(1)} %get-tuple-element.31.coef, f32[3,11,2,384]{3,2,1,0:T(2,128)S(1)} %collective-permute-done.8.from_south, ...), custom_call_target="tpu_custom_call" | custom-call | tf_op jit(solution)/shard_map/round2/pallas_call | solution.py:443
  89.9 1.5 %collective-permute-start.10 = (f32[3,2,360]{2,1,0:T(2,128)S(1)}, f32[3,2,360]{2,1,0:T(2,128)S(1)}, u32[]{:S(2)}, u32[]{:S(2)}) collective-permute-start(f32[3,2,360]{2,1,0:T(2,128)S(1)} %get-tuple-element.41), channel_id=1, source_target_pairs={{0,2},{2,0},{1,3},{3,1},{4,6},{6,4},{5,7},{7,5},{8,10},{10,8},{9,1... | collective-permute-start | bytes 25928 | tf_op jit(solution)/shard_map/ppermute | solution.py:456
  91.4 2.1 %collective-permute-done.10 = f32[3,2,360]{2,1,0:T(2,128)S(1)} collective-permute-done((f32[3,2,360]{2,1,0:T(2,128)S(1)}, f32[3,2,360]{2,1,0:T(2,128)S(1)}, u32[]{:S(2)}, u32[]{:S(2)}) %collective-permute-start.10) | collective-permute-done | bytes 8672 | tf_op jit(solution)/shard_map/ppermute | solution.py:456
  (29 shorter events, 7.1 us)
Async XLA Ops:
  0.6 65.9 %copy-start.9 = (f32[9]{0:T(128)S(1)}, f32[9]{0:T(128)}, u32[]{:S(2)}) copy-start(f32[9]{0:T(128)} %profile.3) | copy-start | bytes 112
  1.3 0.9 copy-start.2
  2.2 0.9 copy-start.3
  3.1 0.8 copy-start.4
  4.0 0.8 copy-start.5
  4.8 0.8 copy-start.6
  5.6 0.7 copy-start.7
  6.3 0.7 copy-start.8
  7.0 0.7 copy-start.10
  8.0 1.5 %collective-permute-start = (f32[8,9,4,128]{3,2,1,0:T(4,128)S(1)}, f32[8,9,4,128]{3,2,1,0:T(4,128)S(1)}, u32[]{:S(2)}, u32[]{:S(2)}) collective-permute-start(f32[8,9,4,128]{3,2,1,0:T(4,128)S(1)} %get-tuple-element.22), channel_id=1, source_target_pairs={{0,1},{1,0},{2,3},{3,2},{4,5},{5,4},{6,7},{7,6},{8,9},{9,8},{10,11... | collective-permute-start | bytes 442376 | tf_op jit(solution)/shard_map/ppermute | solution.py:364
  9.9 56.6 %collective-permute-start.3 = (f32[8,6,4,384]{3,2,1,0:T(4,128)S(1)}, f32[8,6,4,384]{3,2,1,0:T(4,128)S(1)}, u32[]{:S(2)}, u32[]{:S(2)}) collective-permute-start(f32[8,6,4,384]{3,2,1,0:T(4,128)S(1)} %get-tuple-element.26), channel_id=1, source_target_pairs={{0,2},{2,0},{4,6},{6,4},{8,10},{10,8},{12,14},{14,12},{1,3},{3,1},... | collective-permute-start | bytes 884744 | tf_op jit(solution)/shard_map/ppermute | solution.py:53
  12.9 53.7 %collective-permute-start.1 = (f32[7,9,2,384]{3,2,1,0:T(2,128)S(1)}, f32[7,9,2,384]{3,2,1,0:T(2,128)S(1)}, u32[]{:S(2)}, u32[]{:S(2)}) collective-permute-start(f32[7,9,2,384]{3,2,1,0:T(2,128)S(1)} %get-tuple-element.24), channel_id=1, source_target_pairs={{0,4},{2,6},{4,8},{6,10},{8,12},{10,14},{1,5},{3,7},{5,9},{7,11},{... | collective-permute-start | bytes 580616 | tf_op jit(solution)/shard_map/ppermute | solution.py:53
  16.3 50.2 %collective-permute-start.5 = (f32[6,6,2,384]{3,2,1,0:T(2,128)S(1)}, f32[6,6,2,384]{3,2,1,0:T(2,128)S(1)}, u32[]{:S(2)}, u32[]{:S(2)}) collective-permute-start(f32[6,6,2,384]{3,2,1,0:T(2,128)S(1)} %get-tuple-element.28), channel_id=1, source_target_pairs={{4,2},{6,0},{8,6},{10,4},{12,10},{14,8},{5,3},{7,1},{9,7},{11,5},{... | collective-permute-start | bytes 331784 | tf_op jit(solution)/shard_map/ppermute | solution.py:53
  17.6 48.9 %collective-permute-start.4 = (f32[7,6,2,384]{3,2,1,0:T(2,128)S(1)}, f32[7,6,2,384]{3,2,1,0:T(2,128)S(1)}, u32[]{:S(2)}, u32[]{:S(2)}) collective-permute-start(f32[7,6,2,384]{3,2,1,0:T(2,128)S(1)} %get-tuple-element.27), channel_id=1, source_target_pairs={{0,6},{2,4},{4,10},{6,8},{8,14},{10,12},{1,7},{3,5},{5,11},{7,9},{... | collective-permute-start | bytes 387080 | tf_op jit(solution)/shard_map/ppermute | solution.py:53
  23.1 43.4 %collective-permute-start.2 = (f32[6,9,2,384]{3,2,1,0:T(2,128)S(1)}, f32[6,9,2,384]{3,2,1,0:T(2,128)S(1)}, u32[]{:S(2)}, u32[]{:S(2)}) collective-permute-start(f32[6,9,2,384]{3,2,1,0:T(2,128)S(1)} %get-tuple-element.25), channel_id=1, source_target_pairs={{4,0},{6,2},{8,4},{10,6},{12,8},{14,10},{5,1},{7,3},{9,5},{11,7},{... | collective-permute-start | bytes 497672 | tf_op jit(solution)/shard_map/ppermute | solution.py:53
  64.8 1.7 %copy-start = (f32[6,3,15,8,384]{4,3,2,1,0:T(8,128)}, f32[6,3,15,8,384]{4,3,2,1,0:T(8,128)S(1)}, u32[]{:S(2)}) copy-start(f32[6,3,15,8,384]{4,3,2,1,0:T(8,128)S(1)} %forcing.1.refs_6_) | copy-start | bytes 9953284
  66.5 11.8 %copy-start.1 = (f32[6,3,15,8,384]{4,3,2,1,0:T(8,128)S(1)}, f32[6,3,15,8,384]{4,3,2,1,0:T(8,128)}, u32[]{:S(2)}) copy-start(f32[6,3,15,8,384]{4,3,2,1,0:T(8,128)} %copy-done) | copy-start | bytes 9953284
  69.6 4.6 %collective-permute-start.6 = (f32[3,13,2,384]{3,2,1,0:T(2,128)S(1)}, f32[3,13,2,384]{3,2,1,0:T(2,128)S(1)}, u32[]{:S(2)}, u32[]{:S(2)}) collective-permute-start(f32[3,13,2,384]{3,2,1,0:T(2,128)S(1)} %get-tuple-element.32), channel_id=1, source_target_pairs={{0,4},{2,6},{4,8},{6,10},{8,12},{10,14},{1,5},{3,7},{5,9},{7,11},{... | collective-permute-start | bytes 359432 | tf_op jit(solution)/shard_map/ppermute | solution.py:53
  70.9 7.4 %collective-permute-start.7 = (f32[3,13,2,384]{3,2,1,0:T(2,128)S(1)}, f32[3,13,2,384]{3,2,1,0:T(2,128)S(1)}, u32[]{:S(2)}, u32[]{:S(2)}) collective-permute-start(f32[3,13,2,384]{3,2,1,0:T(2,128)S(1)} %get-tuple-element.33), channel_id=1, source_target_pairs={{4,0},{6,2},{8,4},{10,6},{12,8},{14,10},{5,1},{7,3},{9,5},{11,7},{... | collective-permute-start | bytes 359432 | tf_op jit(solution)/shard_map/ppermute | solution.py:53
  79.9 3.7 %collective-permute-start.8 = (f32[3,11,2,384]{3,2,1,0:T(2,128)S(1)}, f32[3,11,2,384]{3,2,1,0:T(2,128)S(1)}, u32[]{:S(2)}, u32[]{:S(2)}) collective-permute-start(f32[3,11,2,384]{3,2,1,0:T(2,128)S(1)} %get-tuple-element.36), channel_id=1, source_target_pairs={{0,4},{2,6},{4,8},{6,10},{8,12},{10,14},{1,5},{3,7},{5,9},{7,11},{... | collective-permute-start | bytes 304136 | tf_op jit(solution)/shard_map/ppermute | solution.py:53
  81.3 6.5 %collective-permute-start.9 = (f32[3,11,2,384]{3,2,1,0:T(2,128)S(1)}, f32[3,11,2,384]{3,2,1,0:T(2,128)S(1)}, u32[]{:S(2)}, u32[]{:S(2)}) collective-permute-start(f32[3,11,2,384]{3,2,1,0:T(2,128)S(1)} %get-tuple-element.37), channel_id=1, source_target_pairs={{4,0},{6,2},{8,4},{10,6},{12,8},{14,10},{5,1},{7,3},{9,5},{11,7},{... | collective-permute-start | bytes 304136 | tf_op jit(solution)/shard_map/ppermute | solution.py:53
  89.9 3.7 %collective-permute-start.10 = (f32[3,2,360]{2,1,0:T(2,128)S(1)}, f32[3,2,360]{2,1,0:T(2,128)S(1)}, u32[]{:S(2)}, u32[]{:S(2)}) collective-permute-start(f32[3,2,360]{2,1,0:T(2,128)S(1)} %get-tuple-element.41), channel_id=1, source_target_pairs={{0,2},{2,0},{1,3},{3,1},{4,6},{6,4},{5,7},{7,5},{8,10},{10,8},{9,1... | collective-permute-start | bytes 25928 | tf_op jit(solution)/shard_map/ppermute | solution.py:456

commit v2 on v1

v2 whole, which is shorter than its diff:
```python
import functools

import jax
import jax.numpy as jnp
from jax import lax
from jax.experimental import pallas as pl
from jax.experimental.pallas import tpu as pltpu
from jax.sharding import PartitionSpec as P

STEPS = 6
WIDTH = 2
ROUNDS = STEPS // WIDTH
LANES = 128
CHUNK = 3072
F32 = jnp.float32
BF16 = jnp.bfloat16
VMEM = pl.BlockSpec(memory_space=pltpu.VMEM)
SMEM = pl.BlockSpec(memory_space=pltpu.SMEM)
HBM = pl.BlockSpec(memory_space=pltpu.HBM)
MIB = 1024 * 1024


def window(margin, levels):
    count = lax.axis_size("levels")
    if count == 1:
        return 0, levels
    if count == 2:
        return lax.axis_index("levels") * (STEPS - margin), levels + margin
    return STEPS - margin, levels + 2 * margin


def level_moves(levels):
    count = lax.axis_size("levels")
    band = lax.axis_index("levels")
    if count == 1:
        return []
    if count == 2:
        return [([(0, 1), (1, 0)], (levels - STEPS) * (1 - band), levels * (1 - band))]
    up = [(i, i + 1) for i in range(count - 1)]
    down = [(i + 1, i) for i in range(count - 1)]
    return [(up, levels - STEPS, 0), (down, 0, STEPS + levels)]


def swap_tiles(value, odd):
    tiles = lax.axis_size("tiles")
    pairs = []
    for low in range(odd, tiles - 1, 2):
        pairs += [(low, low + 1), (low + 1, low)]
    return lax.ppermute(value, "tiles", pairs)


def is_even():
    return lax.rem(lax.axis_index("tiles"), 2) == 0


def own_planes(adj, lon, lat, flags, mix):
    tracers, levels, rows, _ = adj.shape
    last_band = lax.axis_index("levels") == lax.axis_size("levels") - 1
    last_tile = lax.axis_index("tiles") == lax.axis_size("tiles") - 1
    shape = lon.shape
    level_ids = lax.broadcasted_iota(jnp.int32, shape, 0)
    row_ids = lax.broadcasted_iota(jnp.int32, shape, 1)
    top = (level_ids == levels - 1) & last_band
    shut = (row_ids == rows - 1) & last_tile
    first = flags[0].astype(F32)
    second = flags[1].astype(F32)
    lat_open = jnp.where(shut, 0.0, lat[...])
    planes = [adj[t] for t in range(tracers)]
    planes.append(jnp.where(top, 0.0, mix[...]))
    planes.append(lon[...] * first)
    planes.append(lon[...] * (1.0 - first))
    planes.append(lat_open * second)
    planes.append(lat_open * (1.0 - second))
    return planes


def fetch(sources, targets, sems):
    copies = [pltpu.make_async_copy(x, y, sems.at[i]) for i, (x, y) in enumerate(zip(sources, targets))]
    for copy in copies:
        copy.start()
    for copy in copies:
        copy.wait()


def edges_kernel(*refs):
    inputs, (own_out, edge_out), held, buf, sems = refs[:5], refs[5:7], refs[7:12], refs[12], refs[13]
    fetch(inputs, held, sems)
    _, levels, rows, columns = held[0].shape
    width = edge_out.shape[-1]
    tail = columns // LANES * LANES
    gap = columns - tail
    buf[...] = jnp.zeros_like(buf)
    for p, plane in enumerate(own_planes(*held)):
        buf[p, :, 0:rows, 0:columns] = plane
    own_out[...] = buf[:, :, 0:rows, :]
    lane = lax.broadcasted_iota(jnp.int32, (8, LANES), 1)
    for p in range(buf.shape[0]):
        for l in range(levels):
            start = pltpu.roll(buf[p, l, :, 0:LANES], gap, 1)
            end = pltpu.roll(buf[p, l, :, tail : tail + LANES], width - gap, 1)
            both = jnp.where(
                lane >= width - STEPS,
                end,
                jnp.where((lane >= gap) & (lane < gap + STEPS), start, 0.0),
            )
            edge_out[p, l] = both[0:rows]


def payload_kernel(number, *refs):
    inputs, out, held, flat, sems = refs[: 4 + number], refs[4 + number], refs[5 + number : -2], refs[-2], refs[-1]
    fetch(inputs, held, sems)
    misfit, kernel, owner, target = held[:4]
    tracers, levels = misfit.shape[0], kernel.shape[0]
    base = tracers + 2
    flat[...] = jnp.zeros_like(flat)
    flat[0:tracers] = misfit[...]
    flat[tracers : tracers + 1] = owner[...].astype(F32)
    flat[tracers + 1 : base] = target[...].astype(F32).reshape(1, target.shape[0])
    if number == 0:
        flat[base : base + levels] = kernel[...]
    elif number == 1:
        far = inputs[4]

        @pl.when(lax.axis_index("levels") == 0)
        def _():
            flat[base : base + levels] = kernel[...]
            flat[base + levels : base + levels + STEPS] = far[0:STEPS]

        @pl.when(lax.axis_index("levels") == 1)
        def _():
            flat[base : base + STEPS] = far[levels - STEPS : levels]
            flat[base + STEPS : base + STEPS + levels] = kernel[...]
    else:
        flat[base : base + STEPS] = inputs[4][levels - STEPS : levels]
        flat[base + STEPS : base + STEPS + levels] = kernel[...]
        flat[base + STEPS + levels : base + 2 * STEPS + levels] = inputs[5][0:STEPS]
    for copy in range(out.shape[0]):
        for group in range(out.shape[1]):
            out[copy, group] = flat[4 * group : 4 * group + 4]


def with_edges(plane, edge, columns):
    tail = columns // LANES * LANES
    lane = lax.broadcasted_iota(jnp.int32, plane.shape[:-1] + (LANES,), 2)
    return jnp.where(lane < columns - tail, plane[..., tail : tail + LANES], edge)


def levels_kernel(moves, columns, own, edge, *outs):
    tail = columns // LANES * LANES
    for out, (_, start, _) in zip(outs, moves()):
        pick = pl.ds(start, STEPS)
        out[..., 0:tail] = own[:, pick, :, 0:tail]
        for p in range(own.shape[0]):
            out[p, :, :, tail : tail + LANES] = with_edges(own[p, pick], edge[p, pick], columns)


def tiles_kernel(moves, columns, own, edge, *refs):
    number = len(moves())
    far, (body, first_out, second_out) = refs[:number], refs[number:]
    planes, levels, rows, _ = own.shape
    tracers = planes - 5
    tail = columns // LANES * LANES
    mixing, east, west, north, south = range(tracers, planes)
    start, _ = window(0, levels)
    pick = pl.ds(start, levels)
    body[:, pick, :, 0:tail] = own[:, :, :, 0:tail]
    for p in range(planes):
        body[p, pick, :, tail : tail + LANES] = with_edges(own[p], edge[p], columns)
    for part, (_, _, slot) in zip(far, moves()):
        body[:, pl.ds(slot, STEPS)] = part[...]

    def rows_of(out, first, single):
        for entry, p in enumerate(list(range(tracers)) + [mixing, north, south]):
            out[entry] = body[p, :, first : first + WIDTH, :]
        out[tracers + 3, :, 0:1, :] = body[east, :, single : single + 1, :]
        out[tracers + 3, :, 1:2, :] = body[west, :, single : single + 1, :]

    @pl.when(is_even())
    def _():
        rows_of(first_out, rows - WIDTH, rows - 1)
        rows_of(second_out, 0, 0)

    @pl.when(jnp.logical_not(is_even()))
    def _():
        rows_of(first_out, 0, 0)
        rows_of(second_out, rows - WIDTH, rows - 1)


def advance(step, src, dst, coef, forcing, index, profile, flux, levels):
    tracers = src.shape[0]
    first, count = window(STEPS - 1 - step, levels)
    own, _ = window(0, levels)
    lanes = src.shape[-1]
    total = [flux[t] for t in range(tracers)]
    for i in range(count):
        at = first + i
        up, down = coef[0, at + 1], coef[0, at]
        east, west, north, south = (coef[c, at + 1] for c in range(1, 5))
        own_id = at - own
        inside = (own_id >= 0) & (own_id < levels)
        weight = jnp.where(inside, profile[jnp.clip(own_id, 0, levels - 1)], 0.0)
        for t in range(tracers):
            a = src[t, at + 1]
            b = a + up * (src[t, at + 2] - a) + down * (src[t, at] - a)
            moved = b + east * (pltpu.roll(b, lanes - 1, 1) - b) + west * (pltpu.roll(b, 1, 1) - b)
            moved = moved + north * (pltpu.roll(b, 7, 0) - b) + south * (pltpu.roll(b, 1, 0) - b)
            new = moved + forcing[index, t, at]
            dst[t, at + 1] = new
            total[t] = total[t] + weight * new
    for t in range(tracers):
        flux[t] = total[t]


def clear_pads(ref):
    levels = ref.shape[1]
    ref[:, 0:1] = jnp.zeros((ref.shape[0], 1) + ref.shape[2:], F32)
    ref[:, levels - 1 : levels] = jnp.zeros((ref.shape[0], 1) + ref.shape[2:], F32)


def run_steps(number, work, other, coef, forcing, profile, flux, levels):
    refs = [work, other]
    for i in range(WIDTH):
        advance(number * WIDTH + i, refs[i % 2], refs[(i + 1) % 2], coef, forcing, i, profile, flux, levels)
    return refs[WIDTH % 2]


def send_rows(number, state, first_out, second_out, rows, levels):
    start, count = window(STEPS - (number + 1) * WIDTH, levels)
    upper = state[:, pl.ds(start + 1, count), rows - WIDTH : rows, :]
    lower = state[:, pl.ds(start + 1, count), 0:WIDTH, :]
    even = is_even()
    first_out[...] = jnp.where(even, upper, lower)
    second_out[...] = jnp.where(even, lower, upper)


def first_kernel(levels, body, first, second, forcing, profile, *refs):
    state_out, coef_out, flux, first_out, second_out, work, other, raw = refs
    planes, wide, rows, lanes = body.shape
    tracers = planes - 5
    mixing, east, west, north, south = range(tracers, planes)
    raw[...] = jnp.zeros_like(raw)
    flux[...] = jnp.zeros_like(flux)
    clear_pads(work)
    clear_pads(other)
    even = is_even()
    pick = slice(1, wide + 1)
    for p in range(planes):
        ref, plane = (work, p) if p < tracers else (raw, p - tracers)
        ref[plane, pick, 0:rows, :] = body[p]
    for entry, p in enumerate(list(range(tracers)) + [mixing, north, south]):
        ref, plane = (work, p) if p < tracers else (raw, p - tracers)
        ref[plane, pick, rows : rows + WIDTH, :] = jnp.where(even, first[entry], second[entry])
        ref[plane, pick, 8 - WIDTH : 8, :] = jnp.where(even, second[entry], first[entry])
    for k, p in enumerate((east, west)):
        one, two = first[tracers + 3, :, k : k + 1, :], second[tracers + 3, :, k : k + 1, :]
        raw[p - tracers, pick, rows : rows + 1, :] = jnp.where(even, one, two)
        raw[p - tracers, pick, 7:8, :] = jnp.where(even, two, one)
    coef_out[0] = raw[0]
    coef_out[1] = raw[1]
    coef_out[3] = raw[3]
    for l in range(raw.shape[1]):
        coef_out[2, l] = pltpu.roll(raw[2, l], 1, 1)
        coef_out[4, l] = pltpu.roll(raw[4, l], 1, 0)
    last = run_steps(0, work, other, coef_out, forcing, profile, flux, levels)
    state_out[...] = last[...]
    send_rows(0, state_out, first_out, second_out, rows, levels)


def next_kernel(number, levels, rows, state, coef, first, second, forcing, profile, flux_in, *refs):
    work, other = refs[-2:]
    start, count = window(STEPS - number * WIDTH, levels)
    pick = pl.ds(start + 1, count)
    even = is_even()
    work[...] = state[...]
    work[:, pick, rows : rows + WIDTH, :] = jnp.where(even, first[...], second[...])
    work[:, pick, 8 - WIDTH : 8, :] = jnp.where(even, second[...], first[...])
    clear_pads(other)
    if number < ROUNDS - 1:
        state_out, flux, first_out, second_out = refs[:-2]
        flux[...] = flux_in[...]
        last = run_steps(number, work, other, coef, forcing, profile, flux, levels)
        state_out[...] = last[...]
        send_rows(number, state_out, first_out, second_out, rows, levels)
        return
    adjoint, keep, give, flux = refs[:-2]
    flux[...] = flux_in[...]
    last = run_steps(number, work, other, coef, forcing, profile, flux, levels)
    own, _ = window(0, levels)
    columns = adjoint.shape[-1]
    adjoint[...] = last[:, pl.ds(own + 1, levels), 0:rows, 0:columns]
    if lax.axis_size("levels") == 2:
        half = rows // 2
        upper = lax.axis_index("levels") == 1
        low, high = flux[:, 0:half, 0:columns], flux[:, half:rows, 0:columns]
        keep[...] = jnp.where(upper, high, low)
        give[...] = jnp.where(upper, low, high)
    else:
        keep[...] = flux[:, 0:rows, 0:columns]
        give[...] = jnp.zeros_like(give)


def forcing_kernel(number, tracers, levels, rows, columns, near, far, out, left, right, terms, flat, parts):
    sources, groups, _, held = near.shape
    lanes = out.shape[-1]
    subs = lax.axis_size("sub")
    tile, sub = lax.axis_index("tiles"), lax.axis_index("sub")
    for s in range(sources * subs):
        ref = near if s < sources else far
        for group in range(groups):
            flat[4 * group : 4 * group + 4, s * held : (s + 1) * held] = ref[s % sources, group]
    owner = flat[tracers : tracers + 1, :]
    target = flat[tracers + 1 : tracers + 2, :]
    cells = rows * columns
    step = jnp.floor((target + 0.5) * (1.0 / cells))
    cell = target - step * cells
    row = jnp.floor((cell + 0.5) * (1.0 / columns))
    col = cell - row * columns
    owner_tile = jnp.floor((owner + 0.5) * (1.0 / subs))
    row = row + (owner_tile - tile.astype(F32)) * rows
    shift = owner - owner_tile * subs - sub.astype(F32)
    col = col + jnp.where(shift < 0, shift + subs, shift) * columns
    east_side = col < columns + STEPS
    west_side = col >= subs * columns - STEPS
    lane = jnp.where(east_side, col, jnp.where(west_side, col - subs * columns + lanes, -1.0))
    close = (row >= 1 - WIDTH) & (row <= rows + WIDTH - 2)
    key = jnp.where(close, step * 8 + jnp.where(row < 0, row + 8, row), -1.0)
    for start in range(0, lanes, LANES):
        ids = lax.broadcasted_iota(jnp.int32, (LANES, lane.shape[1]), 0).astype(F32) + start
        right[start : start + LANES] = jnp.where(ids == lane, 1.0, 0.0).astype(BF16)
    for t in range(tracers):
        value = flat[...] * flat[t : t + 1, :]
        high = value.astype(BF16).astype(F32)
        parts[0, t] = high
        parts[1, t] = value - high
    first, count = window(STEPS - 1 - WIDTH * number, levels)
    batch = flat.shape[1]
    for i in range(count):
        for t in range(tracers):
            row_id = pl.ds(tracers + 2 + first + i, 1)
            both = [jnp.broadcast_to(parts[k, t, row_id, :], (8, batch)) for k in range(2)]
            terms[i * tracers + t] = jnp.concatenate(both, axis=0).astype(BF16)
    ids = lax.broadcasted_iota(jnp.int32, (8, batch), 0).astype(F32)
    for i in range(WIDTH):
        now = number * WIDTH + i
        begin, size = window(STEPS - 1 - now, levels)
        hit = jnp.where(key == ids + now * 8.0, 1.0, 0.0)
        mask = jnp.concatenate([hit, hit], axis=0).astype(BF16)
        offset = (begin - first) * tracers

        def fill(q, carry, mask=mask, offset=offset):
            left[pl.ds(pl.multiple_of(q * 16, 16), 16), :] = terms[offset + q] * mask
            return carry

        lax.fori_loop(0, size * tracers, fill, 0)
        product = lax.dot_general(
            left[0 : size * tracers * 16, :],
            right[...],
            (((1,), (1,)), ((), ())),
            preferred_element_type=F32,
        )
        for l in range(size):
            for t in range(tracers):
                base = (l * tracers + t) * 16
                value = product[base : base + 8] + product[base + 8 : base + 16]
                if pl.num_programs(0) == 1:
                    out[i, t, begin + l] = value
                else:
                    old = jnp.where(pl.program_id(0) == 0, 0.0, out[i, t, begin + l])
                    out[i, t, begin + l] = old + value


def per_device(
    final_adjoint,
    lon_courant,
    lat_courant,
    upwind_flags,
    vertical_mixing,
    level_profile,
    sounding_owner,
    sounding_target,
    misfit,
    averaging_kernel,
):
    tracers, levels, rows, columns = final_adjoint.shape
    held = misfit.shape[1]
    bands, subs, tiles = (lax.axis_size(name) for name in ("levels", "sub", "tiles"))
    planes = tracers + 5
    lanes = -(-(columns + 2 * STEPS) // LANES) * LANES
    wide = window(STEPS, levels)[1]
    moves = functools.partial(level_moves, levels)
    number = len(moves())
    shape = lambda *dims: jax.ShapeDtypeStruct(dims, F32)
    sub_pairs = [(i, (i + 1) % subs) for i in range(subs)]

    def call(body, limit, flops=0, **kwargs):
        return pl.pallas_call(
            body,
            compiler_params=pltpu.CompilerParams(vmem_limit_bytes=limit * MIB),
            cost_estimate=pl.CostEstimate(flops=flops, bytes_accessed=MIB, transcendentals=0),
            **kwargs,
        )

    def room(*arrays):
        return [pltpu.VMEM(x.shape, x.dtype) for x in arrays]

    beside = [lax.ppermute(averaging_kernel, "levels", pairs) for pairs, _, _ in moves()]
    fields = (final_adjoint, lon_courant, lat_courant, upwind_flags, vertical_mixing)
    own, edge = call(
        edges_kernel,
        60,
        out_shape=(shape(planes, levels, rows, lanes), shape(planes, levels, rows, LANES)),
        in_specs=[HBM] * 5,
        out_specs=(VMEM, VMEM),
        scratch_shapes=room(*fields)
        + [pltpu.VMEM((planes, levels, 8, lanes), F32), pltpu.SemaphoreType.DMA((5,))],
        name="edges",
    )(*fields)
    edge = lax.ppermute(edge, "sub", sub_pairs)
    inputs = (misfit, averaging_kernel, sounding_owner.reshape(1, held), sounding_target, *beside)
    groups = -(-(tracers + 2 + wide) // 4)
    payload = call(
        functools.partial(payload_kernel, number),
        16 if held <= 1024 else 32,
        out_shape=shape(tiles, groups, 4, held),
        in_specs=[HBM] * 4 + [VMEM] * number,
        out_specs=VMEM,
        scratch_shapes=room(*inputs[:4])
        + [pltpu.VMEM((-(-groups // 2) * 8, held), F32), pltpu.SemaphoreType.DMA((4,))],
        name="payload",
    )(*inputs)
    near = lax.all_to_all(payload, "tiles", split_axis=0, concat_axis=0, tiled=True)
    far = lax.ppermute(near, "sub", sub_pairs)

    sent = call(
        functools.partial(levels_kernel, moves, columns),
        8,
        out_shape=[shape(planes, STEPS, rows, lanes)] * number,
        in_specs=[VMEM] * 2,
        out_specs=[VMEM] * number,
        name="levels",
    )(own, edge)
    parts = [lax.ppermute(part, "levels", pairs) for part, (pairs, _, _) in zip(sent, moves())]
    message = shape(tracers + 4, wide, WIDTH, lanes)
    body, first, second = call(
        functools.partial(tiles_kernel, moves, columns),
        8,
        out_shape=(shape(planes, wide, rows, lanes), message, message),
        in_specs=[VMEM] * (2 + number),
        out_specs=[VMEM] * 3,
        name="tiles",
    )(own, edge, *parts)
    first, second = swap_tiles(first, 0), swap_tiles(second, 1)

    sources = max(1, min(tiles, CHUNK // (subs * held)))
    batch = sources * subs * held
    force_shape = (WIDTH, tracers, wide, 8, lanes)

    def forcing_of(round_id):
        count = window(STEPS - 1 - WIDTH * round_id, levels)[1]
        depth = -(-groups // 2) * 8
        block = pl.BlockSpec((sources, groups, 4, held), lambda i: (i, 0, 0, 0))
        return call(
            functools.partial(forcing_kernel, round_id, tracers, levels, rows, columns),
            20 if batch <= CHUNK else 60,
            flops=4 * count * tracers * 16 * batch * lanes,
            out_shape=shape(*force_shape),
            grid=(tiles // sources,),
            in_specs=[block, block],
            out_specs=pl.BlockSpec(force_shape, lambda i: (0, 0, 0, 0, 0)),
            scratch_shapes=[
                pltpu.VMEM((count * tracers * 16, batch), BF16),
                pltpu.VMEM((lanes, batch), BF16),
                pltpu.VMEM((count * tracers, 16, batch), BF16),
                pltpu.VMEM((depth, batch), F32),
                pltpu.VMEM((2, tracers, depth, batch), F32),
            ],
            name="forcing" + str(round_id),
        )(near, far)

    forcings = [forcing_of(i) for i in range(ROUNDS)]
    state_shape = (tracers, wide + 2, 8, lanes)
    coef_shape = (5, wide + 2, 8, lanes)
    flux_shape = (tracers, 8, lanes)

    def messages(round_id):
        count = window(STEPS - round_id * WIDTH, levels)[1]
        return [shape(tracers, count, WIDTH, lanes)] * 2

    scratch = [pltpu.VMEM(state_shape, F32)] * 2
    state, coef, flux, first, second = call(
        functools.partial(first_kernel, levels),
        12,
        out_shape=[shape(*state_shape), shape(*coef_shape), shape(*flux_shape), *messages(1)],
        in_specs=[VMEM] * 4 + [SMEM],
        out_specs=[VMEM] * 5,
        scratch_shapes=scratch + [pltpu.VMEM(coef_shape, F32)],
        name="round0",
    )(body, first, second, forcings[0], level_profile)
    half = rows // 2 if bands == 2 else rows
    for round_id in range(1, ROUNDS):
        first, second = swap_tiles(first, 0), swap_tiles(second, 1)
        if round_id < ROUNDS - 1:
            outs = [shape(*state_shape), shape(*flux_shape), *messages(round_id + 1)]
            extra = []
        else:
            part = shape(tracers, half, columns)
            outs = [shape(tracers, levels, rows, columns), part, part]
            extra = [pltpu.VMEM(flux_shape, F32)]
        results = call(
            functools.partial(next_kernel, round_id, levels, rows),
            12,
            out_shape=outs,
            in_specs=[VMEM] * 5 + [SMEM, VMEM],
            out_specs=[VMEM] * len(outs),
            scratch_shapes=extra + scratch,
            name="round" + str(round_id),
        )(state, coef, first, second, forcings[round_id], level_profile, flux)
        if round_id < ROUNDS - 1:
            state, flux, first, second = results
    adjoint, keep, give = results
    if bands == 2:
        flux_gradient = keep + lax.ppermute(give, "levels", [(0, 1), (1, 0)])
    else:
        flux_gradient = lax.psum_scatter(keep, "levels", scatter_dimension=1, tiled=True)
    return adjoint, flux_gradient


def solution(mesh):
    return jax.shard_map(
        per_device,
        mesh=mesh,
        in_specs=(
            P("groups", "levels", "tiles", "sub"),
            P(("groups", "levels"), "tiles", "sub"),
            P(("groups", "levels"), "tiles", "sub"),
            P(None, ("groups", "levels"), "tiles", "sub"),
            P(("groups", "levels"), "tiles", "sub"),
            P("levels"),
            P(("groups", "tiles", "sub"), None),
            P(("groups", "tiles", "sub")),
            P(None, ("groups", "tiles", "sub")),
            P("levels", ("groups", "tiles", "sub")),
        ),
        out_specs=(P("groups", "levels", "tiles", "sub"), P("groups", ("tiles", "levels"), "sub")),
        check_vma=False,
    )
```

time: 94.8 us -> 59.3 us (0.63)
  blocking collectives: 23.3 us -> 10.7 us
  waiting for transfers between devices: 14.5 us -> 3.37 us
  local copies, waits for them, and re-layouts: 8.73 us -> 1.04 us
  starting transfers between devices: 21.8 us -> 15.1 us
  Pallas kernels: 24.4 us -> 27.4 us
    all_gather x1 -> x0, blocking collectives: 23.3 us -> none  [per_device(): gathered = lax.all_gather(payload, ('levels', 'tiles', 'sub'))]
    ppermute x10, waiting for transfers between devices: 12.4 us -> 1.03 us  [the longest x6 1.01 us: swap_tiles(): return lax.ppermute(value, 'tiles', pairs)]
    all_to_all x0 -> x1, blocking collectives: none -> 10.7 us  [per_device(): lax.all_to_all(payload, 'tiles', split_axis=0, concat_axis=0, tiled=True)]
    unnamed x22 -> x14, local copies, waits for them, and re-layouts: 8.04 us -> 1.04 us
    ppermute x10, starting transfers between devices: 20.3 us -> 13.8 us  [the longest x6 9.13 us: swap_tiles(): return lax.ppermute(value, 'tiles', pairs)]
    pallas_call x6 -> x10, Pallas kernels: 24.4 us -> 27.4 us  [the longest x3 18.7 us: forcing_of(): call(functools.partial(forcing_kernel, round_id, tracers, levels, rows, c...]
  transfers between devices with their start and end apart: 11 -> 11, of which waited for: 6 -> 2; matrix products, arithmetic and copies ran while one was open for 0% -> 0% of each run, Pallas kernels for 18% -> 32%
where the time goes in v2:
time: 59.3 us; the launch traced here: 59 us
  Pallas kernels  27.4 us (46%)
  starting transfers between devices  15.1 us (25%)
  blocking collectives  10.7 us (18%)
  waiting for transfers between devices  3.37 us (6%)
  local copies, waits for them, and re-layouts  1.04 us (2%)
  between operations  0.82 us (1%)
  other arithmetic  0.6 us (1%)
    pallas_call x3, Pallas kernels, forcing_of(): call(functools.partial(forcing_kernel, round_id, tracers, levels, rows, c...  18.7 us
    all_to_all x1, blocking collectives, per_device(): lax.all_to_all(payload, 'tiles', split_axis=0, concat_axis=0, tiled=True)  10.7 us
    ppermute x6, starting transfers between devices, swap_tiles(): return lax.ppermute(value, 'tiles', pairs)  9.13 us
    pallas_call x2, Pallas kernels, per_device(): call(functools.partial(next_kernel, round_id, levels, rows), 12, out_shap...  3.75 us
    ppermute x1, starting transfers between devices, per_device(): lax.ppermute(averaging_kernel, 'levels', pairs)  2.56 us
    pallas_call x1, Pallas kernels, per_device(): call(functools.partial(first_kernel, levels), 12, out_shape=[shape(*state...  2.45 us
    ppermute x1, waiting for transfers between devices, per_device(): flux_gradient = keep + lax.ppermute(give, 'levels', [(0, 1), (1, 0)])  2.34 us
    pallas_call x1, Pallas kernels, per_device(): call(edges_kernel, 60, out_shape=(shape(planes, levels, rows, lanes), sha...  2.1 us
  transfers between devices with their start and end apart: 11, of which 2 were waited for; matrix products, arithmetic and copies ran while one was open for 0% of the time, Pallas kernels for 32%

profile of v2, /device:TPU:0, one launch (start us, length us, event | category | flops | bytes accessed | tf_op | source)
XLA Modules:
  0.0 59.0 jit_solution(4304143872959765992)
XLA Ops:
  0.7 2.1 %edges.1 = (f32[8,9,4,384]{3,2,1,0:T(4,128)}, f32[8,9,4,128]{3,2,1,0:T(4,128)}) custom-call(f32[3,9,4,360]{3,2,1,0:T(4,128)} %refs_0_.2, f32[9,4,360]{2,1,0:T(4,128)} %refs_1_.2, f32[9,4,360]{2,1,0:T(4,128)} %refs_2_.1, s32[2,9,4,360]{3,2,1,0:T(4,128)} %refs_3_.2, f32[9,4,360]{2,1,0:T(4,128)} %refs_4_.1), custom_call_target="tpu_custom_call" | custom-call | bytes 1048576 | tf_op jit(solution)/shard_map/edges/pallas_call | solution.py:408
  2.8 0.5 collective-permute-start
  3.3 2.6 %collective-permute-start.4 = (f32[9,384]{1,0:T(8,128)}, f32[9,384]{1,0:T(8,128)S(1)}, u32[]{:S(2)}, u32[]{:S(2)}) collective-permute-start(f32[9,384]{1,0:T(8,128)} %refs_1_.3), channel_id=1, source_target_pairs={{0,2},{2,0},{1,3},{3,1},{4,6},{6,4},{5,7},{7,5},{8,10},{10,8},{9,1... | collective-permute-start | bytes 41480 | tf_op jit(solution)/shard_map/ppermute | solution.py:406
  5.9 1.0 %copy-done = f32[8,9,4,384]{3,2,1,0:T(4,128)S(1)} copy-done((f32[8,9,4,384]{3,2,1,0:T(4,128)S(1)}, f32[8,9,4,384]{3,2,1,0:T(4,128)}, u32[]{:S(2)}) %copy-start) | copy-done | bytes 442392
  6.9 1.6 %collective-permute-start.1 = (f32[8,6,4,384]{3,2,1,0:T(4,128)S(1)}, f32[8,6,4,384]{3,2,1,0:T(4,128)S(1)}, u32[]{:S(2)}, u32[]{:S(2)}) collective-permute-start(f32[8,6,4,384]{3,2,1,0:T(4,128)S(1)} %levels.1), channel_id=1, source_target_pairs={{0,2},{2,0},{1,3},{3,1},{4,6},{6,4},{5,7},{7,5},{8,10},{10,8},{9,1... | collective-permute-start | bytes 884744 | tf_op jit(solution)/shard_map/ppermute | solution.py:442
  8.5 0.1 payload.1
  8.6 10.7 %all_to_all.5.near = f32[4,5,4,384]{3,2,1,0:T(4,128)S(1)} all-to-all(f32[4,5,4,384]{3,2,1,0:T(4,128)S(1)} %payload.1), channel_id=1, replica_groups=mesh['groups'=2,'tiles'=4,'levels'=2,'sub'=2] {'tiles'}, dimensions={0} | all-to-all | bytes 245760 | tf_op jit(solution)/shard_map/all_to_all | solution.py:431
  19.3 0.3 tiles.1
  19.6 1.2 %collective-permute-start.2 = (f32[7,15,2,384]{3,2,1,0:T(2,128)S(1)}, f32[7,15,2,384]{3,2,1,0:T(2,128)S(1)}, u32[]{:S(2)}, u32[]{:S(2)}) collective-permute-start(f32[7,15,2,384]{3,2,1,0:T(2,128)S(1)} %get-tuple-element.22), channel_id=1, source_target_pairs={{0,4},{4,0},{8,12},{12,8},{1,5},{5,1},{9,13},{13,9},{2,6},{6,2},{1... | collective-permute-start | bytes 967688 | tf_op jit(solution)/shard_map/ppermute | solution.py:49
  20.8 0.8 %collective-permute-start.3 = (f32[7,15,2,384]{3,2,1,0:T(2,128)S(1)}, f32[7,15,2,384]{3,2,1,0:T(2,128)S(1)}, u32[]{:S(2)}, u32[]{:S(2)}) collective-permute-start(f32[7,15,2,384]{3,2,1,0:T(2,128)S(1)} %get-tuple-element.23), channel_id=1, source_target_pairs={{4,8},{8,4},{5,9},{9,5},{6,10},{10,6},{7,11},{11,7},{20,24},{24,20... | collective-permute-start | bytes 967688 | tf_op jit(solution)/shard_map/ppermute | solution.py:49
  21.7 7.0 %forcing0.1.forcing = f32[2,3,15,8,384]{4,3,2,1,0:T(8,128)S(1)} custom-call(f32[4,5,4,384]{3,2,1,0:T(4,128)S(1)} %all_to_all.5.near, f32[4,5,4,384]{3,2,1,0:T(4,128)S(1)} %collective-permute-done.5.far), custom_call_target="tpu_custom_call" | custom-call | flops 3170893824 | bytes 1048576 | tf_op jit(solution)/shard_map/forcing0/pallas_call | solution.py:462
  28.7 1.0 %collective-permute-done.2.first = f32[7,15,2,384]{3,2,1,0:T(2,128)S(1)} collective-permute-done((f32[7,15,2,384]{3,2,1,0:T(2,128)S(1)}, f32[7,15,2,384]{3,2,1,0:T(2,128)S(1)}, u32[]{:S(2)}, u32[]{:S(2)}) %collective-permute-start.2) | collective-permute-done | bytes 322592 | tf_op jit(solution)/shard_map/ppermute | solution.py:49
  29.7 2.4 %round0.1 = (f32[3,17,8,384]{3,2,1,0:T(8,128)S(1)}, f32[5,17,8,384]{3,2,1,0:T(8,128)S(1)}, f32[3,8,384]{2,1,0:T(8,128)S(1)}, f32[3,13,2,384]{3,2,1,0:T(2,128)S(1)}, f32[3,13,2,384]{3,2,1,0:T(2,128)S(1)}) custom-call(f32[8,15,4,384]{3,2,1,0:T(4,128)S(1)} %get-tuple-element.21.body, f32[7,15,2,384]{3,2,1,0:T(2,128)S(1)} %collective-permute-done.2.first, ...), custom_call_target="tpu_custom_call" | custom-call | bytes 1048576 | tf_op jit(solution)/shard_map/round0/pallas_call | solution.py:490
  32.2 3.8 %collective-permute-start.6 = (f32[3,13,2,384]{3,2,1,0:T(2,128)S(1)}, f32[3,13,2,384]{3,2,1,0:T(2,128)S(1)}, u32[]{:S(2)}, u32[]{:S(2)}) collective-permute-start(f32[3,13,2,384]{3,2,1,0:T(2,128)S(1)} %get-tuple-element.26), channel_id=1, source_target_pairs={{0,4},{4,0},{8,12},{12,8},{1,5},{5,1},{9,13},{13,9},{2,6},{6,2},{1... | collective-permute-start | bytes 359432 | tf_op jit(solution)/shard_map/ppermute | solution.py:49
  36.0 0.8 %collective-permute-start.7 = (f32[3,13,2,384]{3,2,1,0:T(2,128)S(1)}, f32[3,13,2,384]{3,2,1,0:T(2,128)S(1)}, u32[]{:S(2)}, u32[]{:S(2)}) collective-permute-start(f32[3,13,2,384]{3,2,1,0:T(2,128)S(1)} %get-tuple-element.27), channel_id=1, source_target_pairs={{4,8},{8,4},{5,9},{9,5},{6,10},{10,6},{7,11},{11,7},{20,24},{24,20... | collective-permute-start | bytes 359432 | tf_op jit(solution)/shard_map/ppermute | solution.py:49
  36.8 6.2 %forcing1.1.forcing = f32[2,3,15,8,384]{4,3,2,1,0:T(8,128)S(1)} custom-call(f32[4,5,4,384]{3,2,1,0:T(4,128)S(1)} %all_to_all.5.near, f32[4,5,4,384]{3,2,1,0:T(4,128)S(1)} %collective-permute-done.5.far), custom_call_target="tpu_custom_call" | custom-call | flops 2717908992 | bytes 1048576 | tf_op jit(solution)/shard_map/forcing1/pallas_call | solution.py:462
  43.1 1.7 %round1.1 = (f32[3,17,8,384]{3,2,1,0:T(8,128)S(1)}, f32[3,8,384]{2,1,0:T(8,128)S(1)}, f32[3,11,2,384]{3,2,1,0:T(2,128)S(1)}, f32[3,11,2,384]{3,2,1,0:T(2,128)S(1)}) custom-call(f32[3,17,8,384]{3,2,1,0:T(8,128)S(1)} %get-tuple-element.24.state, f32[5,17,8,384]{3,2,1,0:T(8,128)S(1)} %get-tuple-element.25.coef, ...), custom_call_target="tpu_custom_call" | custom-call | bytes 1048576 | tf_op jit(solution)/shard_map/round1/pallas_call | solution.py:509
  44.8 1.8 %collective-permute-start.8 = (f32[3,11,2,384]{3,2,1,0:T(2,128)S(1)}, f32[3,11,2,384]{3,2,1,0:T(2,128)S(1)}, u32[]{:S(2)}, u32[]{:S(2)}) collective-permute-start(f32[3,11,2,384]{3,2,1,0:T(2,128)S(1)} %get-tuple-element.30), channel_id=1, source_target_pairs={{0,4},{4,0},{8,12},{12,8},{1,5},{5,1},{9,13},{13,9},{2,6},{6,2},{1... | collective-permute-start | bytes 304136 | tf_op jit(solution)/shard_map/ppermute | solution.py:49
  46.6 0.7 %collective-permute-start.9 = (f32[3,11,2,384]{3,2,1,0:T(2,128)S(1)}, f32[3,11,2,384]{3,2,1,0:T(2,128)S(1)}, u32[]{:S(2)}, u32[]{:S(2)}) collective-permute-start(f32[3,11,2,384]{3,2,1,0:T(2,128)S(1)} %get-tuple-element.31), channel_id=1, source_target_pairs={{4,8},{8,4},{5,9},{9,5},{6,10},{10,6},{7,11},{11,7},{20,24},{24,20... | collective-permute-start | bytes 304136 | tf_op jit(solution)/shard_map/ppermute | solution.py:49
  47.3 5.4 %forcing2.1.forcing = f32[2,3,15,8,384]{4,3,2,1,0:T(8,128)S(1)} custom-call(f32[4,5,4,384]{3,2,1,0:T(4,128)S(1)} %all_to_all.5.near, f32[4,5,4,384]{3,2,1,0:T(4,128)S(1)} %collective-permute-done.5.far), custom_call_target="tpu_custom_call" | custom-call | flops 2264924160 | bytes 1048576 | tf_op jit(solution)/shard_map/forcing2/pallas_call | solution.py:462
  52.7 2.0 %round2.1 = (f32[3,9,4,360]{3,2,1,0:T(4,128)}, f32[3,2,360]{2,1,0:T(2,128)S(1)}, f32[3,2,360]{2,1,0:T(2,128)S(1)}) custom-call(f32[3,17,8,384]{3,2,1,0:T(8,128)S(1)} %get-tuple-element.29.state, f32[5,17,8,384]{3,2,1,0:T(8,128)S(1)} %get-tuple-element.25.coef, f32[3,11,2,384]{3,2,1,0:T(2,128)S(1)} %collective-permute-done.8.first, ...), custom_call_target="tpu_custom_call" | custom-call | bytes 1048576 | tf_op jit(solution)/shard_map/round2/pallas_call | solution.py:509
  54.8 1.3 %collective-permute-start.10 = (f32[3,2,360]{2,1,0:T(2,128)S(1)}, f32[3,2,360]{2,1,0:T(2,128)S(1)}, u32[]{:S(2)}, u32[]{:S(2)}) collective-permute-start(f32[3,2,360]{2,1,0:T(2,128)S(1)} %get-tuple-element.35), channel_id=1, source_target_pairs={{0,2},{2,0},{1,3},{3,1},{4,6},{6,4},{5,7},{7,5},{8,10},{10,8},{9,1... | collective-permute-start | bytes 25928 | tf_op jit(solution)/shard_map/ppermute | solution.py:522
  56.1 2.3 %collective-permute-done.10 = f32[3,2,360]{2,1,0:T(2,128)S(1)} collective-permute-done((f32[3,2,360]{2,1,0:T(2,128)S(1)}, f32[3,2,360]{2,1,0:T(2,128)S(1)}, u32[]{:S(2)}, u32[]{:S(2)}) %collective-permute-start.10) | collective-permute-done | bytes 8672 | tf_op jit(solution)/shard_map/ppermute | solution.py:522
  58.4 0.6 %add.3 = f32[3,2,360]{2,1,0:T(2,128)} add(f32[3,2,360]{2,1,0:T(2,128)S(1)} %get-tuple-element.34, f32[3,2,360]{2,1,0:T(2,128)S(1)} %collective-permute-done.10) | non-fusion elementwise | flops 2160 | bytes 25920 | tf_op jit(solution)/shard_map/add | solution.py:522
  (24 shorter events, 0.1 us)
Async XLA Ops:
  0.6 7.9 %copy-start.2 = (f32[9,384]{1,0:T(8,128)S(1)}, f32[9,384]{1,0:T(8,128)}, u32[]{:S(2)}) copy-start(f32[9,384]{1,0:T(8,128)} %refs_1_.3) | copy-start | bytes 41476
  0.6 7.9 %copy-start.6 = (s32[384,1]{0,1:T(1,128)S(1)}, s32[384,1]{0,1:T(1,128)}, u32[]{:S(2)}) copy-start(s32[384,1]{0,1:T(1,128)} %param.16) | copy-start | bytes 4612
  0.7 7.9 %copy-start.5 = (s32[384]{0:T(512)S(1)}, s32[384]{0:T(512)}, u32[]{:S(2)}) copy-start(s32[384]{0:T(512)} %refs_3_.3) | copy-start | bytes 4612
  0.7 7.9 %copy-start.3 = (f32[3,384]{1,0:T(4,128)S(1)}, f32[3,384]{1,0:T(4,128)}, u32[]{:S(2)}) copy-start(f32[3,384]{1,0:T(4,128)} %refs_0_.3) | copy-start | bytes 13828
  2.8 3.1 %collective-permute-start = (f32[8,9,4,128]{3,2,1,0:T(4,128)}, f32[8,9,4,128]{3,2,1,0:T(4,128)S(1)}, u32[]{:S(2)}, u32[]{:S(2)}) collective-permute-start(f32[8,9,4,128]{3,2,1,0:T(4,128)} %get-tuple-element.20), channel_id=1, source_target_pairs={{0,1},{1,0},{2,3},{3,2},{4,5},{5,4},{6,7},{7,6},{8,9},{9,8},{10,11... | collective-permute-start | bytes 442376 | tf_op jit(solution)/shard_map/ppermute | solution.py:418
  3.3 5.2 %collective-permute-start.4 = (f32[9,384]{1,0:T(8,128)}, f32[9,384]{1,0:T(8,128)S(1)}, u32[]{:S(2)}, u32[]{:S(2)}) collective-permute-start(f32[9,384]{1,0:T(8,128)} %refs_1_.3), channel_id=1, source_target_pairs={{0,2},{2,0},{1,3},{3,1},{4,6},{6,4},{5,7},{7,5},{8,10},{10,8},{9,1... | collective-permute-start | bytes 41480 | tf_op jit(solution)/shard_map/ppermute | solution.py:406
  5.9 1.0 %copy-start = (f32[8,9,4,384]{3,2,1,0:T(4,128)S(1)}, f32[8,9,4,384]{3,2,1,0:T(4,128)}, u32[]{:S(2)}) copy-start(f32[8,9,4,384]{3,2,1,0:T(4,128)} %get-tuple-element.19.own) | copy-start | bytes 1327108
  6.9 12.4 %copy-start.1 = (f32[8,9,4,384]{3,2,1,0:T(4,128)S(1)}, f32[8,9,4,384]{3,2,1,0:T(4,128)}, u32[]{:S(2)}) copy-start(f32[8,9,4,384]{3,2,1,0:T(4,128)} %get-tuple-element.19.own) | copy-start | bytes 1327108
  6.9 12.4 %collective-permute-start.1 = (f32[8,6,4,384]{3,2,1,0:T(4,128)S(1)}, f32[8,6,4,384]{3,2,1,0:T(4,128)S(1)}, u32[]{:S(2)}, u32[]{:S(2)}) collective-permute-start(f32[8,6,4,384]{3,2,1,0:T(4,128)S(1)} %levels.1), channel_id=1, source_target_pairs={{0,2},{2,0},{1,3},{3,1},{4,6},{6,4},{5,7},{7,5},{8,10},{10,8},{9,1... | collective-permute-start | bytes 884744 | tf_op jit(solution)/shard_map/ppermute | solution.py:442
  19.3 2.3 %collective-permute-start.5 = (f32[4,5,4,384]{3,2,1,0:T(4,128)S(1)}, f32[4,5,4,384]{3,2,1,0:T(4,128)S(1)}, u32[]{:S(2)}, u32[]{:S(2)}) collective-permute-start(f32[4,5,4,384]{3,2,1,0:T(4,128)S(1)} %all_to_all.5.near), channel_id=1, source_target_pairs={{0,1},{1,0},{2,3},{3,2},{4,5},{5,4},{6,7},{7,6},{8,9},{9,8},{10,11... | collective-permute-start | bytes 368648 | tf_op jit(solution)/shard_map/ppermute | solution.py:432
  19.6 10.1 %collective-permute-start.2 = (f32[7,15,2,384]{3,2,1,0:T(2,128)S(1)}, f32[7,15,2,384]{3,2,1,0:T(2,128)S(1)}, u32[]{:S(2)}, u32[]{:S(2)}) collective-permute-start(f32[7,15,2,384]{3,2,1,0:T(2,128)S(1)} %get-tuple-element.22), channel_id=1, source_target_pairs={{0,4},{4,0},{8,12},{12,8},{1,5},{5,1},{9,13},{13,9},{2,6},{6,2},{1... | collective-permute-start | bytes 967688 | tf_op jit(solution)/shard_map/ppermute | solution.py:49
  20.8 8.9 %copy-start.4 = (f32[9]{0:T(128)S(1)}, f32[9]{0:T(128)}, u32[]{:S(2)}) copy-start(f32[9]{0:T(128)} %profile.5) | copy-start | bytes 112
  20.8 8.9 %collective-permute-start.3 = (f32[7,15,2,384]{3,2,1,0:T(2,128)S(1)}, f32[7,15,2,384]{3,2,1,0:T(2,128)S(1)}, u32[]{:S(2)}, u32[]{:S(2)}) collective-permute-start(f32[7,15,2,384]{3,2,1,0:T(2,128)S(1)} %get-tuple-element.23), channel_id=1, source_target_pairs={{4,8},{8,4},{5,9},{9,5},{6,10},{10,6},{7,11},{11,7},{20,24},{24,20... | collective-permute-start | bytes 967688 | tf_op jit(solution)/shard_map/ppermute | solution.py:49
  32.2 10.9 %collective-permute-start.6 = (f32[3,13,2,384]{3,2,1,0:T(2,128)S(1)}, f32[3,13,2,384]{3,2,1,0:T(2,128)S(1)}, u32[]{:S(2)}, u32[]{:S(2)}) collective-permute-start(f32[3,13,2,384]{3,2,1,0:T(2,128)S(1)} %get-tuple-element.26), channel_id=1, source_target_pairs={{0,4},{4,0},{8,12},{12,8},{1,5},{5,1},{9,13},{13,9},{2,6},{6,2},{1... | collective-permute-start | bytes 359432 | tf_op jit(solution)/shard_map/ppermute | solution.py:49
  36.0 7.1 %collective-permute-start.7 = (f32[3,13,2,384]{3,2,1,0:T(2,128)S(1)}, f32[3,13,2,384]{3,2,1,0:T(2,128)S(1)}, u32[]{:S(2)}, u32[]{:S(2)}) collective-permute-start(f32[3,13,2,384]{3,2,1,0:T(2,128)S(1)} %get-tuple-element.27), channel_id=1, source_target_pairs={{4,8},{8,4},{5,9},{9,5},{6,10},{10,6},{7,11},{11,7},{20,24},{24,20... | collective-permute-start | bytes 359432 | tf_op jit(solution)/shard_map/ppermute | solution.py:49
  44.8 7.9 %collective-permute-start.8 = (f32[3,11,2,384]{3,2,1,0:T(2,128)S(1)}, f32[3,11,2,384]{3,2,1,0:T(2,128)S(1)}, u32[]{:S(2)}, u32[]{:S(2)}) collective-permute-start(f32[3,11,2,384]{3,2,1,0:T(2,128)S(1)} %get-tuple-element.30), channel_id=1, source_target_pairs={{0,4},{4,0},{8,12},{12,8},{1,5},{5,1},{9,13},{13,9},{2,6},{6,2},{1... | collective-permute-start | bytes 304136 | tf_op jit(solution)/shard_map/ppermute | solution.py:49
  46.6 6.1 %collective-permute-start.9 = (f32[3,11,2,384]{3,2,1,0:T(2,128)S(1)}, f32[3,11,2,384]{3,2,1,0:T(2,128)S(1)}, u32[]{:S(2)}, u32[]{:S(2)}) collective-permute-start(f32[3,11,2,384]{3,2,1,0:T(2,128)S(1)} %get-tuple-element.31), channel_id=1, source_target_pairs={{4,8},{8,4},{5,9},{9,5},{6,10},{10,6},{7,11},{11,7},{20,24},{24,20... | collective-permute-start | bytes 304136 | tf_op jit(solution)/shard_map/ppermute | solution.py:49
  54.8 3.7 %collective-permute-start.10 = (f32[3,2,360]{2,1,0:T(2,128)S(1)}, f32[3,2,360]{2,1,0:T(2,128)S(1)}, u32[]{:S(2)}, u32[]{:S(2)}) collective-permute-start(f32[3,2,360]{2,1,0:T(2,128)S(1)} %get-tuple-element.35), channel_id=1, source_target_pairs={{0,2},{2,0},{1,3},{3,1},{4,6},{6,4},{5,7},{7,5},{8,10},{10,8},{9,1... | collective-permute-start | bytes 25928 | tf_op jit(solution)/shard_map/ppermute | solution.py:522

commit v3 on v2

--- a/solution.py
+++ b/solution.py
@@ -82,9 +82,33 @@
         copy.wait()
 
 
-def edges_kernel(*refs):
-    inputs, (own_out, edge_out), held, buf, sems = refs[:5], refs[5:7], refs[7:12], refs[12], refs[13]
+def soundings_of(number, flat, misfit, kernel, owner, target):
+    tracers, levels = misfit.shape[0], kernel.shape[0]
+    base = tracers + 2
+    flat[...] = jnp.zeros_like(flat)
+    flat[0:tracers] = misfit[...]
+    flat[tracers : tracers + 1] = owner[...].astype(F32)
+    flat[tracers + 1 : base] = target[...].astype(F32).reshape(1, target.shape[0])
+    if number == 1:
+
+        @pl.when(lax.axis_index("levels") == 0)
+        def _():
+            flat[base : base + levels] = kernel[...]
+
+        @pl.when(lax.axis_index("levels") == 1)
+        def _():
+            flat[base + STEPS : base + STEPS + levels] = kernel[...]
+    else:
+        start = base + (STEPS if number else 0)
+        flat[start : start + levels] = kernel[...]
+
+
+def edges_kernel(moves, *refs):
+    inputs, own_out, edge_out, base = refs[:9], refs[9], refs[10], refs[11]
+    outs, held, buf, sems = refs[12:-11], refs[-11:-2], refs[-2], refs[-1]
     fetch(inputs, held, sems)
+    soundings_of(len(moves()), base, *held[5:])
+    held = held[:5]
     _, levels, rows, columns = held[0].shape
     width = edge_out.shape[-1]
     tail = columns // LANES * LANES
@@ -104,39 +128,32 @@
                 jnp.where((lane >= gap) & (lane < gap + STEPS), start, 0.0),
             )
             edge_out[p, l] = both[0:rows]
-
-
-def payload_kernel(number, *refs):
-    inputs, out, held, flat, sems = refs[: 4 + number], refs[4 + number], refs[5 + number : -2], refs[-2], refs[-1]
-    fetch(inputs, held, sems)
-    misfit, kernel, owner, target = held[:4]
-    tracers, levels = misfit.shape[0], kernel.shape[0]
+    for i, (_, start, _) in enumerate(moves()):
+        outs[2 * i][...] = own_out[:, pl.ds(start, STEPS)]
+        outs[2 * i + 1][...] = edge_out[:, pl.ds(start, STEPS)]
+
+
+def payload_kernel(number, levels, tracers, *refs):
+    out, flat = refs[-2:]
     base = tracers + 2
-    flat[...] = jnp.zeros_like(flat)
-    flat[0:tracers] = misfit[...]
-    flat[tracers : tracers + 1] = owner[...].astype(F32)
-    flat[tracers + 1 : base] = target[...].astype(F32).reshape(1, target.shape[0])
-    if number == 0:
-        flat[base : base + levels] = kernel[...]
-    elif number == 1:
-        far = inputs[4]
-
-        @pl.when(lax.axis_index("levels") == 0)
-        def _():
-            flat[base : base + levels] = kernel[...]
-            flat[base + levels : base + levels + STEPS] = far[0:STEPS]
-
-        @pl.when(lax.axis_index("levels") == 1)
-        def _():
-            flat[base : base + STEPS] = far[levels - STEPS : levels]
-            flat[base + STEPS : base + STEPS + levels] = kernel[...]
-    else:
-        flat[base : base + STEPS] = inputs[4][levels - STEPS : levels]
-        flat[base + STEPS : base + STEPS + levels] = kernel[...]
-        flat[base + STEPS + levels : base + 2 * STEPS + levels] = inputs[5][0:STEPS]
-    for copy in range(out.shape[0]):
+    for half in range(2):
+        part = refs[half * (1 + number) : (half + 1) * (1 + number)]
+        flat[...] = part[0][...]
+        if number == 1:
+
+            @pl.when(lax.axis_index("levels") == 0)
+            def _(part=part):
+                flat[base + levels : base + levels + STEPS] = part[1][0:STEPS]
+
+            @pl.when(lax.axis_index("levels") == 1)
+            def _(part=part):
+                flat[base : base + STEPS] = part[1][levels - STEPS : levels]
+
+        if number == 2:
+            flat[base : base + STEPS] = part[1][levels - STEPS : levels]
+            flat[base + STEPS + levels : base + 2 * STEPS + levels] = part[2][0:STEPS]
         for group in range(out.shape[1]):
-            out[copy, group] = flat[4 * group : 4 * group + 4]
+            out[half, group] = flat[4 * group : 4 * group + 4]
 
 
 def with_edges(plane, edge, columns):
@@ -145,18 +162,9 @@
     return jnp.where(lane < columns - tail, plane[..., tail : tail + LANES], edge)
 
 
-def levels_kernel(moves, columns, own, edge, *outs):
-    tail = columns // LANES * LANES
-    for out, (_, start, _) in zip(outs, moves()):
-        pick = pl.ds(start, STEPS)
-        out[..., 0:tail] = own[:, pick, :, 0:tail]
-        for p in range(own.shape[0]):
-            out[p, :, :, tail : tail + LANES] = with_edges(own[p, pick], edge[p, pick], columns)
-
-
 def tiles_kernel(moves, columns, own, edge, *refs):
     number = len(moves())
-    far, (body, first_out, second_out) = refs[:number], refs[number:]
+    far, (body, first_out, second_out) = refs[: 2 * number], refs[2 * number :]
     planes, levels, rows, _ = own.shape
     tracers = planes - 5
     tail = columns // LANES * LANES
@@ -166,8 +174,12 @@
     body[:, pick, :, 0:tail] = own[:, :, :, 0:tail]
     for p in range(planes):
         body[p, pick, :, tail : tail + LANES] = with_edges(own[p], edge[p], columns)
-    for part, (_, _, slot) in zip(far, moves()):
-        body[:, pl.ds(slot, STEPS)] = part[...]
+    for i, (_, _, slot) in enumerate(moves()):
+        part, beside = far[2 * i], far[2 * i + 1]
+        there = pl.ds(slot, STEPS)
+        body[:, there, :, 0:tail] = part[:, :, :, 0:tail]
+        for p in range(planes):
+            body[p, there, :, tail : tail + LANES] = with_edges(part[p], beside[p], columns)
 
     def rows_of(out, first, single):
         for entry, p in enumerate(list(range(tracers)) + [mixing, north, south]):
@@ -299,13 +311,14 @@
         give[...] = jnp.zeros_like(give)
 
 
-def forcing_kernel(number, tracers, levels, rows, columns, near, far, out, left, right, terms, flat, parts):
-    sources, groups, _, held = near.shape
+def forcing_kernel(number, tracers, levels, rows, columns, *refs):
+    got, (out, left, right, terms, flat, parts) = refs[:-6], refs[-6:]
+    sources, groups, _, held = got[0].shape
     lanes = out.shape[-1]
     subs = lax.axis_size("sub")
     tile, sub = lax.axis_index("tiles"), lax.axis_index("sub")
-    for s in range(sources * subs):
-        ref = near if s < sources else far
+    for s in range(sources * len(got)):
+        ref = got[s // sources]
         for group in range(groups):
             flat[4 * group : 4 * group + 4, s * held : (s + 1) * held] = ref[s % sources, group]
     owner = flat[tracers : tracers + 1, :]
@@ -403,56 +416,58 @@
     def room(*arrays):
         return [pltpu.VMEM(x.shape, x.dtype) for x in arrays]
 
-    beside = [lax.ppermute(averaging_kernel, "levels", pairs) for pairs, _, _ in moves()]
+    across = [(pairs, [(a * subs + c, b * subs + d) for a, b in pairs for c, d in sub_pairs]) for pairs, _, _ in moves()]
+    beside = [lax.ppermute(averaging_kernel, "levels", pairs) for pairs, _ in across]
+    crossed = [lax.ppermute(averaging_kernel, ("levels", "sub"), pairs) for _, pairs in across]
     fields = (final_adjoint, lon_courant, lat_courant, upwind_flags, vertical_mixing)
-    own, edge = call(
-        edges_kernel,
+    fields += (misfit, averaging_kernel, sounding_owner.reshape(1, held), sounding_target)
+    level_part, edge_part = shape(planes, STEPS, rows, lanes), shape(planes, STEPS, rows, LANES)
+    groups = -(-(tracers + 2 + wide) // 4)
+    flat_rows = -(-groups // 2) * 8
+    own, edge, payload, *parts = call(
+        functools.partial(edges_kernel, moves),
         60,
-        out_shape=(shape(planes, levels, rows, lanes), shape(planes, levels, rows, LANES)),
-        in_specs=[HBM] * 5,
-        out_specs=(VMEM, VMEM),
+        out_shape=[shape(planes, levels, rows, lanes), shape(planes, levels, rows, LANES)]
+        + [shape(flat_rows, held)]
+        + [level_part, edge_part] * number,
+        in_specs=[HBM] * 9,
+        out_specs=[VMEM] * (3 + 2 * number),
         scratch_shapes=room(*fields)
-        + [pltpu.VMEM((planes, levels, 8, lanes), F32), pltpu.SemaphoreType.DMA((5,))],
+        + [pltpu.VMEM((planes, levels, 8, lanes), F32), pltpu.SemaphoreType.DMA((9,))],
         name="edges",
     )(*fields)
     edge = lax.ppermute(edge, "sub", sub_pairs)
-    inputs = (misfit, averaging_kernel, sounding_owner.reshape(1, held), sounding_target, *beside)
-    groups = -(-(tracers + 2 + wide) // 4)
-    payload = call(
-        functools.partial(payload_kernel, number),
-        16 if held <= 1024 else 32,
-        out_shape=shape(tiles, groups, 4, held),
-        in_specs=[HBM] * 4 + [VMEM] * number,
+    for i, (pairs, cross) in enumerate(across):
+        parts[2 * i] = lax.ppermute(parts[2 * i], "levels", pairs)
+        parts[2 * i + 1] = lax.ppermute(parts[2 * i + 1], ("levels", "sub"), cross)
+    both = call(
+        functools.partial(payload_kernel, number, levels, tracers),
+        8,
+        out_shape=shape(2, groups, 4, held),
+        in_specs=[VMEM] * (2 + 2 * number),
         out_specs=VMEM,
-        scratch_shapes=room(*inputs[:4])
-        + [pltpu.VMEM((-(-groups // 2) * 8, held), F32), pltpu.SemaphoreType.DMA((4,))],
+        scratch_shapes=[pltpu.VMEM((flat_rows, held), F32)],
         name="payload",
-    )(*inputs)
-    near = lax.all_to_all(payload, "tiles", split_axis=0, concat_axis=0, tiled=True)
-    far = lax.ppermute(near, "sub", sub_pairs)
-
-    sent = call(
-        functools.partial(levels_kernel, moves, columns),
-        8,
-        out_shape=[shape(planes, STEPS, rows, lanes)] * number,
-        in_specs=[VMEM] * 2,
-        out_specs=[VMEM] * number,
-        name="levels",
-    )(own, edge)
-    parts = [lax.ppermute(part, "levels", pairs) for part, (pairs, _, _) in zip(sent, moves())]
+    )(payload, *beside, lax.ppermute(payload, "sub", sub_pairs), *crossed)
+    if tiles == 4:
+        got = [both] + [lax.ppermute(both, "tiles", [(i, i ^ k) for i in range(tiles)]) for k in (1, 2, 3)]
+    else:
+        got = [lax.all_gather(both, "tiles", tiled=True)]
+
     message = shape(tracers + 4, wide, WIDTH, lanes)
     body, first, second = call(
         functools.partial(tiles_kernel, moves, columns),
         8,
         out_shape=(shape(planes, wide, rows, lanes), message, message),
-        in_specs=[VMEM] * (2 + number),
+        in_specs=[VMEM] * (2 + 2 * number),
         out_specs=[VMEM] * 3,
         name="tiles",
     )(own, edge, *parts)
     first, second = swap_tiles(first, 0), swap_tiles(second, 1)
 
-    sources = max(1, min(tiles, CHUNK // (subs * held)))
-    batch = sources * subs * held
+    held_here = got[0].shape[0]
+    sources = held_here if len(got) > 1 else max(1, min(held_here, CHUNK // held))
+    batch = sources * len(got) * held
     force_shape = (WIDTH, tracers, wide, 8, lanes)
 
     def forcing_of(round_id):
@@ -464,8 +479,8 @@
             20 if batch <= CHUNK else 60,
             flops=4 * count * tracers * 16 * batch * lanes,
             out_shape=shape(*force_shape),
-            grid=(tiles // sources,),
-            in_specs=[block, block],
+            grid=(held_here // sources,),
+            in_specs=[block] * len(got),
             out_specs=pl.BlockSpec(force_shape, lambda i: (0, 0, 0, 0, 0)),
             scratch_shapes=[
                 pltpu.VMEM((count * tracers * 16, batch), BF16),
@@ -475,7 +490,7 @@
                 pltpu.VMEM((2, tracers, depth, batch), F32),
             ],
             name="forcing" + str(round_id),
-        )(near, far)
+        )(*got)
 
     forcings = [forcing_of(i) for i in range(ROUNDS)]
     state_shape = (tracers, wide + 2, 8, lanes)

time: 59.3 us -> 67.1 us (1.13)
  waiting for transfers between devices: 3.37 us -> 16.3 us
  blocking collectives: 10.7 us -> 0 us
  starting transfers between devices: 15.1 us -> 19.7 us
  local copies, waits for them, and re-layouts: 1.04 us -> 1.78 us
    all_to_all x1 -> x0, blocking collectives: 10.7 us -> none  [per_device(): lax.all_to_all(payload, 'tiles', split_axis=0, concat_axis=0, tiled=True)]
    ppermute x1, waiting for transfers between devices: 0.01 us -> 7.71 us  [per_device(): lax.ppermute(averaging_kernel, 'levels', pairs)]
    ppermute x2 -> x7, starting transfers between devices: 1.57 us -> 8.3 us  [the longest x3 4.78 us: per_device(): lax.ppermute(both, 'tiles', [(i, i ^ k) for i in range(tiles)])]
    ppermute x2 -> x7, waiting for transfers between devices: 0.01 us -> 5.08 us  [the longest x1 3.45 us: per_device(): lax.ppermute(averaging_kernel, ('levels', 'sub'), pairs)]
    ppermute x1, starting transfers between devices: 1.32 us -> 0.15 us  [per_device(): flux_gradient = keep + lax.ppermute(give, 'levels', [(0, 1), (1, 0)])]
    ppermute x1, waiting for transfers between devices: 2.34 us -> 3.51 us  [per_device(): flux_gradient = keep + lax.ppermute(give, 'levels', [(0, 1), (1, 0)])]
    ppermute x6, waiting for transfers between devices: 1.01 us -> 0.02 us  [swap_tiles(): return lax.ppermute(value, 'tiles', pairs)]
    ppermute x1, starting transfers between devices: 2.56 us -> 1.63 us  [per_device(): lax.ppermute(averaging_kernel, 'levels', pairs)]
  transfers between devices with their start and end apart: 11 -> 16, of which waited for: 2 -> 5; matrix products, arithmetic and copies ran while one was open for 0% -> 0% of each run, Pallas kernels for 32% -> 28%
where the time goes in v3:
time: 67.1 us; the launch traced here: 66.8 us
  Pallas kernels  27.6 us (41%)
  starting transfers between devices  19.7 us (29%)
  waiting for transfers between devices  16.3 us (24%)
  local copies, waits for them, and re-layouts  1.78 us (3%)
  between operations  0.78 us (1%)
    pallas_call x3, Pallas kernels, forcing_of(): call(functools.partial(forcing_kernel, round_id, tracers, levels, rows, c...  18.7 us
    ppermute x6, starting transfers between devices, swap_tiles(): return lax.ppermute(value, 'tiles', pairs)  9.62 us
    ppermute x1, waiting for transfers between devices, per_device(): lax.ppermute(averaging_kernel, 'levels', pairs)  7.71 us
    ppermute x3, starting transfers between devices, per_device(): lax.ppermute(both, 'tiles', [(i, i ^ k) for i in range(tiles)])  4.78 us
    pallas_call x2, Pallas kernels, per_device(): call(functools.partial(next_kernel, round_id, levels, rows), 12, out_shap...  3.75 us
    ppermute x1, waiting for transfers between devices, per_device(): flux_gradient = keep + lax.ppermute(give, 'levels', [(0, 1), (1, 0)])  3.51 us
    ppermute x1, waiting for transfers between devices, per_device(): lax.ppermute(averaging_kernel, ('levels', 'sub'), pairs)  3.45 us
    ppermute x1, starting transfers between devices, per_device(): parts[2 * i] = lax.ppermute(parts[2 * i], 'levels', pairs)  3 us
  transfers between devices with their start and end apart: 16, of which 5 were waited for; matrix products, arithmetic and copies ran while one was open for 0% of the time, Pallas kernels for 28%

profile of v3, /device:TPU:0, one launch (start us, length us, event | category | flops | bytes accessed | tf_op | source)
XLA Modules:
  0.0 66.8 jit_solution(13598858808977357438)
XLA Ops:
  0.6 2.4 %edges.1 = (f32[8,9,4,384]{3,2,1,0:T(4,128)}, f32[8,9,4,128]{3,2,1,0:T(4,128)}, f32[24,384]{1,0:T(8,128)}, f32[8,6,4,384]{3,2,1,0:T(4,128)}, f32[8,6,4,128]{3,2,1,0:T(4,128)}) custom-call(f32[3,9,4,360]{3,2,1,0:T(4,128)} %refs_0_.1, f32[9,4,360]{2,1,0:T(4,128)} %refs_1_.1, f32[9,4,360]{2,1,0:T(4,128)} %refs_2_.1, s32[2,9,4,360]{3,2,1,0:T(4,128)} %refs_3_.1, ...), custom_call_target="tpu_custom_call" | custom-call | bytes 1048576 | tf_op jit(solution)/shard_map/edges/pallas_call | solution.py:427
  3.0 3.0 %collective-permute-start.1 = (f32[8,6,4,384]{3,2,1,0:T(4,128)}, f32[8,6,4,384]{3,2,1,0:T(4,128)S(1)}, u32[]{:S(2)}, u32[]{:S(2)}) collective-permute-start(f32[8,6,4,384]{3,2,1,0:T(4,128)} %get-tuple-element.24), channel_id=1, source_target_pairs={{0,2},{2,0},{1,3},{3,1},{4,6},{6,4},{5,7},{7,5},{8,10},{10,8},{9,1... | collective-permute-start | bytes 884744 | tf_op jit(solution)/shard_map/ppermute | solution.py:441
  6.5 1.6 %collective-permute-start.5 = (f32[9,384]{1,0:T(8,128)}, f32[9,384]{1,0:T(8,128)S(1)}, u32[]{:S(2)}, u32[]{:S(2)}) collective-permute-start(f32[9,384]{1,0:T(8,128)} %refs_6_.1), channel_id=1, source_target_pairs={{0,2},{2,0},{1,3},{3,1},{4,6},{6,4},{5,7},{7,5},{8,10},{10,8},{9,1... | collective-permute-start | bytes 41480 | tf_op jit(solution)/shard_map/ppermute | solution.py:420
  8.2 7.7 %collective-permute-done.5.refs_1_ = f32[9,384]{1,0:T(8,128)S(1)} collective-permute-done((f32[9,384]{1,0:T(8,128)}, f32[9,384]{1,0:T(8,128)S(1)}, u32[]{:S(2)}, u32[]{:S(2)}) %collective-permute-start.5) | collective-permute-done | bytes 13856 | tf_op jit(solution)/shard_map/ppermute | solution.py:420
  15.9 3.4 %collective-permute-done.7.refs_3_ = f32[9,384]{1,0:T(8,128)S(1)} collective-permute-done((f32[9,384]{1,0:T(8,128)}, f32[9,384]{1,0:T(8,128)S(1)}, u32[]{:S(2)}, u32[]{:S(2)}) %collective-permute-start.7) | collective-permute-done | bytes 13856 | tf_op jit(solution)/shard_map/ppermute | solution.py:421
  19.3 0.8 %copy-done.1 = f32[24,384]{1,0:T(8,128)S(1)} copy-done((f32[24,384]{1,0:T(8,128)S(1)}, f32[24,384]{1,0:T(8,128)}, u32[]{:S(2)}) %copy-start.1) | copy-done | bytes 36888
  20.1 4.1 %collective-permute-start.10 = (f32[2,5,4,384]{3,2,1,0:T(4,128)S(1)}, f32[2,5,4,384]{3,2,1,0:T(4,128)S(1)}, u32[]{:S(2)}, u32[]{:S(2)}) collective-permute-start(f32[2,5,4,384]{3,2,1,0:T(4,128)S(1)} %payload.1.refs_0_), channel_id=1, source_target_pairs={{0,12},{4,8},{8,4},{12,0},{1,13},{5,9},{9,5},{13,1},{2,14},{6,10},... | collective-permute-start | bytes 184328 | tf_op jit(solution)/shard_map/ppermute | solution.py:453
  24.3 0.6 collective-permute-start.9
  24.9 1.0 %copy-done = f32[8,9,4,384]{3,2,1,0:T(4,128)S(1)} copy-done((f32[8,9,4,384]{3,2,1,0:T(4,128)S(1)}, f32[8,9,4,384]{3,2,1,0:T(4,128)}, u32[]{:S(2)}) %copy-start) | copy-done | bytes 442392
  26.3 1.5 %collective-permute-start.3 = (f32[7,15,2,384]{3,2,1,0:T(2,128)S(1)}, f32[7,15,2,384]{3,2,1,0:T(2,128)S(1)}, u32[]{:S(2)}, u32[]{:S(2)}) collective-permute-start(f32[7,15,2,384]{3,2,1,0:T(2,128)S(1)} %get-tuple-element.27), channel_id=1, source_target_pairs={{0,4},{4,0},{8,12},{12,8},{1,5},{5,1},{9,13},{13,9},{2,6},{6,2},{1... | collective-permute-start | bytes 967688 | tf_op jit(solution)/shard_map/ppermute | solution.py:49
  27.7 0.8 %collective-permute-start.4 = (f32[7,15,2,384]{3,2,1,0:T(2,128)S(1)}, f32[7,15,2,384]{3,2,1,0:T(2,128)S(1)}, u32[]{:S(2)}, u32[]{:S(2)}) collective-permute-start(f32[7,15,2,384]{3,2,1,0:T(2,128)S(1)} %get-tuple-element.28), channel_id=1, source_target_pairs={{4,8},{8,4},{5,9},{9,5},{6,10},{10,6},{7,11},{11,7},{20,24},{24,20... | collective-permute-start | bytes 967688 | tf_op jit(solution)/shard_map/ppermute | solution.py:49
  28.5 1.0 %collective-permute-done.8.refs_1_ = f32[2,5,4,384]{3,2,1,0:T(4,128)S(1)} collective-permute-done((f32[2,5,4,384]{3,2,1,0:T(4,128)S(1)}, f32[2,5,4,384]{3,2,1,0:T(4,128)S(1)}, u32[]{:S(2)}, u32[]{:S(2)}) %collective-permute-start.8) | collective-permute-done | bytes 61472 | tf_op jit(solution)/shard_map/ppermute | solution.py:453
  29.5 0.6 collective-permute-done.9.refs_2_
  30.2 7.0 %forcing0.1.forcing = f32[2,3,15,8,384]{4,3,2,1,0:T(8,128)S(1)} custom-call(f32[2,5,4,384]{3,2,1,0:T(4,128)S(1)} %payload.1.refs_0_, f32[2,5,4,384]{3,2,1,0:T(4,128)S(1)} %collective-permute-done.8.refs_1_, f32[2,5,4,384]{3,2,1,0:T(4,128)S(1)} %collective-permute-done.9.refs_2_, f32[2,5,4,384]{3,2,1,0:T(4,128)S(1)} %collective-permute-done.10.refs_3_), custom_call_target="tpu_custom_call" | custom-call | flops 3170893824 | bytes 1048576 | tf_op jit(solution)/shard_map/forcing0/pallas_call | solution.py:477
  37.2 2.5 %round0.1 = (f32[3,17,8,384]{3,2,1,0:T(8,128)S(1)}, f32[5,17,8,384]{3,2,1,0:T(8,128)S(1)}, f32[3,8,384]{2,1,0:T(8,128)S(1)}, f32[3,13,2,384]{3,2,1,0:T(2,128)S(1)}, f32[3,13,2,384]{3,2,1,0:T(2,128)S(1)}) custom-call(f32[8,15,4,384]{3,2,1,0:T(4,128)S(1)} %get-tuple-element.26.body, f32[7,15,2,384]{3,2,1,0:T(2,128)S(1)} %collective-permute-done.3.first, ...), custom_call_target="tpu_custom_call" | custom-call | bytes 1048576 | tf_op jit(solution)/shard_map/round0/pallas_call | solution.py:505
  39.7 3.2 %collective-permute-start.11 = (f32[3,13,2,384]{3,2,1,0:T(2,128)S(1)}, f32[3,13,2,384]{3,2,1,0:T(2,128)S(1)}, u32[]{:S(2)}, u32[]{:S(2)}) collective-permute-start(f32[3,13,2,384]{3,2,1,0:T(2,128)S(1)} %get-tuple-element.32), channel_id=1, source_target_pairs={{0,4},{4,0},{8,12},{12,8},{1,5},{5,1},{9,13},{13,9},{2,6},{6,2},{1... | collective-permute-start | bytes 359432 | tf_op jit(solution)/shard_map/ppermute | solution.py:49
  42.9 0.8 %collective-permute-start.12 = (f32[3,13,2,384]{3,2,1,0:T(2,128)S(1)}, f32[3,13,2,384]{3,2,1,0:T(2,128)S(1)}, u32[]{:S(2)}, u32[]{:S(2)}) collective-permute-start(f32[3,13,2,384]{3,2,1,0:T(2,128)S(1)} %get-tuple-element.33), channel_id=1, source_target_pairs={{4,8},{8,4},{5,9},{9,5},{6,10},{10,6},{7,11},{11,7},{20,24},{24,20... | collective-permute-start | bytes 359432 | tf_op jit(solution)/shard_map/ppermute | solution.py:49
  43.7 6.2 %forcing1.1.forcing = f32[2,3,15,8,384]{4,3,2,1,0:T(8,128)S(1)} custom-call(f32[2,5,4,384]{3,2,1,0:T(4,128)S(1)} %payload.1.refs_0_, f32[2,5,4,384]{3,2,1,0:T(4,128)S(1)} %collective-permute-done.8.refs_1_, f32[2,5,4,384]{3,2,1,0:T(4,128)S(1)} %collective-permute-done.9.refs_2_, f32[2,5,4,384]{3,2,1,0:T(4,128)S(1)} %collective-permute-done.10.refs_3_), custom_call_target="tpu_custom_call" | custom-call | flops 2717908992 | bytes 1048576 | tf_op jit(solution)/shard_map/forcing1/pallas_call | solution.py:477
  50.0 1.7 %round1.1 = (f32[3,17,8,384]{3,2,1,0:T(8,128)S(1)}, f32[3,8,384]{2,1,0:T(8,128)S(1)}, f32[3,11,2,384]{3,2,1,0:T(2,128)S(1)}, f32[3,11,2,384]{3,2,1,0:T(2,128)S(1)}) custom-call(f32[3,17,8,384]{3,2,1,0:T(8,128)S(1)} %get-tuple-element.30.state, f32[5,17,8,384]{3,2,1,0:T(8,128)S(1)} %get-tuple-element.31.coef, ...), custom_call_target="tpu_custom_call" | custom-call | bytes 1048576 | tf_op jit(solution)/shard_map/round1/pallas_call | solution.py:524
  51.7 2.7 %collective-permute-start.13 = (f32[3,11,2,384]{3,2,1,0:T(2,128)S(1)}, f32[3,11,2,384]{3,2,1,0:T(2,128)S(1)}, u32[]{:S(2)}, u32[]{:S(2)}) collective-permute-start(f32[3,11,2,384]{3,2,1,0:T(2,128)S(1)} %get-tuple-element.36), channel_id=1, source_target_pairs={{0,4},{4,0},{8,12},{12,8},{1,5},{5,1},{9,13},{13,9},{2,6},{6,2},{1... | collective-permute-start | bytes 304136 | tf_op jit(solution)/shard_map/ppermute | solution.py:49
  54.4 0.7 collective-permute-start.14
  55.0 5.4 %forcing2.1.forcing = f32[2,3,15,8,384]{4,3,2,1,0:T(8,128)S(1)} custom-call(f32[2,5,4,384]{3,2,1,0:T(4,128)S(1)} %payload.1.refs_0_, f32[2,5,4,384]{3,2,1,0:T(4,128)S(1)} %collective-permute-done.8.refs_1_, f32[2,5,4,384]{3,2,1,0:T(4,128)S(1)} %collective-permute-done.9.refs_2_, f32[2,5,4,384]{3,2,1,0:T(4,128)S(1)} %collective-permute-done.10.refs_3_), custom_call_target="tpu_custom_call" | custom-call | flops 2264924160 | bytes 1048576 | tf_op jit(solution)/shard_map/forcing2/pallas_call | solution.py:477
  60.5 2.0 %round2.1 = (f32[3,9,4,360]{3,2,1,0:T(4,128)}, f32[3,2,360]{2,1,0:T(2,128)S(1)}, f32[3,2,360]{2,1,0:T(2,128)S(1)}) custom-call(f32[3,17,8,384]{3,2,1,0:T(8,128)S(1)} %get-tuple-element.35.state, f32[5,17,8,384]{3,2,1,0:T(8,128)S(1)} %get-tuple-element.31.coef, f32[3,11,2,384]{3,2,1,0:T(2,128)S(1)} %collective-permute-done.13.first, ...), custom_call_target="tpu_custom_call" | custom-call | bytes 1048576 | tf_op jit(solution)/shard_map/round2/pallas_call | solution.py:524
  62.7 3.5 %collective-permute-done.15 = f32[3,2,360]{2,1,0:T(2,128)S(1)} collective-permute-done((f32[3,2,360]{2,1,0:T(2,128)S(1)}, f32[3,2,360]{2,1,0:T(2,128)S(1)}, u32[]{:S(2)}, u32[]{:S(2)}) %collective-permute-start.15) | collective-permute-done | bytes 8672 | tf_op jit(solution)/shard_map/ppermute | solution.py:537
  (24 shorter events, 1.7 us)
Async XLA Ops:
  3.0 21.9 %collective-permute-start.1 = (f32[8,6,4,384]{3,2,1,0:T(4,128)}, f32[8,6,4,384]{3,2,1,0:T(4,128)S(1)}, u32[]{:S(2)}, u32[]{:S(2)}) collective-permute-start(f32[8,6,4,384]{3,2,1,0:T(4,128)} %get-tuple-element.24), channel_id=1, source_target_pairs={{0,2},{2,0},{1,3},{3,1},{4,6},{6,4},{5,7},{7,5},{8,10},{10,8},{9,1... | collective-permute-start | bytes 884744 | tf_op jit(solution)/shard_map/ppermute | solution.py:441
  6.0 18.9 %collective-permute-start = (f32[8,9,4,128]{3,2,1,0:T(4,128)}, f32[8,9,4,128]{3,2,1,0:T(4,128)S(1)}, u32[]{:S(2)}, u32[]{:S(2)}) collective-permute-start(f32[8,9,4,128]{3,2,1,0:T(4,128)} %get-tuple-element.23), channel_id=1, source_target_pairs={{0,1},{1,0},{2,3},{3,2},{4,5},{5,4},{6,7},{7,6},{8,9},{9,8},{10,11... | collective-permute-start | bytes 442376 | tf_op jit(solution)/shard_map/ppermute | solution.py:439
  6.0 18.3 %collective-permute-start.2 = (f32[8,6,4,128]{3,2,1,0:T(4,128)}, f32[8,6,4,128]{3,2,1,0:T(4,128)S(1)}, u32[]{:S(2)}, u32[]{:S(2)}) collective-permute-start(f32[8,6,4,128]{3,2,1,0:T(4,128)} %get-tuple-element.25), channel_id=1, source_target_pairs={{0,3},{1,2},{2,1},{3,0},{4,7},{5,6},{6,5},{7,4},{8,11},{9,10},{10,... | collective-permute-start | bytes 294920 | tf_op jit(solution)/shard_map/ppermute | solution.py:442
  6.2 13.1 %collective-permute-start.6 = (f32[24,384]{1,0:T(8,128)}, f32[24,384]{1,0:T(8,128)S(1)}, u32[]{:S(2)}, u32[]{:S(2)}) collective-permute-start(f32[24,384]{1,0:T(8,128)} %get-tuple-element.29.refs_0_), channel_id=1, source_target_pairs={{0,1},{1,0},{2,3},{3,2},{4,5},{5,4},{6,7},{7,6},{8,9},{9,8},{10,11... | collective-permute-start | bytes 110600 | tf_op jit(solution)/shard_map/ppermute | solution.py:451
  6.5 9.3 %collective-permute-start.5 = (f32[9,384]{1,0:T(8,128)}, f32[9,384]{1,0:T(8,128)S(1)}, u32[]{:S(2)}, u32[]{:S(2)}) collective-permute-start(f32[9,384]{1,0:T(8,128)} %refs_6_.1), channel_id=1, source_target_pairs={{0,2},{2,0},{1,3},{3,1},{4,6},{6,4},{5,7},{7,5},{8,10},{10,8},{9,1... | collective-permute-start | bytes 41480 | tf_op jit(solution)/shard_map/ppermute | solution.py:420
  15.9 3.5 %collective-permute-start.7 = (f32[9,384]{1,0:T(8,128)}, f32[9,384]{1,0:T(8,128)S(1)}, u32[]{:S(2)}, u32[]{:S(2)}) collective-permute-start(f32[9,384]{1,0:T(8,128)} %refs_6_.1), channel_id=1, source_target_pairs={{0,3},{1,2},{2,1},{3,0},{4,7},{5,6},{6,5},{7,4},{8,11},{9,10},{10,... | collective-permute-start | bytes 41480 | tf_op jit(solution)/shard_map/ppermute | solution.py:421
  19.3 0.8 %copy-start.1 = (f32[24,384]{1,0:T(8,128)S(1)}, f32[24,384]{1,0:T(8,128)}, u32[]{:S(2)}) copy-start(f32[24,384]{1,0:T(8,128)} %get-tuple-element.29.refs_0_) | copy-start | bytes 110596
  20.1 8.4 %collective-permute-start.10 = (f32[2,5,4,384]{3,2,1,0:T(4,128)S(1)}, f32[2,5,4,384]{3,2,1,0:T(4,128)S(1)}, u32[]{:S(2)}, u32[]{:S(2)}) collective-permute-start(f32[2,5,4,384]{3,2,1,0:T(4,128)S(1)} %payload.1.refs_0_), channel_id=1, source_target_pairs={{0,12},{4,8},{8,4},{12,0},{1,13},{5,9},{9,5},{13,1},{2,14},{6,10},... | collective-permute-start | bytes 184328 | tf_op jit(solution)/shard_map/ppermute | solution.py:453
  24.3 5.2 %collective-permute-start.8 = (f32[2,5,4,384]{3,2,1,0:T(4,128)S(1)}, f32[2,5,4,384]{3,2,1,0:T(4,128)S(1)}, u32[]{:S(2)}, u32[]{:S(2)}) collective-permute-start(f32[2,5,4,384]{3,2,1,0:T(4,128)S(1)} %payload.1.refs_0_), channel_id=1, source_target_pairs={{0,4},{4,0},{8,12},{12,8},{1,5},{5,1},{9,13},{13,9},{2,6},{6,2},{1... | collective-permute-start | bytes 184328 | tf_op jit(solution)/shard_map/ppermute | solution.py:453
  24.3 5.9 %collective-permute-start.9 = (f32[2,5,4,384]{3,2,1,0:T(4,128)S(1)}, f32[2,5,4,384]{3,2,1,0:T(4,128)S(1)}, u32[]{:S(2)}, u32[]{:S(2)}) collective-permute-start(f32[2,5,4,384]{3,2,1,0:T(4,128)S(1)} %payload.1.refs_0_), channel_id=1, source_target_pairs={{0,8},{4,12},{8,0},{12,4},{1,9},{5,13},{9,1},{13,5},{2,10},{6,14},... | collective-permute-start | bytes 184328 | tf_op jit(solution)/shard_map/ppermute | solution.py:453
  24.9 1.0 %copy-start = (f32[8,9,4,384]{3,2,1,0:T(4,128)S(1)}, f32[8,9,4,384]{3,2,1,0:T(4,128)}, u32[]{:S(2)}) copy-start(f32[8,9,4,384]{3,2,1,0:T(4,128)} %get-tuple-element.22.own) | copy-start | bytes 1327108
  26.3 10.9 %collective-permute-start.3 = (f32[7,15,2,384]{3,2,1,0:T(2,128)S(1)}, f32[7,15,2,384]{3,2,1,0:T(2,128)S(1)}, u32[]{:S(2)}, u32[]{:S(2)}) collective-permute-start(f32[7,15,2,384]{3,2,1,0:T(2,128)S(1)} %get-tuple-element.27), channel_id=1, source_target_pairs={{0,4},{4,0},{8,12},{12,8},{1,5},{5,1},{9,13},{13,9},{2,6},{6,2},{1... | collective-permute-start | bytes 967688 | tf_op jit(solution)/shard_map/ppermute | solution.py:49
  27.7 9.5 %copy-start.2 = (f32[9]{0:T(128)S(1)}, f32[9]{0:T(128)}, u32[]{:S(2)}) copy-start(f32[9]{0:T(128)} %profile.5) | copy-start | bytes 112
  27.7 9.5 %collective-permute-start.4 = (f32[7,15,2,384]{3,2,1,0:T(2,128)S(1)}, f32[7,15,2,384]{3,2,1,0:T(2,128)S(1)}, u32[]{:S(2)}, u32[]{:S(2)}) collective-permute-start(f32[7,15,2,384]{3,2,1,0:T(2,128)S(1)} %get-tuple-element.28), channel_id=1, source_target_pairs={{4,8},{8,4},{5,9},{9,5},{6,10},{10,6},{7,11},{11,7},{20,24},{24,20... | collective-permute-start | bytes 967688 | tf_op jit(solution)/shard_map/ppermute | solution.py:49
  39.7 10.3 %collective-permute-start.11 = (f32[3,13,2,384]{3,2,1,0:T(2,128)S(1)}, f32[3,13,2,384]{3,2,1,0:T(2,128)S(1)}, u32[]{:S(2)}, u32[]{:S(2)}) collective-permute-start(f32[3,13,2,384]{3,2,1,0:T(2,128)S(1)} %get-tuple-element.32), channel_id=1, source_target_pairs={{0,4},{4,0},{8,12},{12,8},{1,5},{5,1},{9,13},{13,9},{2,6},{6,2},{1... | collective-permute-start | bytes 359432 | tf_op jit(solution)/shard_map/ppermute | solution.py:49
  42.9 7.1 %collective-permute-start.12 = (f32[3,13,2,384]{3,2,1,0:T(2,128)S(1)}, f32[3,13,2,384]{3,2,1,0:T(2,128)S(1)}, u32[]{:S(2)}, u32[]{:S(2)}) collective-permute-start(f32[3,13,2,384]{3,2,1,0:T(2,128)S(1)} %get-tuple-element.33), channel_id=1, source_target_pairs={{4,8},{8,4},{5,9},{9,5},{6,10},{10,6},{7,11},{11,7},{20,24},{24,20... | collective-permute-start | bytes 359432 | tf_op jit(solution)/shard_map/ppermute | solution.py:49
  51.7 8.8 %collective-permute-start.13 = (f32[3,11,2,384]{3,2,1,0:T(2,128)S(1)}, f32[3,11,2,384]{3,2,1,0:T(2,128)S(1)}, u32[]{:S(2)}, u32[]{:S(2)}) collective-permute-start(f32[3,11,2,384]{3,2,1,0:T(2,128)S(1)} %get-tuple-element.36), channel_id=1, source_target_pairs={{0,4},{4,0},{8,12},{12,8},{1,5},{5,1},{9,13},{13,9},{2,6},{6,2},{1... | collective-permute-start | bytes 304136 | tf_op jit(solution)/shard_map/ppermute | solution.py:49
  54.4 6.1 %collective-permute-start.14 = (f32[3,11,2,384]{3,2,1,0:T(2,128)S(1)}, f32[3,11,2,384]{3,2,1,0:T(2,128)S(1)}, u32[]{:S(2)}, u32[]{:S(2)}) collective-permute-start(f32[3,11,2,384]{3,2,1,0:T(2,128)S(1)} %get-tuple-element.37), channel_id=1, source_target_pairs={{4,8},{8,4},{5,9},{9,5},{6,10},{10,6},{7,11},{11,7},{20,24},{24,20... | collective-permute-start | bytes 304136 | tf_op jit(solution)/shard_map/ppermute | solution.py:49
  62.5 3.7 %collective-permute-start.15 = (f32[3,2,360]{2,1,0:T(2,128)S(1)}, f32[3,2,360]{2,1,0:T(2,128)S(1)}, u32[]{:S(2)}, u32[]{:S(2)}) collective-permute-start(f32[3,2,360]{2,1,0:T(2,128)S(1)} %get-tuple-element.41), channel_id=1, source_target_pairs={{0,2},{2,0},{1,3},{3,1},{4,6},{6,4},{5,7},{7,5},{8,10},{10,8},{9,1... | collective-permute-start | bytes 25928 | tf_op jit(solution)/shard_map/ppermute | solution.py:537

commit v4 on v3

--- a/solution.py
+++ b/solution.py
@@ -8,7 +8,8 @@
 from jax.sharding import PartitionSpec as P
 
 STEPS = 6
-WIDTH = 2
+WIDTH = 3
+FORCED = ((0, 1, 2, 3), (4, 5))
 ROUNDS = STEPS // WIDTH
 LANES = 128
 CHUNK = 3072
@@ -181,33 +182,39 @@
         for p in range(planes):
             body[p, there, :, tail : tail + LANES] = with_edges(part[p], beside[p], columns)
 
-    def rows_of(out, first, single):
-        for entry, p in enumerate(list(range(tracers)) + [mixing, north, south]):
-            out[entry] = body[p, :, first : first + WIDTH, :]
-        out[tracers + 3, :, 0:1, :] = body[east, :, single : single + 1, :]
-        out[tracers + 3, :, 1:2, :] = body[west, :, single : single + 1, :]
+    def rows_of(out, first, third):
+        near = list(range(tracers)) + [mixing, north, south, east, west]
+        for entry, p in enumerate(near):
+            out[entry] = body[p, :, first : first + 2, :]
+        for k, p in enumerate(list(range(tracers)) + [mixing, south, south]):
+            half = slice(k % 2, k % 2 + 1)
+            out[len(near) + k // 2, :, half, :] = body[p, :, third : third + 1, :]
 
     @pl.when(is_even())
     def _():
-        rows_of(first_out, rows - WIDTH, rows - 1)
-        rows_of(second_out, 0, 0)
+        rows_of(first_out, rows - 2, rows - 3)
+        rows_of(second_out, 0, 2)
 
     @pl.when(jnp.logical_not(is_even()))
     def _():
-        rows_of(first_out, 0, 0)
-        rows_of(second_out, rows - WIDTH, rows - 1)
-
-
-def advance(step, src, dst, coef, forcing, index, profile, flux, levels):
+        rows_of(first_out, 0, 2)
+        rows_of(second_out, rows - 2, rows - 3)
+
+
+def advance(step, src, dst, outer, coef, forcing, profile, flux, levels):
     tracers = src.shape[0]
     first, count = window(STEPS - 1 - step, levels)
     own, _ = window(0, levels)
     lanes = src.shape[-1]
+    ids = lax.broadcasted_iota(jnp.int32, src.shape[-2:], 0)
+    force, index = forcing(step)
     total = [flux[t] for t in range(tracers)]
     for i in range(count):
         at = first + i
         up, down = coef[0, at + 1], coef[0, at]
         east, west, north, south = (coef[c, at + 1] for c in range(1, 5))
+        if outer is not None:
+            up_outer, down_outer = coef[5, at + 1], coef[5, at]
         own_id = at - own
         inside = (own_id >= 0) & (own_id < levels)
         weight = jnp.where(inside, profile[jnp.clip(own_id, 0, levels - 1)], 0.0)
@@ -215,8 +222,14 @@
             a = src[t, at + 1]
             b = a + up * (src[t, at + 2] - a) + down * (src[t, at] - a)
             moved = b + east * (pltpu.roll(b, lanes - 1, 1) - b) + west * (pltpu.roll(b, 1, 1) - b)
-            moved = moved + north * (pltpu.roll(b, 7, 0) - b) + south * (pltpu.roll(b, 1, 0) - b)
-            new = moved + forcing[index, t, at]
+            above, below = pltpu.roll(b, 7, 0), pltpu.roll(b, 1, 0)
+            if outer is not None:
+                a = outer[t, at + 1]
+                b_outer = a + up_outer * (outer[t, at + 2] - a) + down_outer * (outer[t, at] - a)
+                above = jnp.where(ids == 5, b_outer, above)
+                below = jnp.where(ids == 6, b_outer, below)
+            moved = moved + north * (above - b) + south * (below - b)
+            new = moved + force[index, t, at]
             dst[t, at + 1] = new
             total[t] = total[t] + weight * new
     for t in range(tracers):
@@ -229,24 +242,49 @@
     ref[:, levels - 1 : levels] = jnp.zeros((ref.shape[0], 1) + ref.shape[2:], F32)
 
 
-def run_steps(number, work, other, coef, forcing, profile, flux, levels):
+def forced_in(number):
+    return [i for i, steps in enumerate(FORCED) if any(step // WIDTH == number for step in steps)]
+
+
+def run_steps(number, work, other, outer, coef, forcings, profile, flux, levels):
+    def forcing(step):
+        for i, ref in zip(forced_in(number), forcings):
+            if step in FORCED[i]:
+                return ref, FORCED[i].index(step)
+
     refs = [work, other]
     for i in range(WIDTH):
-        advance(number * WIDTH + i, refs[i % 2], refs[(i + 1) % 2], coef, forcing, i, profile, flux, levels)
+        extra = outer if i == 0 else None
+        advance(number * WIDTH + i, refs[i % 2], refs[(i + 1) % 2], extra, coef, forcing, profile, flux, levels)
     return refs[WIDTH % 2]
 
 
 def send_rows(number, state, first_out, second_out, rows, levels):
     start, count = window(STEPS - (number + 1) * WIDTH, levels)
-    upper = state[:, pl.ds(start + 1, count), rows - WIDTH : rows, :]
-    lower = state[:, pl.ds(start + 1, count), 0:WIDTH, :]
+    pick = pl.ds(start + 1, count)
+    tracers = state.shape[0]
     even = is_even()
-    first_out[...] = jnp.where(even, upper, lower)
-    second_out[...] = jnp.where(even, lower, upper)
-
-
-def first_kernel(levels, body, first, second, forcing, profile, *refs):
-    state_out, coef_out, flux, first_out, second_out, work, other, raw = refs
+    for t in range(tracers):
+        upper, lower = state[t, pick, rows - 2 : rows, :], state[t, pick, 0:2, :]
+        first_out[t] = jnp.where(even, upper, lower)
+        second_out[t] = jnp.where(even, lower, upper)
+        upper, lower = state[t, pick, rows - 3 : rows - 2, :], state[t, pick, 2:3, :]
+        entry, half = tracers + t // 2, slice(t % 2, t % 2 + 1)
+        first_out[entry, :, half, :] = jnp.where(even, upper, lower)
+        second_out[entry, :, half, :] = jnp.where(even, lower, upper)
+
+
+def place_outer(ref, plane, pick, first, second, entry, half):
+    even = is_even()
+    one, two = first[entry, :, half : half + 1, :], second[entry, :, half : half + 1, :]
+    ref[plane, pick, 5:6, :] = jnp.where(even, one, two)
+    ref[plane, pick, 6:7, :] = jnp.where(even, two, one)
+
+
+def first_kernel(levels, body, first, second, *refs):
+    count = len(forced_in(0))
+    forcings, profile = refs[:count], refs[count]
+    state_out, coef_out, flux, first_out, second_out, work, other, outer, raw = refs[count + 1 :]
     planes, wide, rows, lanes = body.shape
     tracers = planes - 5
     mixing, east, west, north, south = range(tracers, planes)
@@ -254,49 +292,61 @@
     flux[...] = jnp.zeros_like(flux)
     clear_pads(work)
     clear_pads(other)
+    clear_pads(outer)
     even = is_even()
     pick = slice(1, wide + 1)
     for p in range(planes):
         ref, plane = (work, p) if p < tracers else (raw, p - tracers)
         ref[plane, pick, 0:rows, :] = body[p]
-    for entry, p in enumerate(list(range(tracers)) + [mixing, north, south]):
+    near = list(range(tracers)) + [mixing, north, south, east, west]
+    for entry, p in enumerate(near):
         ref, plane = (work, p) if p < tracers else (raw, p - tracers)
-        ref[plane, pick, rows : rows + WIDTH, :] = jnp.where(even, first[entry], second[entry])
-        ref[plane, pick, 8 - WIDTH : 8, :] = jnp.where(even, second[entry], first[entry])
-    for k, p in enumerate((east, west)):
-        one, two = first[tracers + 3, :, k : k + 1, :], second[tracers + 3, :, k : k + 1, :]
-        raw[p - tracers, pick, rows : rows + 1, :] = jnp.where(even, one, two)
-        raw[p - tracers, pick, 7:8, :] = jnp.where(even, two, one)
+        ref[plane, pick, rows : rows + 2, :] = jnp.where(even, first[entry], second[entry])
+        ref[plane, pick, 6:8, :] = jnp.where(even, second[entry], first[entry])
+    for k in range(tracers):
+        place_outer(outer, k, pick, first, second, len(near) + k // 2, k % 2)
+    for plane, k in ((5, tracers), (6, tracers + 1)):
+        place_outer(raw, plane, pick, first, second, len(near) + k // 2, k % 2)
     coef_out[0] = raw[0]
     coef_out[1] = raw[1]
     coef_out[3] = raw[3]
+    coef_out[5] = raw[5]
+    ids = lax.broadcasted_iota(jnp.int32, (8, lanes), 0)
     for l in range(raw.shape[1]):
         coef_out[2, l] = pltpu.roll(raw[2, l], 1, 1)
-        coef_out[4, l] = pltpu.roll(raw[4, l], 1, 0)
-    last = run_steps(0, work, other, coef_out, forcing, profile, flux, levels)
+        coef_out[4, l] = jnp.where(ids == 6, raw[6, l], pltpu.roll(raw[4, l], 1, 0))
+    last = run_steps(0, work, other, outer, coef_out, forcings, profile, flux, levels)
     state_out[...] = last[...]
     send_rows(0, state_out, first_out, second_out, rows, levels)
 
 
-def next_kernel(number, levels, rows, state, coef, first, second, forcing, profile, flux_in, *refs):
-    work, other = refs[-2:]
-    start, count = window(STEPS - number * WIDTH, levels)
-    pick = pl.ds(start + 1, count)
+def next_kernel(number, levels, rows, state, coef, first, second, *refs):
+    count = len(forced_in(number))
+    forcings, profile, flux_in = refs[:count], refs[count], refs[count + 1]
+    refs = refs[count + 2 :]
+    work, other, outer = refs[-3:]
+    start, size = window(STEPS - number * WIDTH, levels)
+    pick = pl.ds(start + 1, size)
     even = is_even()
+    tracers = state.shape[0]
     work[...] = state[...]
-    work[:, pick, rows : rows + WIDTH, :] = jnp.where(even, first[...], second[...])
-    work[:, pick, 8 - WIDTH : 8, :] = jnp.where(even, second[...], first[...])
+    for t in range(tracers):
+        work[t, pick, rows : rows + 2, :] = jnp.where(even, first[t], second[t])
+        work[t, pick, 6:8, :] = jnp.where(even, second[t], first[t])
     clear_pads(other)
+    clear_pads(outer)
+    for t in range(tracers):
+        place_outer(outer, t, pick, first, second, tracers + t // 2, t % 2)
     if number < ROUNDS - 1:
-        state_out, flux, first_out, second_out = refs[:-2]
+        state_out, flux, first_out, second_out = refs[:-3]
         flux[...] = flux_in[...]
-        last = run_steps(number, work, other, coef, forcing, profile, flux, levels)
+        last = run_steps(number, work, other, outer, coef, forcings, profile, flux, levels)
         state_out[...] = last[...]
         send_rows(number, state_out, first_out, second_out, rows, levels)
         return
-    adjoint, keep, give, flux = refs[:-2]
+    adjoint, keep, give, flux = refs[:-3]
     flux[...] = flux_in[...]
-    last = run_steps(number, work, other, coef, forcing, profile, flux, levels)
+    last = run_steps(number, work, other, outer, coef, forcings, profile, flux, levels)
     own, _ = window(0, levels)
     columns = adjoint.shape[-1]
     adjoint[...] = last[:, pl.ds(own + 1, levels), 0:rows, 0:columns]
@@ -311,7 +361,7 @@
         give[...] = jnp.zeros_like(give)
 
 
-def forcing_kernel(number, tracers, levels, rows, columns, *refs):
+def forcing_kernel(steps, tracers, levels, rows, columns, *refs):
     got, (out, left, right, terms, flat, parts) = refs[:-6], refs[-6:]
     sources, groups, _, held = got[0].shape
     lanes = out.shape[-1]
@@ -345,7 +395,7 @@
         high = value.astype(BF16).astype(F32)
         parts[0, t] = high
         parts[1, t] = value - high
-    first, count = window(STEPS - 1 - WIDTH * number, levels)
+    first, count = window(STEPS - 1 - steps[0], levels)
     batch = flat.shape[1]
     for i in range(count):
         for t in range(tracers):
@@ -353,8 +403,7 @@
             both = [jnp.broadcast_to(parts[k, t, row_id, :], (8, batch)) for k in range(2)]
             terms[i * tracers + t] = jnp.concatenate(both, axis=0).astype(BF16)
     ids = lax.broadcasted_iota(jnp.int32, (8, batch), 0).astype(F32)
-    for i in range(WIDTH):
-        now = number * WIDTH + i
+    for i, now in enumerate(steps):
         begin, size = window(STEPS - 1 - now, levels)
         hit = jnp.where(key == ids + now * 8.0, 1.0, 0.0)
         mask = jnp.concatenate([hit, hit], axis=0).astype(BF16)
@@ -437,6 +486,8 @@
         name="edges",
     )(*fields)
     edge = lax.ppermute(edge, "sub", sub_pairs)
+    swapped = lax.ppermute(payload, "sub", sub_pairs)
+    parts, beside, crossed, swapped = lax.optimization_barrier((parts, beside, crossed, swapped))
     for i, (pairs, cross) in enumerate(across):
         parts[2 * i] = lax.ppermute(parts[2 * i], "levels", pairs)
         parts[2 * i + 1] = lax.ppermute(parts[2 * i + 1], ("levels", "sub"), cross)
@@ -448,13 +499,13 @@
         out_specs=VMEM,
         scratch_shapes=[pltpu.VMEM((flat_rows, held), F32)],
         name="payload",
-    )(payload, *beside, lax.ppermute(payload, "sub", sub_pairs), *crossed)
+    )(payload, *beside, swapped, *crossed)
     if tiles == 4:
         got = [both] + [lax.ppermute(both, "tiles", [(i, i ^ k) for i in range(tiles)]) for k in (1, 2, 3)]
     else:
         got = [lax.all_gather(both, "tiles", tiled=True)]
 
-    message = shape(tracers + 4, wide, WIDTH, lanes)
+    message = shape(tracers + 5 + (tracers + 3) // 2, wide, 2, lanes)
     body, first, second = call(
         functools.partial(tiles_kernel, moves, columns),
         8,
@@ -468,16 +519,14 @@
     held_here = got[0].shape[0]
     sources = held_here if len(got) > 1 else max(1, min(held_here, CHUNK // held))
     batch = sources * len(got) * held
-    force_shape = (WIDTH, tracers, wide, 8, lanes)
-
-    def forcing_of(round_id):
-        count = window(STEPS - 1 - WIDTH * round_id, levels)[1]
-        depth = -(-groups // 2) * 8
+    def forcing_of(steps):
+        count = window(STEPS - 1 - steps[0], levels)[1]
+        force_shape = (len(steps), tracers, wide, 8, lanes)
         block = pl.BlockSpec((sources, groups, 4, held), lambda i: (i, 0, 0, 0))
         return call(
-            functools.partial(forcing_kernel, round_id, tracers, levels, rows, columns),
+            functools.partial(forcing_kernel, steps, tracers, levels, rows, columns),
             20 if batch <= CHUNK else 60,
-            flops=4 * count * tracers * 16 * batch * lanes,
+            flops=2 * len(steps) * count * tracers * 16 * batch * lanes,
             out_shape=shape(*force_shape),
             grid=(held_here // sources,),
             in_specs=[block] * len(got),
@@ -486,31 +535,31 @@
                 pltpu.VMEM((count * tracers * 16, batch), BF16),
                 pltpu.VMEM((lanes, batch), BF16),
                 pltpu.VMEM((count * tracers, 16, batch), BF16),
-                pltpu.VMEM((depth, batch), F32),
-                pltpu.VMEM((2, tracers, depth, batch), F32),
+                pltpu.VMEM((flat_rows, batch), F32),
+                pltpu.VMEM((2, tracers, flat_rows, batch), F32),
             ],
-            name="forcing" + str(round_id),
+            name="forcing" + str(steps[0]),
         )(*got)
 
-    forcings = [forcing_of(i) for i in range(ROUNDS)]
+    forcings = [forcing_of(steps) for steps in FORCED]
     state_shape = (tracers, wide + 2, 8, lanes)
-    coef_shape = (5, wide + 2, 8, lanes)
+    coef_shape = (6, wide + 2, 8, lanes)
     flux_shape = (tracers, 8, lanes)
 
     def messages(round_id):
         count = window(STEPS - round_id * WIDTH, levels)[1]
-        return [shape(tracers, count, WIDTH, lanes)] * 2
-
-    scratch = [pltpu.VMEM(state_shape, F32)] * 2
+        return [shape(tracers + (tracers + 1) // 2, count, 2, lanes)] * 2
+
+    scratch = [pltpu.VMEM(state_shape, F32)] * 3
     state, coef, flux, first, second = call(
         functools.partial(first_kernel, levels),
-        12,
+        16,
         out_shape=[shape(*state_shape), shape(*coef_shape), shape(*flux_shape), *messages(1)],
-        in_specs=[VMEM] * 4 + [SMEM],
+        in_specs=[VMEM] * (3 + len(forced_in(0))) + [SMEM],
         out_specs=[VMEM] * 5,
-        scratch_shapes=scratch + [pltpu.VMEM(coef_shape, F32)],
+        scratch_shapes=scratch + [pltpu.VMEM((7, wide + 2, 8, lanes), F32)],
         name="round0",
-    )(body, first, second, forcings[0], level_profile)
+    )(body, first, second, *[forcings[i] for i in forced_in(0)], level_profile)
     half = rows // 2 if bands == 2 else rows
     for round_id in range(1, ROUNDS):
         first, second = swap_tiles(first, 0), swap_tiles(second, 1)
@@ -523,13 +572,13 @@
             extra = [pltpu.VMEM(flux_shape, F32)]
         results = call(
             functools.partial(next_kernel, round_id, levels, rows),
-            12,
+            16,
             out_shape=outs,
-            in_specs=[VMEM] * 5 + [SMEM, VMEM],
+            in_specs=[VMEM] * (4 + len(forced_in(round_id))) + [SMEM, VMEM],
             out_specs=[VMEM] * len(outs),
             scratch_shapes=extra + scratch,
             name="round" + str(round_id),
-        )(state, coef, first, second, forcings[round_id], level_profile, flux)
+        )(state, coef, first, second, *[forcings[i] for i in forced_in(round_id)], level_profile, flux)
         if round_id < ROUNDS - 1:
             state, flux, first, second = results
     adjoint, keep, give = results

time: 67.1 us -> 59.5 us (0.89)
  waiting for transfers between devices: 16.3 us -> 11.1 us
  Pallas kernels: 27.6 us -> 25.7 us
    ppermute x1, waiting for transfers between devices: 7.71 us -> 1.95 us  [per_device(): lax.ppermute(averaging_kernel, 'levels', pairs)]
    ppermute x6 -> x4, starting transfers between devices: 9.62 us -> 5.43 us  [swap_tiles(): return lax.ppermute(value, 'tiles', pairs)]
    ppermute x1, waiting for transfers between devices: 0.01 us -> 3.45 us  [per_device(): parts[2 * i + 1] = lax.ppermute(parts[2 * i + 1], ('levels', 'sub'), cross)]
    ppermute x3, starting transfers between devices: 4.78 us -> 7.83 us  [per_device(): lax.ppermute(both, 'tiles', [(i, i ^ k) for i in range(tiles)])]
    ppermute x1, starting transfers between devices: 3 us -> 0.58 us  [per_device(): parts[2 * i] = lax.ppermute(parts[2 * i], 'levels', pairs)]
    pallas_call x6 -> x4, Pallas kernels: 24.9 us -> 22.8 us  [the longest x2 17.1 us: forcing_of(): call(functools.partial(forcing_kernel, steps, tracers, levels, rows, colu...]
    ppermute x1, waiting for transfers between devices: 3.45 us -> 1.44 us  [per_device(): lax.ppermute(averaging_kernel, ('levels', 'sub'), pairs)]
    ppermute x3, waiting for transfers between devices: 1.62 us -> 0.6 us  [per_device(): lax.ppermute(both, 'tiles', [(i, i ^ k) for i in range(tiles)])]
  transfers between devices with their start and end apart: 16 -> 14, of which waited for: 5 -> 6; matrix products, arithmetic and copies ran while one was open for 0% -> 0% of each run, Pallas kernels for 28% -> 30%
where the time goes in v4:
time: 59.5 us; the launch traced here: 59.2 us
  Pallas kernels  25.7 us (43%)
  starting transfers between devices  19.4 us (33%)
  waiting for transfers between devices  11.1 us (19%)
  local copies, waits for them, and re-layouts  1.79 us (3%)
  between operations  0.75 us (1%)
  other arithmetic  0.6 us (1%)
    pallas_call x2, Pallas kernels, forcing_of(): call(functools.partial(forcing_kernel, steps, tracers, levels, rows, colu...  17.1 us
    ppermute x3, starting transfers between devices, per_device(): lax.ppermute(both, 'tiles', [(i, i ^ k) for i in range(tiles)])  7.83 us
    ppermute x4, starting transfers between devices, swap_tiles(): return lax.ppermute(value, 'tiles', pairs)  5.43 us
    ppermute x1, waiting for transfers between devices, per_device(): parts[2 * i + 1] = lax.ppermute(parts[2 * i + 1], ('levels', 'sub'), cross)  3.45 us
    pallas_call x1, Pallas kernels, per_device(): call(functools.partial(first_kernel, levels), 16, out_shape=[shape(*state...  3.14 us
    ppermute x1, waiting for transfers between devices, per_device(): flux_gradient = keep + lax.ppermute(give, 'levels', [(0, 1), (1, 0)])  2.86 us
    pallas_call x1, Pallas kernels, per_device(): call(functools.partial(next_kernel, round_id, levels, rows), 16, out_shap...  2.61 us
    ppermute x1, starting transfers between devices, per_device(): lax.ppermute(averaging_kernel, 'levels', pairs)  2.56 us
  transfers between devices with their start and end apart: 14, of which 6 were waited for; matrix products, arithmetic and copies ran while one was open for 0% of the time, Pallas kernels for 30%

profile of v4, /device:TPU:0, one launch (start us, length us, event | category | flops | bytes accessed | tf_op | source)
XLA Modules:
  0.0 59.2 jit_solution(12576331039765981875)
XLA Ops:
  0.6 2.4 %edges.1 = (f32[8,9,4,384]{3,2,1,0:T(4,128)}, f32[8,9,4,128]{3,2,1,0:T(4,128)}, f32[24,384]{1,0:T(8,128)}, f32[8,6,4,384]{3,2,1,0:T(4,128)}, f32[8,6,4,128]{3,2,1,0:T(4,128)}) custom-call(f32[3,9,4,360]{3,2,1,0:T(4,128)} %refs_0_.1, f32[9,4,360]{2,1,0:T(4,128)} %refs_1_.2, f32[9,4,360]{2,1,0:T(4,128)} %refs_2_.2, s32[2,9,4,360]{3,2,1,0:T(4,128)} %refs_3_.1, ...), custom_call_target="tpu_custom_call" | custom-call | bytes 1048576 | tf_op jit(solution)/shard_map/edges/pallas_call | solution.py:476
  3.5 2.6 %collective-permute-start.1 = (f32[9,384]{1,0:T(8,128)}, f32[9,384]{1,0:T(8,128)S(1)}, u32[]{:S(2)}, u32[]{:S(2)}) collective-permute-start(f32[9,384]{1,0:T(8,128)} %refs_6_.1), channel_id=1, source_target_pairs={{0,2},{2,0},{1,3},{3,1},{4,6},{6,4},{5,7},{7,5},{8,10},{10,8},{9,1... | collective-permute-start | bytes 41480 | tf_op jit(solution)/shard_map/ppermute | solution.py:469
  6.2 1.9 %collective-permute-done.1.refs_1_ = f32[9,384]{1,0:T(8,128)S(1)} collective-permute-done((f32[9,384]{1,0:T(8,128)}, f32[9,384]{1,0:T(8,128)S(1)}, u32[]{:S(2)}, u32[]{:S(2)}) %collective-permute-start.1) | collective-permute-done | bytes 13856 | tf_op jit(solution)/shard_map/ppermute | solution.py:469
  8.1 1.4 %collective-permute-done.2.refs_3_ = f32[9,384]{1,0:T(8,128)S(1)} collective-permute-done((f32[9,384]{1,0:T(8,128)}, f32[9,384]{1,0:T(8,128)S(1)}, u32[]{:S(2)}, u32[]{:S(2)}) %collective-permute-start.2) | collective-permute-done | bytes 13856 | tf_op jit(solution)/shard_map/ppermute | solution.py:470
  10.1 0.9 %collective-permute-start.5 = (f32[8,6,4,128]{3,2,1,0:T(4,128)}, f32[8,6,4,128]{3,2,1,0:T(4,128)S(1)}, u32[]{:S(2)}, u32[]{:S(2)}) collective-permute-start(f32[8,6,4,128]{3,2,1,0:T(4,128)} %get-tuple-element.29), channel_id=1, source_target_pairs={{0,3},{1,2},{2,1},{3,0},{4,7},{5,6},{6,5},{7,4},{8,11},{9,10},{10,... | collective-permute-start | bytes 294920 | tf_op jit(solution)/shard_map/ppermute | solution.py:493
  11.1 0.6 %collective-permute-start = (f32[8,9,4,128]{3,2,1,0:T(4,128)}, f32[8,9,4,128]{3,2,1,0:T(4,128)S(1)}, u32[]{:S(2)}, u32[]{:S(2)}) collective-permute-start(f32[8,9,4,128]{3,2,1,0:T(4,128)} %get-tuple-element.24), channel_id=1, source_target_pairs={{0,1},{1,0},{2,3},{3,2},{4,5},{5,4},{6,7},{7,6},{8,9},{9,8},{10,11... | collective-permute-start | bytes 442376 | tf_op jit(solution)/shard_map/ppermute | solution.py:488
  11.7 0.8 %copy-done.1 = f32[24,384]{1,0:T(8,128)S(1)} copy-done((f32[24,384]{1,0:T(8,128)S(1)}, f32[24,384]{1,0:T(8,128)}, u32[]{:S(2)}) %copy-start.1) | copy-done | bytes 36888
  12.5 1.6 %collective-permute-start.8 = (f32[2,5,4,384]{3,2,1,0:T(4,128)S(1)}, f32[2,5,4,384]{3,2,1,0:T(4,128)S(1)}, u32[]{:S(2)}, u32[]{:S(2)}) collective-permute-start(f32[2,5,4,384]{3,2,1,0:T(4,128)S(1)} %payload.1.refs_0_), channel_id=1, source_target_pairs={{0,4},{4,0},{8,12},{12,8},{1,5},{5,1},{9,13},{13,9},{2,6},{6,2},{1... | collective-permute-start | bytes 184328 | tf_op jit(solution)/shard_map/ppermute | solution.py:504
  14.1 2.6 %collective-permute-start.9 = (f32[2,5,4,384]{3,2,1,0:T(4,128)S(1)}, f32[2,5,4,384]{3,2,1,0:T(4,128)S(1)}, u32[]{:S(2)}, u32[]{:S(2)}) collective-permute-start(f32[2,5,4,384]{3,2,1,0:T(4,128)S(1)} %payload.1.refs_0_), channel_id=1, source_target_pairs={{0,8},{4,12},{8,0},{12,4},{1,9},{5,13},{9,1},{13,5},{2,10},{6,14},... | collective-permute-start | bytes 184328 | tf_op jit(solution)/shard_map/ppermute | solution.py:504
  16.7 3.5 %collective-permute-done.5.refs_1_ = f32[8,6,4,128]{3,2,1,0:T(4,128)S(1)} collective-permute-done((f32[8,6,4,128]{3,2,1,0:T(4,128)}, f32[8,6,4,128]{3,2,1,0:T(4,128)S(1)}, u32[]{:S(2)}, u32[]{:S(2)}) %collective-permute-start.5) | collective-permute-done | bytes 98336 | tf_op jit(solution)/shard_map/ppermute | solution.py:493
  20.2 3.6 %collective-permute-start.10 = (f32[2,5,4,384]{3,2,1,0:T(4,128)S(1)}, f32[2,5,4,384]{3,2,1,0:T(4,128)S(1)}, u32[]{:S(2)}, u32[]{:S(2)}) collective-permute-start(f32[2,5,4,384]{3,2,1,0:T(4,128)S(1)} %payload.1.refs_0_), channel_id=1, source_target_pairs={{0,12},{4,8},{8,4},{12,0},{1,13},{5,9},{9,5},{13,1},{2,14},{6,10},... | collective-permute-start | bytes 184328 | tf_op jit(solution)/shard_map/ppermute | solution.py:504
  23.8 1.0 %copy-done = f32[8,9,4,384]{3,2,1,0:T(4,128)S(1)} copy-done((f32[8,9,4,384]{3,2,1,0:T(4,128)S(1)}, f32[8,9,4,384]{3,2,1,0:T(4,128)}, u32[]{:S(2)}) %copy-start) | copy-done | bytes 442392
  25.3 0.7 %collective-permute-start.7 = (f32[11,15,2,384]{3,2,1,0:T(2,128)S(1)}, f32[11,15,2,384]{3,2,1,0:T(2,128)S(1)}, u32[]{:S(2)}, u32[]{:S(2)}) collective-permute-start(f32[11,15,2,384]{3,2,1,0:T(2,128)S(1)} %get-tuple-element.32), channel_id=1, source_target_pairs={{4,8},{8,4},{5,9},{9,5},{6,10},{10,6},{7,11},{11,7},{20,24},{24,20... | collective-permute-start | bytes 1520648 | tf_op jit(solution)/shard_map/ppermute | solution.py:50
  26.1 0.6 %collective-permute-done.10.refs_3_ = f32[2,5,4,384]{3,2,1,0:T(4,128)S(1)} collective-permute-done((f32[2,5,4,384]{3,2,1,0:T(4,128)S(1)}, f32[2,5,4,384]{3,2,1,0:T(4,128)S(1)}, u32[]{:S(2)}, u32[]{:S(2)}) %collective-permute-start.10) | collective-permute-done | bytes 61472 | tf_op jit(solution)/shard_map/ppermute | solution.py:504
  26.7 11.7 %forcing0.1.refs_0_ = f32[4,3,15,8,384]{4,3,2,1,0:T(8,128)S(1)} custom-call(f32[2,5,4,384]{3,2,1,0:T(4,128)S(1)} %payload.1.refs_0_, f32[2,5,4,384]{3,2,1,0:T(4,128)S(1)} %collective-permute-done.8.refs_1_, f32[2,5,4,384]{3,2,1,0:T(4,128)S(1)} %collective-permute-done.9.refs_2_, f32[2,5,4,384]{3,2,1,0:T(4,128)S(1)} %collective-permute-done.10.refs_3_), custom_call_target="tpu_custom_call" | custom-call | flops 6341787648 | bytes 1048576 | tf_op jit(solution)/shard_map/forcing0/pallas_call | solution.py:526
  38.3 0.8 %collective-permute-done.6.first = f32[11,15,2,384]{3,2,1,0:T(2,128)S(1)} collective-permute-done((f32[11,15,2,384]{3,2,1,0:T(2,128)S(1)}, f32[11,15,2,384]{3,2,1,0:T(2,128)S(1)}, u32[]{:S(2)}, u32[]{:S(2)}) %collective-permute-start.6) | collective-permute-done | bytes 506912 | tf_op jit(solution)/shard_map/ppermute | solution.py:50
  39.1 3.1 %round0.1 = (f32[3,17,8,384]{3,2,1,0:T(8,128)S(1)}, f32[6,17,8,384]{3,2,1,0:T(8,128)S(1)}, f32[3,8,384]{2,1,0:T(8,128)S(1)}, f32[5,12,2,384]{3,2,1,0:T(2,128)S(1)}, f32[5,12,2,384]{3,2,1,0:T(2,128)S(1)}) custom-call(f32[8,15,4,384]{3,2,1,0:T(4,128)S(1)} %get-tuple-element.30.body, f32[11,15,2,384]{3,2,1,0:T(2,128)S(1)} %collective-permute-done.6.first, ...), custom_call_target="tpu_custom_call" | custom-call | bytes 1048576 | tf_op jit(solution)/shard_map/round0/pallas_call | solution.py:554
  42.2 3.8 %collective-permute-start.11 = (f32[5,12,2,384]{3,2,1,0:T(2,128)S(1)}, f32[5,12,2,384]{3,2,1,0:T(2,128)S(1)}, u32[]{:S(2)}, u32[]{:S(2)}) collective-permute-start(f32[5,12,2,384]{3,2,1,0:T(2,128)S(1)} %get-tuple-element.38), channel_id=1, source_target_pairs={{0,4},{4,0},{8,12},{12,8},{1,5},{5,1},{9,13},{13,9},{2,6},{6,2},{1... | collective-permute-start | bytes 552968 | tf_op jit(solution)/shard_map/ppermute | solution.py:50
  46.1 0.8 %collective-permute-start.12 = (f32[5,12,2,384]{3,2,1,0:T(2,128)S(1)}, f32[5,12,2,384]{3,2,1,0:T(2,128)S(1)}, u32[]{:S(2)}, u32[]{:S(2)}) collective-permute-start(f32[5,12,2,384]{3,2,1,0:T(2,128)S(1)} %get-tuple-element.39), channel_id=1, source_target_pairs={{4,8},{8,4},{5,9},{9,5},{6,10},{10,6},{7,11},{11,7},{20,24},{24,20... | collective-permute-start | bytes 552968 | tf_op jit(solution)/shard_map/ppermute | solution.py:50
  46.9 5.4 %forcing4.1.refs_1_ = f32[2,3,15,8,384]{4,3,2,1,0:T(8,128)S(1)} custom-call(f32[2,5,4,384]{3,2,1,0:T(4,128)S(1)} %payload.1.refs_0_, f32[2,5,4,384]{3,2,1,0:T(4,128)S(1)} %collective-permute-done.8.refs_1_, f32[2,5,4,384]{3,2,1,0:T(4,128)S(1)} %collective-permute-done.9.refs_2_, f32[2,5,4,384]{3,2,1,0:T(4,128)S(1)} %collective-permute-done.10.refs_3_), custom_call_target="tpu_custom_call" | custom-call | flops 2264924160 | bytes 1048576 | tf_op jit(solution)/shard_map/forcing4/pallas_call | solution.py:526
  52.4 2.6 %round1.1 = (f32[3,9,4,360]{3,2,1,0:T(4,128)}, f32[3,2,360]{2,1,0:T(2,128)S(1)}, f32[3,2,360]{2,1,0:T(2,128)S(1)}) custom-call(f32[3,17,8,384]{3,2,1,0:T(8,128)S(1)} %get-tuple-element.36.state, f32[6,17,8,384]{3,2,1,0:T(8,128)S(1)} %get-tuple-element.37.coef, f32[5,12,2,384]{3,2,1,0:T(2,128)S(1)} %collective-permute-done.11.first, ...), custom_call_target="tpu_custom_call" | custom-call | bytes 1048576 | tf_op jit(solution)/shard_map/round1/pallas_call | solution.py:573
  55.0 0.8 %collective-permute-start.13 = (f32[3,2,360]{2,1,0:T(2,128)S(1)}, f32[3,2,360]{2,1,0:T(2,128)S(1)}, u32[]{:S(2)}, u32[]{:S(2)}) collective-permute-start(f32[3,2,360]{2,1,0:T(2,128)S(1)} %get-tuple-element.43), channel_id=1, source_target_pairs={{0,2},{2,0},{1,3},{3,1},{4,6},{6,4},{5,7},{7,5},{8,10},{10,8},{9,1... | collective-permute-start | bytes 25928 | tf_op jit(solution)/shard_map/ppermute | solution.py:586
  55.8 2.9 %collective-permute-done.13 = f32[3,2,360]{2,1,0:T(2,128)S(1)} collective-permute-done((f32[3,2,360]{2,1,0:T(2,128)S(1)}, f32[3,2,360]{2,1,0:T(2,128)S(1)}, u32[]{:S(2)}, u32[]{:S(2)}) %collective-permute-start.13) | collective-permute-done | bytes 8672 | tf_op jit(solution)/shard_map/ppermute | solution.py:586
  58.6 0.6 %add.3 = f32[3,2,360]{2,1,0:T(2,128)} add(f32[3,2,360]{2,1,0:T(2,128)S(1)} %get-tuple-element.42, f32[3,2,360]{2,1,0:T(2,128)S(1)} %collective-permute-done.13) | non-fusion elementwise | flops 2160 | bytes 25920 | tf_op jit(solution)/shard_map/add | solution.py:586
  (18 shorter events, 1.7 us)
Async XLA Ops:
  3.0 6.5 %collective-permute-start.3 = (f32[24,384]{1,0:T(8,128)}, f32[24,384]{1,0:T(8,128)S(1)}, u32[]{:S(2)}, u32[]{:S(2)}) collective-permute-start(f32[24,384]{1,0:T(8,128)} %get-tuple-element.27.refs_0_), channel_id=1, source_target_pairs={{0,1},{1,0},{2,3},{3,2},{4,5},{5,4},{6,7},{7,6},{8,9},{9,8},{10,11... | collective-permute-start | bytes 110600 | tf_op jit(solution)/shard_map/ppermute | solution.py:489
  3.5 4.6 %collective-permute-start.1 = (f32[9,384]{1,0:T(8,128)}, f32[9,384]{1,0:T(8,128)S(1)}, u32[]{:S(2)}, u32[]{:S(2)}) collective-permute-start(f32[9,384]{1,0:T(8,128)} %refs_6_.1), channel_id=1, source_target_pairs={{0,2},{2,0},{1,3},{3,1},{4,6},{6,4},{5,7},{7,5},{8,10},{10,8},{9,1... | collective-permute-start | bytes 41480 | tf_op jit(solution)/shard_map/ppermute | solution.py:469
  6.1 3.5 %collective-permute-start.2 = (f32[9,384]{1,0:T(8,128)}, f32[9,384]{1,0:T(8,128)S(1)}, u32[]{:S(2)}, u32[]{:S(2)}) collective-permute-start(f32[9,384]{1,0:T(8,128)} %refs_6_.1), channel_id=1, source_target_pairs={{0,3},{1,2},{2,1},{3,0},{4,7},{5,6},{6,5},{7,4},{8,11},{9,10},{10,... | collective-permute-start | bytes 41480 | tf_op jit(solution)/shard_map/ppermute | solution.py:470
  9.6 14.2 %collective-permute-start.4 = (f32[8,6,4,384]{3,2,1,0:T(4,128)}, f32[8,6,4,384]{3,2,1,0:T(4,128)S(1)}, u32[]{:S(2)}, u32[]{:S(2)}) collective-permute-start(f32[8,6,4,384]{3,2,1,0:T(4,128)} %get-tuple-element.28), channel_id=1, source_target_pairs={{0,2},{2,0},{1,3},{3,1},{4,6},{6,4},{5,7},{7,5},{8,10},{10,8},{9,1... | collective-permute-start | bytes 884744 | tf_op jit(solution)/shard_map/ppermute | solution.py:492
  10.1 10.0 %collective-permute-start.5 = (f32[8,6,4,128]{3,2,1,0:T(4,128)}, f32[8,6,4,128]{3,2,1,0:T(4,128)S(1)}, u32[]{:S(2)}, u32[]{:S(2)}) collective-permute-start(f32[8,6,4,128]{3,2,1,0:T(4,128)} %get-tuple-element.29), channel_id=1, source_target_pairs={{0,3},{1,2},{2,1},{3,0},{4,7},{5,6},{6,5},{7,4},{8,11},{9,10},{10,... | collective-permute-start | bytes 294920 | tf_op jit(solution)/shard_map/ppermute | solution.py:493
  11.1 12.7 %collective-permute-start = (f32[8,9,4,128]{3,2,1,0:T(4,128)}, f32[8,9,4,128]{3,2,1,0:T(4,128)S(1)}, u32[]{:S(2)}, u32[]{:S(2)}) collective-permute-start(f32[8,9,4,128]{3,2,1,0:T(4,128)} %get-tuple-element.24), channel_id=1, source_target_pairs={{0,1},{1,0},{2,3},{3,2},{4,5},{5,4},{6,7},{7,6},{8,9},{9,8},{10,11... | collective-permute-start | bytes 442376 | tf_op jit(solution)/shard_map/ppermute | solution.py:488
  11.7 0.8 %copy-start.1 = (f32[24,384]{1,0:T(8,128)S(1)}, f32[24,384]{1,0:T(8,128)}, u32[]{:S(2)}) copy-start(f32[24,384]{1,0:T(8,128)} %get-tuple-element.27.refs_0_) | copy-start | bytes 110596
  12.5 13.5 %collective-permute-start.8 = (f32[2,5,4,384]{3,2,1,0:T(4,128)S(1)}, f32[2,5,4,384]{3,2,1,0:T(4,128)S(1)}, u32[]{:S(2)}, u32[]{:S(2)}) collective-permute-start(f32[2,5,4,384]{3,2,1,0:T(4,128)S(1)} %payload.1.refs_0_), channel_id=1, source_target_pairs={{0,4},{4,0},{8,12},{12,8},{1,5},{5,1},{9,13},{13,9},{2,6},{6,2},{1... | collective-permute-start | bytes 184328 | tf_op jit(solution)/shard_map/ppermute | solution.py:504
  14.1 11.9 %collective-permute-start.9 = (f32[2,5,4,384]{3,2,1,0:T(4,128)S(1)}, f32[2,5,4,384]{3,2,1,0:T(4,128)S(1)}, u32[]{:S(2)}, u32[]{:S(2)}) collective-permute-start(f32[2,5,4,384]{3,2,1,0:T(4,128)S(1)} %payload.1.refs_0_), channel_id=1, source_target_pairs={{0,8},{4,12},{8,0},{12,4},{1,9},{5,13},{9,1},{13,5},{2,10},{6,14},... | collective-permute-start | bytes 184328 | tf_op jit(solution)/shard_map/ppermute | solution.py:504
  20.2 6.5 %collective-permute-start.10 = (f32[2,5,4,384]{3,2,1,0:T(4,128)S(1)}, f32[2,5,4,384]{3,2,1,0:T(4,128)S(1)}, u32[]{:S(2)}, u32[]{:S(2)}) collective-permute-start(f32[2,5,4,384]{3,2,1,0:T(4,128)S(1)} %payload.1.refs_0_), channel_id=1, source_target_pairs={{0,12},{4,8},{8,4},{12,0},{1,13},{5,9},{9,5},{13,1},{2,14},{6,10},... | collective-permute-start | bytes 184328 | tf_op jit(solution)/shard_map/ppermute | solution.py:504
  23.8 1.0 %copy-start = (f32[8,9,4,384]{3,2,1,0:T(4,128)S(1)}, f32[8,9,4,384]{3,2,1,0:T(4,128)}, u32[]{:S(2)}) copy-start(f32[8,9,4,384]{3,2,1,0:T(4,128)} %get-tuple-element.23.own) | copy-start | bytes 1327108
  25.2 13.8 %collective-permute-start.6 = (f32[11,15,2,384]{3,2,1,0:T(2,128)S(1)}, f32[11,15,2,384]{3,2,1,0:T(2,128)S(1)}, u32[]{:S(2)}, u32[]{:S(2)}) collective-permute-start(f32[11,15,2,384]{3,2,1,0:T(2,128)S(1)} %get-tuple-element.31), channel_id=1, source_target_pairs={{0,4},{4,0},{8,12},{12,8},{1,5},{5,1},{9,13},{13,9},{2,6},{6,2},{1... | collective-permute-start | bytes 1520648 | tf_op jit(solution)/shard_map/ppermute | solution.py:50
  25.3 13.8 %copy-start.2 = (f32[9]{0:T(128)S(1)}, f32[9]{0:T(128)}, u32[]{:S(2)}) copy-start(f32[9]{0:T(128)} %refs_2_.3) | copy-start | bytes 112
  25.3 13.8 %collective-permute-start.7 = (f32[11,15,2,384]{3,2,1,0:T(2,128)S(1)}, f32[11,15,2,384]{3,2,1,0:T(2,128)S(1)}, u32[]{:S(2)}, u32[]{:S(2)}) collective-permute-start(f32[11,15,2,384]{3,2,1,0:T(2,128)S(1)} %get-tuple-element.32), channel_id=1, source_target_pairs={{4,8},{8,4},{5,9},{9,5},{6,10},{10,6},{7,11},{11,7},{20,24},{24,20... | collective-permute-start | bytes 1520648 | tf_op jit(solution)/shard_map/ppermute | solution.py:50
  42.2 10.1 %collective-permute-start.11 = (f32[5,12,2,384]{3,2,1,0:T(2,128)S(1)}, f32[5,12,2,384]{3,2,1,0:T(2,128)S(1)}, u32[]{:S(2)}, u32[]{:S(2)}) collective-permute-start(f32[5,12,2,384]{3,2,1,0:T(2,128)S(1)} %get-tuple-element.38), channel_id=1, source_target_pairs={{0,4},{4,0},{8,12},{12,8},{1,5},{5,1},{9,13},{13,9},{2,6},{6,2},{1... | collective-permute-start | bytes 552968 | tf_op jit(solution)/shard_map/ppermute | solution.py:50
  46.1 6.3 %collective-permute-start.12 = (f32[5,12,2,384]{3,2,1,0:T(2,128)S(1)}, f32[5,12,2,384]{3,2,1,0:T(2,128)S(1)}, u32[]{:S(2)}, u32[]{:S(2)}) collective-permute-start(f32[5,12,2,384]{3,2,1,0:T(2,128)S(1)} %get-tuple-element.39), channel_id=1, source_target_pairs={{4,8},{8,4},{5,9},{9,5},{6,10},{10,6},{7,11},{11,7},{20,24},{24,20... | collective-permute-start | bytes 552968 | tf_op jit(solution)/shard_map/ppermute | solution.py:50
  55.0 3.7 %collective-permute-start.13 = (f32[3,2,360]{2,1,0:T(2,128)S(1)}, f32[3,2,360]{2,1,0:T(2,128)S(1)}, u32[]{:S(2)}, u32[]{:S(2)}) collective-permute-start(f32[3,2,360]{2,1,0:T(2,128)S(1)} %get-tuple-element.43), channel_id=1, source_target_pairs={{0,2},{2,0},{1,3},{3,1},{4,6},{6,4},{5,7},{7,5},{8,10},{10,8},{9,1... | collective-permute-start | bytes 25928 | tf_op jit(solution)/shard_map/ppermute | solution.py:586

commit v5 on v4

--- a/solution.py
+++ b/solution.py
@@ -9,7 +9,7 @@
 
 STEPS = 6
 WIDTH = 3
-FORCED = ((0, 1, 2, 3), (4, 5))
+FORCED = ((0, 1, 2), (3, 4, 5))
 ROUNDS = STEPS // WIDTH
 LANES = 128
 CHUNK = 3072
@@ -106,7 +106,7 @@
 
 def edges_kernel(moves, *refs):
     inputs, own_out, edge_out, base = refs[:9], refs[9], refs[10], refs[11]
-    outs, held, buf, sems = refs[12:-11], refs[-11:-2], refs[-2], refs[-1]
+    held, buf, sems = refs[-11:-2], refs[-2], refs[-1]
     fetch(inputs, held, sems)
     soundings_of(len(moves()), base, *held[5:])
     held = held[:5]
@@ -129,10 +129,6 @@
                 jnp.where((lane >= gap) & (lane < gap + STEPS), start, 0.0),
             )
             edge_out[p, l] = both[0:rows]
-    for i, (_, start, _) in enumerate(moves()):
-        outs[2 * i][...] = own_out[:, pl.ds(start, STEPS)]
-        outs[2 * i + 1][...] = edge_out[:, pl.ds(start, STEPS)]
-
 
 def payload_kernel(number, levels, tracers, *refs):
     out, flat = refs[-2:]
@@ -163,24 +159,10 @@
     return jnp.where(lane < columns - tail, plane[..., tail : tail + LANES], edge)
 
 
-def tiles_kernel(moves, columns, own, edge, *refs):
-    number = len(moves())
-    far, (body, first_out, second_out) = refs[: 2 * number], refs[2 * number :]
-    planes, levels, rows, _ = own.shape
+def tile_messages(body, first_out, second_out):
+    planes, _, rows, _ = body.shape
     tracers = planes - 5
-    tail = columns // LANES * LANES
     mixing, east, west, north, south = range(tracers, planes)
-    start, _ = window(0, levels)
-    pick = pl.ds(start, levels)
-    body[:, pick, :, 0:tail] = own[:, :, :, 0:tail]
-    for p in range(planes):
-        body[p, pick, :, tail : tail + LANES] = with_edges(own[p], edge[p], columns)
-    for i, (_, _, slot) in enumerate(moves()):
-        part, beside = far[2 * i], far[2 * i + 1]
-        there = pl.ds(slot, STEPS)
-        body[:, there, :, 0:tail] = part[:, :, :, 0:tail]
-        for p in range(planes):
-            body[p, there, :, tail : tail + LANES] = with_edges(part[p], beside[p], columns)
 
     def rows_of(out, first, third):
         near = list(range(tracers)) + [mixing, north, south, east, west]
@@ -199,6 +181,21 @@
     def _():
         rows_of(first_out, 0, 2)
         rows_of(second_out, rows - 2, rows - 3)
+
+
+def spread_kernel(moves, columns, own, edge, body, first_out, second_out, *outs):
+    tail = columns // LANES * LANES
+    body[:, :, :, 0:tail] = own[:, :, :, 0:tail]
+    for p in range(own.shape[0]):
+        body[p, :, :, tail : tail + LANES] = with_edges(own[p], edge[p], columns)
+    for out, (_, start, _) in zip(outs, moves()):
+        out[...] = body[:, pl.ds(start, STEPS)]
+    tile_messages(body, first_out, second_out)
+
+
+def far_kernel(number, *refs):
+    for i in range(number):
+        tile_messages(refs[i], refs[number + 2 * i], refs[number + 2 * i + 1])
 
 
 def advance(step, src, dst, outer, coef, forcing, profile, flux, levels):
@@ -281,11 +278,14 @@
     ref[plane, pick, 6:7, :] = jnp.where(even, two, one)
 
 
-def first_kernel(levels, body, first, second, *refs):
+def first_kernel(moves, levels, *refs):
+    number = len(moves())
+    groups = [refs[3 * i : 3 * i + 3] for i in range(1 + number)]
+    refs = refs[3 * (1 + number) :]
     count = len(forced_in(0))
     forcings, profile = refs[:count], refs[count]
     state_out, coef_out, flux, first_out, second_out, work, other, outer, raw = refs[count + 1 :]
-    planes, wide, rows, lanes = body.shape
+    planes, _, rows, lanes = groups[0][0].shape
     tracers = planes - 5
     mixing, east, west, north, south = range(tracers, planes)
     raw[...] = jnp.zeros_like(raw)
@@ -294,19 +294,21 @@
     clear_pads(other)
     clear_pads(outer)
     even = is_even()
-    pick = slice(1, wide + 1)
-    for p in range(planes):
-        ref, plane = (work, p) if p < tracers else (raw, p - tracers)
-        ref[plane, pick, 0:rows, :] = body[p]
-    near = list(range(tracers)) + [mixing, north, south, east, west]
-    for entry, p in enumerate(near):
-        ref, plane = (work, p) if p < tracers else (raw, p - tracers)
-        ref[plane, pick, rows : rows + 2, :] = jnp.where(even, first[entry], second[entry])
-        ref[plane, pick, 6:8, :] = jnp.where(even, second[entry], first[entry])
-    for k in range(tracers):
-        place_outer(outer, k, pick, first, second, len(near) + k // 2, k % 2)
-    for plane, k in ((5, tracers), (6, tracers + 1)):
-        place_outer(raw, plane, pick, first, second, len(near) + k // 2, k % 2)
+    starts = [window(0, levels)[0]] + [slot for _, _, slot in moves()]
+    for (body, first, second), start in zip(groups, starts):
+        pick = pl.ds(start + 1, body.shape[1])
+        for p in range(planes):
+            ref, plane = (work, p) if p < tracers else (raw, p - tracers)
+            ref[plane, pick, 0:rows, :] = body[p]
+        near = list(range(tracers)) + [mixing, north, south, east, west]
+        for entry, p in enumerate(near):
+            ref, plane = (work, p) if p < tracers else (raw, p - tracers)
+            ref[plane, pick, rows : rows + 2, :] = jnp.where(even, first[entry], second[entry])
+            ref[plane, pick, 6:8, :] = jnp.where(even, second[entry], first[entry])
+        for k in range(tracers):
+            place_outer(outer, k, pick, first, second, len(near) + k // 2, k % 2)
+        for plane, k in ((5, tracers), (6, tracers + 1)):
+            place_outer(raw, plane, pick, first, second, len(near) + k // 2, k % 2)
     coef_out[0] = raw[0]
     coef_out[1] = raw[1]
     coef_out[3] = raw[3]
@@ -361,10 +363,9 @@
         give[...] = jnp.zeros_like(give)
 
 
-def forcing_kernel(steps, tracers, levels, rows, columns, *refs):
-    got, (out, left, right, terms, flat, parts) = refs[:-6], refs[-6:]
+def prepare(tracers, levels, rows, columns, got, terms, right, keys, flat, parts):
     sources, groups, _, held = got[0].shape
-    lanes = out.shape[-1]
+    lanes = right.shape[0]
     subs = lax.axis_size("sub")
     tile, sub = lax.axis_index("tiles"), lax.axis_index("sub")
     for s in range(sources * len(got)):
@@ -395,17 +396,32 @@
         high = value.astype(BF16).astype(F32)
         parts[0, t] = high
         parts[1, t] = value - high
-    first, count = window(STEPS - 1 - steps[0], levels)
+    first, count = window(STEPS - 1, levels)
     batch = flat.shape[1]
     for i in range(count):
         for t in range(tracers):
             row_id = pl.ds(tracers + 2 + first + i, 1)
             both = [jnp.broadcast_to(parts[k, t, row_id, :], (8, batch)) for k in range(2)]
             terms[i * tracers + t] = jnp.concatenate(both, axis=0).astype(BF16)
+    keys[...] = jnp.broadcast_to(key, keys.shape)
+
+
+def prepare_kernel(tracers, levels, rows, columns, *refs):
+    prepare(tracers, levels, rows, columns, refs[:-5], *refs[-5:])
+
+
+def forcing_kernel(steps, tracers, levels, rows, columns, *refs):
+    if len(refs) > 5:
+        out, left, terms, right, keys = refs[-7:-2]
+        prepare(tracers, levels, rows, columns, refs[:-7], terms, right, keys, *refs[-2:])
+    else:
+        terms, right, keys, out, left = refs
+    first, _ = window(STEPS - 1, levels)
+    batch = keys.shape[1]
     ids = lax.broadcasted_iota(jnp.int32, (8, batch), 0).astype(F32)
     for i, now in enumerate(steps):
         begin, size = window(STEPS - 1 - now, levels)
-        hit = jnp.where(key == ids + now * 8.0, 1.0, 0.0)
+        hit = jnp.where(keys[...] == ids + now * 8.0, 1.0, 0.0)
         mask = jnp.concatenate([hit, hit], axis=0).astype(BF16)
         offset = (begin - first) * tracers
 
@@ -470,27 +486,34 @@
     crossed = [lax.ppermute(averaging_kernel, ("levels", "sub"), pairs) for _, pairs in across]
     fields = (final_adjoint, lon_courant, lat_courant, upwind_flags, vertical_mixing)
     fields += (misfit, averaging_kernel, sounding_owner.reshape(1, held), sounding_target)
-    level_part, edge_part = shape(planes, STEPS, rows, lanes), shape(planes, STEPS, rows, LANES)
     groups = -(-(tracers + 2 + wide) // 4)
     flat_rows = -(-groups // 2) * 8
-    own, edge, payload, *parts = call(
+    own, edge, payload = call(
         functools.partial(edges_kernel, moves),
         60,
         out_shape=[shape(planes, levels, rows, lanes), shape(planes, levels, rows, LANES)]
-        + [shape(flat_rows, held)]
-        + [level_part, edge_part] * number,
+        + [shape(flat_rows, held)],
         in_specs=[HBM] * 9,
-        out_specs=[VMEM] * (3 + 2 * number),
+        out_specs=[VMEM] * 3,
         scratch_shapes=room(*fields)
         + [pltpu.VMEM((planes, levels, 8, lanes), F32), pltpu.SemaphoreType.DMA((9,))],
         name="edges",
     )(*fields)
     edge = lax.ppermute(edge, "sub", sub_pairs)
     swapped = lax.ppermute(payload, "sub", sub_pairs)
-    parts, beside, crossed, swapped = lax.optimization_barrier((parts, beside, crossed, swapped))
-    for i, (pairs, cross) in enumerate(across):
-        parts[2 * i] = lax.ppermute(parts[2 * i], "levels", pairs)
-        parts[2 * i + 1] = lax.ppermute(parts[2 * i + 1], ("levels", "sub"), cross)
+    edge, beside, crossed, swapped = lax.optimization_barrier((edge, beside, crossed, swapped))
+    depth = tracers + 5 + (tracers + 3) // 2
+    body, first, second, *parts = call(
+        functools.partial(spread_kernel, moves, columns),
+        8,
+        out_shape=[shape(planes, levels, rows, lanes)]
+        + [shape(depth, levels, 2, lanes)] * 2
+        + [shape(planes, STEPS, rows, lanes)] * number,
+        in_specs=[VMEM] * 2,
+        out_specs=[VMEM] * (3 + number),
+        name="spread",
+    )(own, edge)
+    parts = [lax.ppermute(part, "levels", pairs) for part, (pairs, _) in zip(parts, across)]
     both = call(
         functools.partial(payload_kernel, number, levels, tracers),
         8,
@@ -505,39 +528,57 @@
     else:
         got = [lax.all_gather(both, "tiles", tiled=True)]
 
-    message = shape(tracers + 5 + (tracers + 3) // 2, wide, 2, lanes)
-    body, first, second = call(
-        functools.partial(tiles_kernel, moves, columns),
-        8,
-        out_shape=(shape(planes, wide, rows, lanes), message, message),
-        in_specs=[VMEM] * (2 + 2 * number),
-        out_specs=[VMEM] * 3,
-        name="tiles",
-    )(own, edge, *parts)
-    first, second = swap_tiles(first, 0), swap_tiles(second, 1)
+    blocks = [body, swap_tiles(first, 0), swap_tiles(second, 1)]
 
     held_here = got[0].shape[0]
     sources = held_here if len(got) > 1 else max(1, min(held_here, CHUNK // held))
     batch = sources * len(got) * held
+    count = window(STEPS - 1, levels)[1] * tracers
+    sizes = (tracers, levels, rows, columns)
+    prepared = [((count, 16, batch), BF16), ((lanes, batch), BF16), ((8, batch), F32)]
+    working = [pltpu.VMEM((flat_rows, batch), F32), pltpu.VMEM((2, tracers, flat_rows, batch), F32)]
+    if held_here == sources:
+        got = call(
+            functools.partial(prepare_kernel, *sizes),
+            16,
+            out_shape=[jax.ShapeDtypeStruct(*x) for x in prepared],
+            in_specs=[VMEM] * len(got),
+            out_specs=[VMEM] * 3,
+            scratch_shapes=working,
+            name="prepare",
+        )(*got)
+        parts, got = lax.optimization_barrier((parts, got))
+    if number:
+        far = call(
+            functools.partial(far_kernel, number),
+            8,
+            out_shape=[shape(depth, STEPS, 2, lanes)] * (2 * number),
+            in_specs=[VMEM] * number,
+            out_specs=[VMEM] * (2 * number),
+            name="far",
+        )(*parts)
+    for i in range(number):
+        blocks += [parts[i], swap_tiles(far[2 * i], 0), swap_tiles(far[2 * i + 1], 1)]
+
     def forcing_of(steps):
-        count = window(STEPS - 1 - steps[0], levels)[1]
         force_shape = (len(steps), tracers, wide, 8, lanes)
+        scratch = [pltpu.VMEM((count * 16, batch), BF16)]
         block = pl.BlockSpec((sources, groups, 4, held), lambda i: (i, 0, 0, 0))
+        specs, limit = [block], 60
+        if len(got) == 3:
+            specs = [pl.BlockSpec(x.shape, lambda i, rank=x.ndim: (0,) * rank) for x in got]
+            limit = 24
+        else:
+            scratch += [pltpu.VMEM(*x) for x in prepared] + working
         return call(
-            functools.partial(forcing_kernel, steps, tracers, levels, rows, columns),
-            20 if batch <= CHUNK else 60,
-            flops=2 * len(steps) * count * tracers * 16 * batch * lanes,
+            functools.partial(forcing_kernel, steps, *sizes),
+            limit,
+            flops=2 * len(steps) * count * 16 * batch * lanes,
             out_shape=shape(*force_shape),
             grid=(held_here // sources,),
-            in_specs=[block] * len(got),
+            in_specs=specs,
             out_specs=pl.BlockSpec(force_shape, lambda i: (0, 0, 0, 0, 0)),
-            scratch_shapes=[
-                pltpu.VMEM((count * tracers * 16, batch), BF16),
-                pltpu.VMEM((lanes, batch), BF16),
-                pltpu.VMEM((count * tracers, 16, batch), BF16),
-                pltpu.VMEM((flat_rows, batch), F32),
-                pltpu.VMEM((2, tracers, flat_rows, batch), F32),
-            ],
+            scratch_shapes=scratch,
             name="forcing" + str(steps[0]),
         )(*got)
 
@@ -552,14 +593,14 @@
 
     scratch = [pltpu.VMEM(state_shape, F32)] * 3
     state, coef, flux, first, second = call(
-        functools.partial(first_kernel, levels),
+        functools.partial(first_kernel, moves, levels),
         16,
         out_shape=[shape(*state_shape), shape(*coef_shape), shape(*flux_shape), *messages(1)],
-        in_specs=[VMEM] * (3 + len(forced_in(0))) + [SMEM],
+        in_specs=[VMEM] * (len(blocks) + len(forced_in(0))) + [SMEM],
         out_specs=[VMEM] * 5,
         scratch_shapes=scratch + [pltpu.VMEM((7, wide + 2, 8, lanes), F32)],
         name="round0",
-    )(body, first, second, *[forcings[i] for i in forced_in(0)], level_profile)
+    )(*blocks, *[forcings[i] for i in forced_in(0)], level_profile)
     half = rows // 2 if bands == 2 else rows
     for round_id in range(1, ROUNDS):
         first, second = swap_tiles(first, 0), swap_tiles(second, 1)

time: 59.5 us -> 55.1 us (0.926)
  starting transfers between devices: 19.4 us -> 16.9 us
  Pallas kernels: 25.7 us -> 23.7 us
    ppermute x3, waiting for transfers between devices: 0.6 us -> 5.17 us  [per_device(): lax.ppermute(both, 'tiles', [(i, i ^ k) for i in range(tiles)])]
    ppermute x2 -> x1, waiting for transfers between devices: 3.45 us -> 0.01 us  [per_device(): lax.ppermute(part, 'levels', pairs)]
    ppermute x3, starting transfers between devices: 7.83 us -> 4.45 us  [per_device(): lax.ppermute(both, 'tiles', [(i, i ^ k) for i in range(tiles)])]
    pallas_call x4 -> x6, Pallas kernels: 20.7 us -> 18.9 us  [the longest x2 13.7 us: forcing_of(): call(functools.partial(forcing_kernel, steps, *sizes), limit, flops=2 * l...]
    ppermute x4 -> x6, starting transfers between devices: 5.43 us -> 7 us  [swap_tiles(): return lax.ppermute(value, 'tiles', pairs)]
    ppermute x2 -> x1, starting transfers between devices: 1.52 us -> 0.4 us  [per_device(): lax.ppermute(part, 'levels', pairs)]
    ppermute x4 -> x6, waiting for transfers between devices: 0.76 us -> 0.02 us  [swap_tiles(): return lax.ppermute(value, 'tiles', pairs)]
    ppermute x1, waiting for transfers between devices: 2.86 us -> 2.15 us  [per_device(): flux_gradient = keep + lax.ppermute(give, 'levels', [(0, 1), (1, 0)])]
  transfers between devices with their start and end apart: 14 -> 15, of which waited for: 6 -> 5; matrix products, arithmetic and copies ran while one was open for 0% -> 0% of each run, Pallas kernels for 30% -> 29%
where the time goes in v5:
time: 55.1 us; the launch traced here: 54.8 us
  Pallas kernels  23.7 us (43%)
  starting transfers between devices  16.9 us (31%)
  waiting for transfers between devices  11 us (20%)
  local copies, waits for them, and re-layouts  1.78 us (3%)
  between operations  0.78 us (1%)
  other arithmetic  0.6 us (1%)
    pallas_call x2, Pallas kernels, forcing_of(): call(functools.partial(forcing_kernel, steps, *sizes), limit, flops=2 * l...  13.7 us
    ppermute x6, starting transfers between devices, swap_tiles(): return lax.ppermute(value, 'tiles', pairs)  7 us
    ppermute x3, waiting for transfers between devices, per_device(): lax.ppermute(both, 'tiles', [(i, i ^ k) for i in range(tiles)])  5.17 us
    ppermute x3, starting transfers between devices, per_device(): lax.ppermute(both, 'tiles', [(i, i ^ k) for i in range(tiles)])  4.45 us
    pallas_call x1, Pallas kernels, per_device(): call(functools.partial(first_kernel, moves, levels), 16, out_shape=[shape...  3.02 us
    ppermute x1, starting transfers between devices, per_device(): lax.ppermute(averaging_kernel, 'levels', pairs)  2.92 us
    pallas_call x1, Pallas kernels, per_device(): call(functools.partial(next_kernel, round_id, levels, rows), 16, out_shap...  2.59 us
    ppermute x1, waiting for transfers between devices, per_device(): flux_gradient = keep + lax.ppermute(give, 'levels', [(0, 1), (1, 0)])  2.15 us
  transfers between devices with their start and end apart: 15, of which 5 were waited for; matrix products, arithmetic and copies ran while one was open for 0% of the time, Pallas kernels for 29%

profile of v5, /device:TPU:0, one launch (start us, length us, event | category | flops | bytes accessed | tf_op | source)
XLA Modules:
  0.0 54.8 jit_solution(12402568644081005938)
XLA Ops:
  0.6 2.1 %edges.1 = (f32[8,9,4,384]{3,2,1,0:T(4,128)}, f32[8,9,4,128]{3,2,1,0:T(4,128)}, f32[24,384]{1,0:T(8,128)}) custom-call(f32[3,9,4,360]{3,2,1,0:T(4,128)} %refs_0_.1, f32[9,4,360]{2,1,0:T(4,128)} %refs_1_.2, f32[9,4,360]{2,1,0:T(4,128)} %refs_2_.1, s32[2,9,4,360]{3,2,1,0:T(4,128)} %refs_3_.1, f32[9,4,360]{2,1,0:T(4,128)} %refs_4_.1, f32[3,384]{1,0:T(4,128)} %refs_5_.1, ...), custom_call_target="tpu_custom_call" | custom-call | bytes 1048576 | tf_op jit(solution)/shard_map/edges/pallas_call | solution.py:491
  2.8 0.5 collective-permute-start
  3.4 2.9 %collective-permute-start.1 = (f32[9,384]{1,0:T(8,128)}, f32[9,384]{1,0:T(8,128)S(1)}, u32[]{:S(2)}, u32[]{:S(2)}) collective-permute-start(f32[9,384]{1,0:T(8,128)} %refs_6_.1), channel_id=1, source_target_pairs={{0,2},{2,0},{1,3},{3,1},{4,6},{6,4},{5,7},{7,5},{8,10},{10,8},{9,1... | collective-permute-start | bytes 41480 | tf_op jit(solution)/shard_map/ppermute | solution.py:485
  6.3 2.0 %collective-permute-done.1.refs_1_ = f32[9,384]{1,0:T(8,128)S(1)} collective-permute-done((f32[9,384]{1,0:T(8,128)}, f32[9,384]{1,0:T(8,128)S(1)}, u32[]{:S(2)}, u32[]{:S(2)}) %collective-permute-start.1) | collective-permute-done | bytes 13856 | tf_op jit(solution)/shard_map/ppermute | solution.py:485
  8.3 1.7 %collective-permute-done.2.refs_3_ = f32[9,384]{1,0:T(8,128)S(1)} collective-permute-done((f32[9,384]{1,0:T(8,128)}, f32[9,384]{1,0:T(8,128)S(1)}, u32[]{:S(2)}, u32[]{:S(2)}) %collective-permute-start.2) | collective-permute-done | bytes 13856 | tf_op jit(solution)/shard_map/ppermute | solution.py:486
  10.0 1.0 %copy-done = f32[8,9,4,384]{3,2,1,0:T(4,128)S(1)} copy-done((f32[8,9,4,384]{3,2,1,0:T(4,128)S(1)}, f32[8,9,4,384]{3,2,1,0:T(4,128)}, u32[]{:S(2)}) %copy-start) | copy-done | bytes 442392
  11.7 0.8 %copy-done.1 = f32[24,384]{1,0:T(8,128)S(1)} copy-done((f32[24,384]{1,0:T(8,128)S(1)}, f32[24,384]{1,0:T(8,128)}, u32[]{:S(2)}) %copy-start.1) | copy-done | bytes 36888
  12.5 1.9 %collective-permute-start.7 = (f32[2,5,4,384]{3,2,1,0:T(4,128)S(1)}, f32[2,5,4,384]{3,2,1,0:T(4,128)S(1)}, u32[]{:S(2)}, u32[]{:S(2)}) collective-permute-start(f32[2,5,4,384]{3,2,1,0:T(4,128)S(1)} %payload.1.refs_0_), channel_id=1, source_target_pairs={{0,4},{4,0},{8,12},{12,8},{1,5},{5,1},{9,13},{13,9},{2,6},{6,2},{1... | collective-permute-start | bytes 184328 | tf_op jit(solution)/shard_map/ppermute | solution.py:527
  14.4 2.6 %collective-permute-start.8 = (f32[2,5,4,384]{3,2,1,0:T(4,128)S(1)}, f32[2,5,4,384]{3,2,1,0:T(4,128)S(1)}, u32[]{:S(2)}, u32[]{:S(2)}) collective-permute-start(f32[2,5,4,384]{3,2,1,0:T(4,128)S(1)} %payload.1.refs_0_), channel_id=1, source_target_pairs={{0,8},{4,12},{8,0},{12,4},{1,9},{5,13},{9,1},{13,5},{2,10},{6,14},... | collective-permute-start | bytes 184328 | tf_op jit(solution)/shard_map/ppermute | solution.py:527
  17.0 0.9 %collective-permute-start.4 = (f32[11,9,2,384]{3,2,1,0:T(2,128)S(1)}, f32[11,9,2,384]{3,2,1,0:T(2,128)S(1)}, u32[]{:S(2)}, u32[]{:S(2)}) collective-permute-start(f32[11,9,2,384]{3,2,1,0:T(2,128)S(1)} %get-tuple-element.35), channel_id=1, source_target_pairs={{0,4},{4,0},{8,12},{12,8},{1,5},{5,1},{9,13},{13,9},{2,6},{6,2},{1... | collective-permute-start | bytes 912392 | tf_op jit(solution)/shard_map/ppermute | solution.py:50
  17.9 0.7 %collective-permute-start.5 = (f32[11,9,2,384]{3,2,1,0:T(2,128)S(1)}, f32[11,9,2,384]{3,2,1,0:T(2,128)S(1)}, u32[]{:S(2)}, u32[]{:S(2)}) collective-permute-start(f32[11,9,2,384]{3,2,1,0:T(2,128)S(1)} %get-tuple-element.36), channel_id=1, source_target_pairs={{4,8},{8,4},{5,9},{9,5},{6,10},{10,6},{7,11},{11,7},{20,24},{24,20... | collective-permute-start | bytes 912392 | tf_op jit(solution)/shard_map/ppermute | solution.py:50
  18.5 2.3 %collective-permute-done.8.refs_2_ = f32[2,5,4,384]{3,2,1,0:T(4,128)S(1)} collective-permute-done((f32[2,5,4,384]{3,2,1,0:T(4,128)S(1)}, f32[2,5,4,384]{3,2,1,0:T(4,128)S(1)}, u32[]{:S(2)}, u32[]{:S(2)}) %collective-permute-start.8) | collective-permute-done | bytes 61472 | tf_op jit(solution)/shard_map/ppermute | solution.py:527
  20.8 2.9 %collective-permute-done.9.refs_3_ = f32[2,5,4,384]{3,2,1,0:T(4,128)S(1)} collective-permute-done((f32[2,5,4,384]{3,2,1,0:T(4,128)S(1)}, f32[2,5,4,384]{3,2,1,0:T(4,128)S(1)}, u32[]{:S(2)}, u32[]{:S(2)}) %collective-permute-start.9) | collective-permute-done | bytes 61472 | tf_op jit(solution)/shard_map/ppermute | solution.py:527
  23.7 1.7 %prepare.1 = (bf16[42,16,3072]{2,1,0:T(8,128)(2,1)S(1)}, bf16[384,3072]{1,0:T(8,128)(2,1)S(1)}, f32[8,3072]{1,0:T(8,128)S(1)}) custom-call(f32[2,5,4,384]{3,2,1,0:T(4,128)S(1)} %payload.1.refs_0_, f32[2,5,4,384]{3,2,1,0:T(4,128)S(1)} %collective-permute-done.7.refs_1_, f32[2,5,4,384]{3,2,1,0:T(4,128)S(1)} %collective-permute-done.8.refs_2_, ...), custom_call_target="tpu_custom_call" | custom-call | bytes 1048576 | tf_op jit(solution)/shard_map/prepare/pallas_call | solution.py:541
  25.8 0.8 %collective-permute-start.11 = (f32[11,6,2,384]{3,2,1,0:T(2,128)S(1)}, f32[11,6,2,384]{3,2,1,0:T(2,128)S(1)}, u32[]{:S(2)}, u32[]{:S(2)}) collective-permute-start(f32[11,6,2,384]{3,2,1,0:T(2,128)S(1)} %get-tuple-element.46), channel_id=1, source_target_pairs={{4,8},{8,4},{5,9},{9,5},{6,10},{10,6},{7,11},{11,7},{20,24},{24,20... | collective-permute-start | bytes 608264 | tf_op jit(solution)/shard_map/ppermute | solution.py:50
  26.6 7.7 %forcing0.1.refs_6_ = f32[3,3,15,8,384]{4,3,2,1,0:T(8,128)S(1)} custom-call(bf16[42,16,3072]{2,1,0:T(8,128)(2,1)S(1)} %get-tuple-element.47.refs_0_, bf16[384,3072]{1,0:T(8,128)(2,1)S(1)} %get-tuple-element.48.refs_1_, f32[8,3072]{1,0:T(8,128)S(1)} %get-tuple-element.49.refs_2_), custom_call_target="tpu_custom_call" | custom-call | flops 4756340736 | bytes 1048576 | tf_op jit(solution)/shard_map/forcing0/pallas_call | solution.py:573
  34.4 3.0 %round0.1 = (f32[3,17,8,384]{3,2,1,0:T(8,128)S(1)}, f32[6,17,8,384]{3,2,1,0:T(8,128)S(1)}, f32[3,8,384]{2,1,0:T(8,128)S(1)}, f32[5,12,2,384]{3,2,1,0:T(2,128)S(1)}, f32[5,12,2,384]{3,2,1,0:T(2,128)S(1)}) custom-call(f32[8,9,4,384]{3,2,1,0:T(4,128)S(1)} %get-tuple-element.34.refs_0_, f32[11,9,2,384]{3,2,1,0:T(2,128)S(1)} %collective-permute-done.4.refs_1_, ...), custom_call_target="tpu_custom_call" | custom-call | bytes 1048576 | tf_op jit(solution)/shard_map/round0/pallas_call | solution.py:595
  37.4 3.6 %collective-permute-start.12 = (f32[5,12,2,384]{3,2,1,0:T(2,128)S(1)}, f32[5,12,2,384]{3,2,1,0:T(2,128)S(1)}, u32[]{:S(2)}, u32[]{:S(2)}) collective-permute-start(f32[5,12,2,384]{3,2,1,0:T(2,128)S(1)} %get-tuple-element.52), channel_id=1, source_target_pairs={{0,4},{4,0},{8,12},{12,8},{1,5},{5,1},{9,13},{13,9},{2,6},{6,2},{1... | collective-permute-start | bytes 552968 | tf_op jit(solution)/shard_map/ppermute | solution.py:50
  41.0 0.8 %collective-permute-start.13 = (f32[5,12,2,384]{3,2,1,0:T(2,128)S(1)}, f32[5,12,2,384]{3,2,1,0:T(2,128)S(1)}, u32[]{:S(2)}, u32[]{:S(2)}) collective-permute-start(f32[5,12,2,384]{3,2,1,0:T(2,128)S(1)} %get-tuple-element.53), channel_id=1, source_target_pairs={{4,8},{8,4},{5,9},{9,5},{6,10},{10,6},{7,11},{11,7},{20,24},{24,20... | collective-permute-start | bytes 552968 | tf_op jit(solution)/shard_map/ppermute | solution.py:50
  41.8 6.1 %forcing3.1.refs_0_ = f32[3,3,15,8,384]{4,3,2,1,0:T(8,128)S(1)} custom-call(bf16[42,16,3072]{2,1,0:T(8,128)(2,1)S(1)} %get-tuple-element.47.refs_0_, bf16[384,3072]{1,0:T(8,128)(2,1)S(1)} %get-tuple-element.48.refs_1_, f32[8,3072]{1,0:T(8,128)S(1)} %get-tuple-element.49.refs_2_), custom_call_target="tpu_custom_call" | custom-call | flops 4756340736 | bytes 1048576 | tf_op jit(solution)/shard_map/forcing3/pallas_call | solution.py:573
  47.9 2.6 %round1.1 = (f32[3,9,4,360]{3,2,1,0:T(4,128)}, f32[3,2,360]{2,1,0:T(2,128)S(1)}, f32[3,2,360]{2,1,0:T(2,128)S(1)}) custom-call(f32[3,17,8,384]{3,2,1,0:T(8,128)S(1)} %get-tuple-element.50.state, f32[6,17,8,384]{3,2,1,0:T(8,128)S(1)} %get-tuple-element.51.coef, f32[5,12,2,384]{3,2,1,0:T(2,128)S(1)} %collective-permute-done.12.first, ...), custom_call_target="tpu_custom_call" | custom-call | bytes 1048576 | tf_op jit(solution)/shard_map/round1/pallas_call | solution.py:614
  50.5 1.5 %collective-permute-start.14 = (f32[3,2,360]{2,1,0:T(2,128)S(1)}, f32[3,2,360]{2,1,0:T(2,128)S(1)}, u32[]{:S(2)}, u32[]{:S(2)}) collective-permute-start(f32[3,2,360]{2,1,0:T(2,128)S(1)} %get-tuple-element.57), channel_id=1, source_target_pairs={{0,2},{2,0},{1,3},{3,1},{4,6},{6,4},{5,7},{7,5},{8,10},{10,8},{9,1... | collective-permute-start | bytes 25928 | tf_op jit(solution)/shard_map/ppermute | solution.py:627
  52.0 2.1 %collective-permute-done.14 = f32[3,2,360]{2,1,0:T(2,128)S(1)} collective-permute-done((f32[3,2,360]{2,1,0:T(2,128)S(1)}, f32[3,2,360]{2,1,0:T(2,128)S(1)}, u32[]{:S(2)}, u32[]{:S(2)}) %collective-permute-start.14) | collective-permute-done | bytes 8672 | tf_op jit(solution)/shard_map/ppermute | solution.py:627
  54.2 0.6 %add.3 = f32[3,2,360]{2,1,0:T(2,128)} add(f32[3,2,360]{2,1,0:T(2,128)S(1)} %get-tuple-element.56, f32[3,2,360]{2,1,0:T(2,128)S(1)} %collective-permute-done.14) | non-fusion elementwise | flops 2160 | bytes 25920 | tf_op jit(solution)/shard_map/add | solution.py:627
  (22 shorter events, 1.2 us)
Async XLA Ops:
  2.8 7.2 %collective-permute-start = (f32[8,9,4,128]{3,2,1,0:T(4,128)}, f32[8,9,4,128]{3,2,1,0:T(4,128)S(1)}, u32[]{:S(2)}, u32[]{:S(2)}) collective-permute-start(f32[8,9,4,128]{3,2,1,0:T(4,128)} %get-tuple-element.31), channel_id=1, source_target_pairs={{0,1},{1,0},{2,3},{3,2},{4,5},{5,4},{6,7},{7,6},{8,9},{9,8},{10,11... | collective-permute-start | bytes 442376 | tf_op jit(solution)/shard_map/ppermute | solution.py:502
  3.3 6.7 %collective-permute-start.3 = (f32[24,384]{1,0:T(8,128)}, f32[24,384]{1,0:T(8,128)S(1)}, u32[]{:S(2)}, u32[]{:S(2)}) collective-permute-start(f32[24,384]{1,0:T(8,128)} %get-tuple-element.32.refs_0_), channel_id=1, source_target_pairs={{0,1},{1,0},{2,3},{3,2},{4,5},{5,4},{6,7},{7,6},{8,9},{9,8},{10,11... | collective-permute-start | bytes 110600 | tf_op jit(solution)/shard_map/ppermute | solution.py:503
  3.4 4.9 %collective-permute-start.1 = (f32[9,384]{1,0:T(8,128)}, f32[9,384]{1,0:T(8,128)S(1)}, u32[]{:S(2)}, u32[]{:S(2)}) collective-permute-start(f32[9,384]{1,0:T(8,128)} %refs_6_.1), channel_id=1, source_target_pairs={{0,2},{2,0},{1,3},{3,1},{4,6},{6,4},{5,7},{7,5},{8,10},{10,8},{9,1... | collective-permute-start | bytes 41480 | tf_op jit(solution)/shard_map/ppermute | solution.py:485
  6.3 3.7 %collective-permute-start.2 = (f32[9,384]{1,0:T(8,128)}, f32[9,384]{1,0:T(8,128)S(1)}, u32[]{:S(2)}, u32[]{:S(2)}) collective-permute-start(f32[9,384]{1,0:T(8,128)} %refs_6_.1), channel_id=1, source_target_pairs={{0,3},{1,2},{2,1},{3,0},{4,7},{5,6},{6,5},{7,4},{8,11},{9,10},{10,... | collective-permute-start | bytes 41480 | tf_op jit(solution)/shard_map/ppermute | solution.py:486
  10.0 1.0 %copy-start = (f32[8,9,4,384]{3,2,1,0:T(4,128)S(1)}, f32[8,9,4,384]{3,2,1,0:T(4,128)}, u32[]{:S(2)}) copy-start(f32[8,9,4,384]{3,2,1,0:T(4,128)} %get-tuple-element.30.own) | copy-start | bytes 1327108
  11.3 14.1 %collective-permute-start.6 = (f32[8,6,4,384]{3,2,1,0:T(4,128)S(1)}, f32[8,6,4,384]{3,2,1,0:T(4,128)S(1)}, u32[]{:S(2)}, u32[]{:S(2)}) collective-permute-start(f32[8,6,4,384]{3,2,1,0:T(4,128)S(1)} %get-tuple-element.37), channel_id=1, source_target_pairs={{0,2},{2,0},{1,3},{3,1},{4,6},{6,4},{5,7},{7,5},{8,10},{10,8},{9,1... | collective-permute-start | bytes 884744 | tf_op jit(solution)/shard_map/ppermute | solution.py:516
  11.7 0.8 %copy-start.1 = (f32[24,384]{1,0:T(8,128)S(1)}, f32[24,384]{1,0:T(8,128)}, u32[]{:S(2)}) copy-start(f32[24,384]{1,0:T(8,128)} %get-tuple-element.32.refs_0_) | copy-start | bytes 110596
  12.5 5.4 %collective-permute-start.7 = (f32[2,5,4,384]{3,2,1,0:T(4,128)S(1)}, f32[2,5,4,384]{3,2,1,0:T(4,128)S(1)}, u32[]{:S(2)}, u32[]{:S(2)}) collective-permute-start(f32[2,5,4,384]{3,2,1,0:T(4,128)S(1)} %payload.1.refs_0_), channel_id=1, source_target_pairs={{0,4},{4,0},{8,12},{12,8},{1,5},{5,1},{9,13},{13,9},{2,6},{6,2},{1... | collective-permute-start | bytes 184328 | tf_op jit(solution)/shard_map/ppermute | solution.py:527
  14.4 6.4 %collective-permute-start.8 = (f32[2,5,4,384]{3,2,1,0:T(4,128)S(1)}, f32[2,5,4,384]{3,2,1,0:T(4,128)S(1)}, u32[]{:S(2)}, u32[]{:S(2)}) collective-permute-start(f32[2,5,4,384]{3,2,1,0:T(4,128)S(1)} %payload.1.refs_0_), channel_id=1, source_target_pairs={{0,8},{4,12},{8,0},{12,4},{1,9},{5,13},{9,1},{13,5},{2,10},{6,14},... | collective-permute-start | bytes 184328 | tf_op jit(solution)/shard_map/ppermute | solution.py:527
  17.0 6.7 %collective-permute-start.9 = (f32[2,5,4,384]{3,2,1,0:T(4,128)S(1)}, f32[2,5,4,384]{3,2,1,0:T(4,128)S(1)}, u32[]{:S(2)}, u32[]{:S(2)}) collective-permute-start(f32[2,5,4,384]{3,2,1,0:T(4,128)S(1)} %payload.1.refs_0_), channel_id=1, source_target_pairs={{0,12},{4,8},{8,4},{12,0},{1,13},{5,9},{9,5},{13,1},{2,14},{6,10},... | collective-permute-start | bytes 184328 | tf_op jit(solution)/shard_map/ppermute | solution.py:527
  17.0 17.4 %collective-permute-start.4 = (f32[11,9,2,384]{3,2,1,0:T(2,128)S(1)}, f32[11,9,2,384]{3,2,1,0:T(2,128)S(1)}, u32[]{:S(2)}, u32[]{:S(2)}) collective-permute-start(f32[11,9,2,384]{3,2,1,0:T(2,128)S(1)} %get-tuple-element.35), channel_id=1, source_target_pairs={{0,4},{4,0},{8,12},{12,8},{1,5},{5,1},{9,13},{13,9},{2,6},{6,2},{1... | collective-permute-start | bytes 912392 | tf_op jit(solution)/shard_map/ppermute | solution.py:50
  17.9 16.5 %collective-permute-start.5 = (f32[11,9,2,384]{3,2,1,0:T(2,128)S(1)}, f32[11,9,2,384]{3,2,1,0:T(2,128)S(1)}, u32[]{:S(2)}, u32[]{:S(2)}) collective-permute-start(f32[11,9,2,384]{3,2,1,0:T(2,128)S(1)} %get-tuple-element.36), channel_id=1, source_target_pairs={{4,8},{8,4},{5,9},{9,5},{6,10},{10,6},{7,11},{11,7},{20,24},{24,20... | collective-permute-start | bytes 912392 | tf_op jit(solution)/shard_map/ppermute | solution.py:50
  25.6 8.7 %collective-permute-start.10 = (f32[11,6,2,384]{3,2,1,0:T(2,128)S(1)}, f32[11,6,2,384]{3,2,1,0:T(2,128)S(1)}, u32[]{:S(2)}, u32[]{:S(2)}) collective-permute-start(f32[11,6,2,384]{3,2,1,0:T(2,128)S(1)} %get-tuple-element.45), channel_id=1, source_target_pairs={{0,4},{4,0},{8,12},{12,8},{1,5},{5,1},{9,13},{13,9},{2,6},{6,2},{1... | collective-permute-start | bytes 608264 | tf_op jit(solution)/shard_map/ppermute | solution.py:50
  25.8 8.5 %copy-start.2 = (f32[9]{0:T(128)S(1)}, f32[9]{0:T(128)}, u32[]{:S(2)}) copy-start(f32[9]{0:T(128)} %refs_1_.3) | copy-start | bytes 112
  25.8 8.5 %collective-permute-start.11 = (f32[11,6,2,384]{3,2,1,0:T(2,128)S(1)}, f32[11,6,2,384]{3,2,1,0:T(2,128)S(1)}, u32[]{:S(2)}, u32[]{:S(2)}) collective-permute-start(f32[11,6,2,384]{3,2,1,0:T(2,128)S(1)} %get-tuple-element.46), channel_id=1, source_target_pairs={{4,8},{8,4},{5,9},{9,5},{6,10},{10,6},{7,11},{11,7},{20,24},{24,20... | collective-permute-start | bytes 608264 | tf_op jit(solution)/shard_map/ppermute | solution.py:50
  37.4 10.5 %collective-permute-start.12 = (f32[5,12,2,384]{3,2,1,0:T(2,128)S(1)}, f32[5,12,2,384]{3,2,1,0:T(2,128)S(1)}, u32[]{:S(2)}, u32[]{:S(2)}) collective-permute-start(f32[5,12,2,384]{3,2,1,0:T(2,128)S(1)} %get-tuple-element.52), channel_id=1, source_target_pairs={{0,4},{4,0},{8,12},{12,8},{1,5},{5,1},{9,13},{13,9},{2,6},{6,2},{1... | collective-permute-start | bytes 552968 | tf_op jit(solution)/shard_map/ppermute | solution.py:50
  41.0 6.9 %collective-permute-start.13 = (f32[5,12,2,384]{3,2,1,0:T(2,128)S(1)}, f32[5,12,2,384]{3,2,1,0:T(2,128)S(1)}, u32[]{:S(2)}, u32[]{:S(2)}) collective-permute-start(f32[5,12,2,384]{3,2,1,0:T(2,128)S(1)} %get-tuple-element.53), channel_id=1, source_target_pairs={{4,8},{8,4},{5,9},{9,5},{6,10},{10,6},{7,11},{11,7},{20,24},{24,20... | collective-permute-start | bytes 552968 | tf_op jit(solution)/shard_map/ppermute | solution.py:50
  50.5 3.7 %collective-permute-start.14 = (f32[3,2,360]{2,1,0:T(2,128)S(1)}, f32[3,2,360]{2,1,0:T(2,128)S(1)}, u32[]{:S(2)}, u32[]{:S(2)}) collective-permute-start(f32[3,2,360]{2,1,0:T(2,128)S(1)} %get-tuple-element.57), channel_id=1, source_target_pairs={{0,2},{2,0},{1,3},{3,1},{4,6},{6,4},{5,7},{7,5},{8,10},{10,8},{9,1... | collective-permute-start | bytes 25928 | tf_op jit(solution)/shard_map/ppermute | solution.py:627

commit v6 on v5

--- a/solution.py
+++ b/solution.py
@@ -9,7 +9,7 @@
 
 STEPS = 6
 WIDTH = 3
-FORCED = ((0, 1, 2), (3, 4, 5))
+FORCED = ((0, 1, 2, 5), (3, 4))
 ROUNDS = STEPS // WIDTH
 LANES = 128
 CHUNK = 3072
@@ -411,40 +411,42 @@
 
 
 def forcing_kernel(steps, tracers, levels, rows, columns, *refs):
-    if len(refs) > 5:
-        out, left, terms, right, keys = refs[-7:-2]
-        prepare(tracers, levels, rows, columns, refs[:-7], terms, right, keys, *refs[-2:])
+    if len(refs) > 4:
+        out, terms, right, keys = refs[-6:-2]
+        prepare(tracers, levels, rows, columns, refs[:-6], terms, right, keys, *refs[-2:])
     else:
-        terms, right, keys, out, left = refs
+        terms, right, keys, out = refs
     first, _ = window(STEPS - 1, levels)
     batch = keys.shape[1]
     ids = lax.broadcasted_iota(jnp.int32, (8, batch), 0).astype(F32)
     for i, now in enumerate(steps):
         begin, size = window(STEPS - 1 - now, levels)
-        hit = jnp.where(keys[...] == ids + now * 8.0, 1.0, 0.0)
+        last = now % WIDTH == WIDTH - 1 and 2 * rows == 8
+        if last and now - WIDTH in steps:
+            continue
+        mate = now + WIDTH if last and now + WIDTH in steps else None
+        wanted = ids + now * 8.0
+        if mate is not None:
+            wanted = jnp.where(ids < rows, wanted, ids - rows + mate * 8.0)
+        hit = jnp.where(keys[...] == wanted, 1.0, 0.0)
         mask = jnp.concatenate([hit, hit], axis=0).astype(BF16)
-        offset = (begin - first) * tracers
-
-        def fill(q, carry, mask=mask, offset=offset):
-            left[pl.ds(pl.multiple_of(q * 16, 16), 16), :] = terms[offset + q] * mask
-            return carry
-
-        lax.fori_loop(0, size * tracers, fill, 0)
+        pick = pl.ds((begin - first) * tracers, size * tracers)
+        left = (terms[pick] * mask[None]).reshape(size * tracers * 16, batch)
         product = lax.dot_general(
-            left[0 : size * tracers * 16, :],
-            right[...],
-            (((1,), (1,)), ((), ())),
-            preferred_element_type=F32,
+            left, right[...], (((1,), (1,)), ((), ())), preferred_element_type=F32
         )
         for l in range(size):
             for t in range(tracers):
                 base = (l * tracers + t) * 16
                 value = product[base : base + 8] + product[base + 8 : base + 16]
-                if pl.num_programs(0) == 1:
-                    out[i, t, begin + l] = value
-                else:
-                    old = jnp.where(pl.program_id(0) == 0, 0.0, out[i, t, begin + l])
-                    out[i, t, begin + l] = old + value
+                places = [((i, t, begin + l), value)]
+                if mate is not None:
+                    places.append(((steps.index(mate), t, begin + l), pltpu.roll(value, rows, 0)))
+                for place, part in places:
+                    if pl.num_programs(0) == 1:
+                        out[place] = part
+                    else:
+                        out[place] = jnp.where(pl.program_id(0) == 0, 0.0, out[place]) + part
 
 
 def per_device(
@@ -481,9 +483,7 @@
     def room(*arrays):
         return [pltpu.VMEM(x.shape, x.dtype) for x in arrays]
 
-    across = [(pairs, [(a * subs + c, b * subs + d) for a, b in pairs for c, d in sub_pairs]) for pairs, _, _ in moves()]
-    beside = [lax.ppermute(averaging_kernel, "levels", pairs) for pairs, _ in across]
-    crossed = [lax.ppermute(averaging_kernel, ("levels", "sub"), pairs) for _, pairs in across]
+    beside = [lax.ppermute(averaging_kernel, "levels", pairs) for pairs, _, _ in moves()]
     fields = (final_adjoint, lon_courant, lat_courant, upwind_flags, vertical_mixing)
     fields += (misfit, averaging_kernel, sounding_owner.reshape(1, held), sounding_target)
     groups = -(-(tracers + 2 + wide) // 4)
@@ -501,7 +501,8 @@
     )(*fields)
     edge = lax.ppermute(edge, "sub", sub_pairs)
     swapped = lax.ppermute(payload, "sub", sub_pairs)
-    edge, beside, crossed, swapped = lax.optimization_barrier((edge, beside, crossed, swapped))
+    edge, beside, swapped = lax.optimization_barrier((edge, beside, swapped))
+    crossed = [lax.ppermute(part, "sub", sub_pairs) for part in beside]
     depth = tracers + 5 + (tracers + 3) // 2
     body, first, second, *parts = call(
         functools.partial(spread_kernel, moves, columns),
@@ -513,7 +514,7 @@
         out_specs=[VMEM] * (3 + number),
         name="spread",
     )(own, edge)
-    parts = [lax.ppermute(part, "levels", pairs) for part, (pairs, _) in zip(parts, across)]
+    parts = [lax.ppermute(part, "levels", pairs) for part, (pairs, _, _) in zip(parts, moves())]
     both = call(
         functools.partial(payload_kernel, number, levels, tracers),
         8,
@@ -562,7 +563,7 @@
 
     def forcing_of(steps):
         force_shape = (len(steps), tracers, wide, 8, lanes)
-        scratch = [pltpu.VMEM((count * 16, batch), BF16)]
+        scratch = []
         block = pl.BlockSpec((sources, groups, 4, held), lambda i: (i, 0, 0, 0))
         specs, limit = [block], 60
         if len(got) == 3:

time: 55.1 us -> 52 us (0.944)
  Pallas kernels: 23.7 us -> 19.4 us
    pallas_call x2, Pallas kernels: 13.7 us -> 9.47 us  [forcing_of(): call(functools.partial(forcing_kernel, steps, *sizes), limit, flops=2 * l...]
    ppermute x1, starting transfers between devices: 0.4 us -> 2.09 us  [per_device(): lax.ppermute(part, 'levels', pairs)]
    ppermute x1, starting transfers between devices: 1.51 us -> 0.53 us  [per_device(): flux_gradient = keep + lax.ppermute(give, 'levels', [(0, 1), (1, 0)])]
    ppermute x1, waiting for transfers between devices: 2.15 us -> 3.14 us  [per_device(): flux_gradient = keep + lax.ppermute(give, 'levels', [(0, 1), (1, 0)])]
  transfers between devices with their start and end apart: 15 -> 15, of which waited for: 5 -> 5; matrix products, arithmetic and copies ran while one was open for 0% -> 0% of each run, Pallas kernels for 29% -> 22%
where the time goes in v6:
time: 52 us; the launch traced here: 51.5 us
  Pallas kernels  19.4 us (37%)
  starting transfers between devices  17.3 us (33%)
  waiting for transfers between devices  11.5 us (22%)
  local copies, waits for them, and re-layouts  1.78 us (3%)
  between operations  0.78 us (2%)
  other arithmetic  0.6 us (1%)
    pallas_call x2, Pallas kernels, forcing_of(): call(functools.partial(forcing_kernel, steps, *sizes), limit, flops=2 * l...  9.47 us
    ppermute x6, starting transfers between devices, swap_tiles(): return lax.ppermute(value, 'tiles', pairs)  6.75 us
    ppermute x3, waiting for transfers between devices, per_device(): lax.ppermute(both, 'tiles', [(i, i ^ k) for i in range(tiles)])  5.15 us
    ppermute x3, starting transfers between devices, per_device(): lax.ppermute(both, 'tiles', [(i, i ^ k) for i in range(tiles)])  4.45 us
    ppermute x1, waiting for transfers between devices, per_device(): flux_gradient = keep + lax.ppermute(give, 'levels', [(0, 1), (1, 0)])  3.14 us
    pallas_call x1, Pallas kernels, per_device(): call(functools.partial(first_kernel, moves, levels), 16, out_shape=[shape...  3.04 us
    ppermute x1, starting transfers between devices, per_device(): lax.ppermute(averaging_kernel, 'levels', pairs)  2.92 us
    pallas_call x1, Pallas kernels, per_device(): call(functools.partial(next_kernel, round_id, levels, rows), 16, out_shap...  2.61 us
  transfers between devices with their start and end apart: 15, of which 5 were waited for; matrix products, arithmetic and copies ran while one was open for 0% of the time, Pallas kernels for 22%

profile of v6, /device:TPU:0, one launch (start us, length us, event | category | flops | bytes accessed | tf_op | source)
XLA Modules:
  0.0 51.5 jit_solution(3761458137638320893)
XLA Ops:
  0.6 2.1 %edges.1 = (f32[8,9,4,384]{3,2,1,0:T(4,128)}, f32[8,9,4,128]{3,2,1,0:T(4,128)}, f32[24,384]{1,0:T(8,128)}) custom-call(f32[3,9,4,360]{3,2,1,0:T(4,128)} %refs_0_.1, f32[9,4,360]{2,1,0:T(4,128)} %refs_1_.1, f32[9,4,360]{2,1,0:T(4,128)} %refs_2_.2, s32[2,9,4,360]{3,2,1,0:T(4,128)} %refs_3_.1, f32[9,4,360]{2,1,0:T(4,128)} %refs_4_.1, f32[3,384]{1,0:T(4,128)} %refs_5_.1, ...), custom_call_target="tpu_custom_call" | custom-call | bytes 1048576 | tf_op jit(solution)/shard_map/edges/pallas_call | solution.py:491
  3.4 2.9 %collective-permute-start.1 = (f32[9,384]{1,0:T(8,128)}, f32[9,384]{1,0:T(8,128)S(1)}, u32[]{:S(2)}, u32[]{:S(2)}) collective-permute-start(f32[9,384]{1,0:T(8,128)} %refs_6_.1), channel_id=1, source_target_pairs={{0,2},{2,0},{1,3},{3,1},{4,6},{6,4},{5,7},{7,5},{8,10},{10,8},{9,1... | collective-permute-start | bytes 41480 | tf_op jit(solution)/shard_map/ppermute | solution.py:486
  6.3 2.0 %collective-permute-done.1.refs_1_ = f32[9,384]{1,0:T(8,128)S(1)} collective-permute-done((f32[9,384]{1,0:T(8,128)}, f32[9,384]{1,0:T(8,128)S(1)}, u32[]{:S(2)}, u32[]{:S(2)}) %collective-permute-start.1) | collective-permute-done | bytes 13856 | tf_op jit(solution)/shard_map/ppermute | solution.py:486
  8.3 1.0 %copy-done = f32[8,9,4,384]{3,2,1,0:T(4,128)S(1)} copy-done((f32[8,9,4,384]{3,2,1,0:T(4,128)S(1)}, f32[8,9,4,384]{3,2,1,0:T(4,128)}, u32[]{:S(2)}) %copy-start) | copy-done | bytes 442392
  9.6 2.1 %collective-permute-start.5 = (f32[8,6,4,384]{3,2,1,0:T(4,128)S(1)}, f32[8,6,4,384]{3,2,1,0:T(4,128)S(1)}, u32[]{:S(2)}, u32[]{:S(2)}) collective-permute-start(f32[8,6,4,384]{3,2,1,0:T(4,128)S(1)} %get-tuple-element.36), channel_id=1, source_target_pairs={{0,2},{2,0},{1,3},{3,1},{4,6},{6,4},{5,7},{7,5},{8,10},{10,8},{9,1... | collective-permute-start | bytes 884744 | tf_op jit(solution)/shard_map/ppermute | solution.py:517
  11.7 1.2 %collective-permute-done.6.refs_3_ = f32[9,384]{1,0:T(8,128)S(1)} collective-permute-done((f32[9,384]{1,0:T(8,128)S(1)}, f32[9,384]{1,0:T(8,128)S(1)}, u32[]{:S(2)}, u32[]{:S(2)}) %collective-permute-start.6) | collective-permute-done | bytes 13856 | tf_op jit(solution)/shard_map/ppermute | solution.py:505
  12.9 0.8 %copy-done.1 = f32[24,384]{1,0:T(8,128)S(1)} copy-done((f32[24,384]{1,0:T(8,128)S(1)}, f32[24,384]{1,0:T(8,128)}, u32[]{:S(2)}) %copy-start.1) | copy-done | bytes 36888
  13.7 1.6 %collective-permute-start.7 = (f32[2,5,4,384]{3,2,1,0:T(4,128)S(1)}, f32[2,5,4,384]{3,2,1,0:T(4,128)S(1)}, u32[]{:S(2)}, u32[]{:S(2)}) collective-permute-start(f32[2,5,4,384]{3,2,1,0:T(4,128)S(1)} %payload.1.refs_0_), channel_id=1, source_target_pairs={{0,4},{4,0},{8,12},{12,8},{1,5},{5,1},{9,13},{13,9},{2,6},{6,2},{1... | collective-permute-start | bytes 184328 | tf_op jit(solution)/shard_map/ppermute | solution.py:528
  15.3 2.6 %collective-permute-start.8 = (f32[2,5,4,384]{3,2,1,0:T(4,128)S(1)}, f32[2,5,4,384]{3,2,1,0:T(4,128)S(1)}, u32[]{:S(2)}, u32[]{:S(2)}) collective-permute-start(f32[2,5,4,384]{3,2,1,0:T(4,128)S(1)} %payload.1.refs_0_), channel_id=1, source_target_pairs={{0,8},{4,12},{8,0},{12,4},{1,9},{5,13},{9,1},{13,5},{2,10},{6,14},... | collective-permute-start | bytes 184328 | tf_op jit(solution)/shard_map/ppermute | solution.py:528
  18.2 0.7 %collective-permute-start.3 = (f32[11,9,2,384]{3,2,1,0:T(2,128)S(1)}, f32[11,9,2,384]{3,2,1,0:T(2,128)S(1)}, u32[]{:S(2)}, u32[]{:S(2)}) collective-permute-start(f32[11,9,2,384]{3,2,1,0:T(2,128)S(1)} %get-tuple-element.34), channel_id=1, source_target_pairs={{0,4},{4,0},{8,12},{12,8},{1,5},{5,1},{9,13},{13,9},{2,6},{6,2},{1... | collective-permute-start | bytes 912392 | tf_op jit(solution)/shard_map/ppermute | solution.py:50
  18.8 0.7 %collective-permute-start.4 = (f32[11,9,2,384]{3,2,1,0:T(2,128)S(1)}, f32[11,9,2,384]{3,2,1,0:T(2,128)S(1)}, u32[]{:S(2)}, u32[]{:S(2)}) collective-permute-start(f32[11,9,2,384]{3,2,1,0:T(2,128)S(1)} %get-tuple-element.35), channel_id=1, source_target_pairs={{4,8},{8,4},{5,9},{9,5},{6,10},{10,6},{7,11},{11,7},{20,24},{24,20... | collective-permute-start | bytes 912392 | tf_op jit(solution)/shard_map/ppermute | solution.py:50
  19.5 2.6 %collective-permute-done.8.refs_2_ = f32[2,5,4,384]{3,2,1,0:T(4,128)S(1)} collective-permute-done((f32[2,5,4,384]{3,2,1,0:T(4,128)S(1)}, f32[2,5,4,384]{3,2,1,0:T(4,128)S(1)}, u32[]{:S(2)}, u32[]{:S(2)}) %collective-permute-start.8) | collective-permute-done | bytes 61472 | tf_op jit(solution)/shard_map/ppermute | solution.py:528
  22.1 2.6 %collective-permute-done.9.refs_3_ = f32[2,5,4,384]{3,2,1,0:T(4,128)S(1)} collective-permute-done((f32[2,5,4,384]{3,2,1,0:T(4,128)S(1)}, f32[2,5,4,384]{3,2,1,0:T(4,128)S(1)}, u32[]{:S(2)}, u32[]{:S(2)}) %collective-permute-start.9) | collective-permute-done | bytes 61472 | tf_op jit(solution)/shard_map/ppermute | solution.py:528
  24.7 1.7 %prepare.1 = (bf16[42,16,3072]{2,1,0:T(8,128)(2,1)S(1)}, bf16[384,3072]{1,0:T(8,128)(2,1)S(1)}, f32[8,3072]{1,0:T(8,128)S(1)}) custom-call(f32[2,5,4,384]{3,2,1,0:T(4,128)S(1)} %payload.1.refs_0_, f32[2,5,4,384]{3,2,1,0:T(4,128)S(1)} %collective-permute-done.7.refs_1_, f32[2,5,4,384]{3,2,1,0:T(4,128)S(1)} %collective-permute-done.8.refs_2_, ...), custom_call_target="tpu_custom_call" | custom-call | bytes 1048576 | tf_op jit(solution)/shard_map/prepare/pallas_call | solution.py:542
  26.8 0.8 %collective-permute-start.11 = (f32[11,6,2,384]{3,2,1,0:T(2,128)S(1)}, f32[11,6,2,384]{3,2,1,0:T(2,128)S(1)}, u32[]{:S(2)}, u32[]{:S(2)}) collective-permute-start(f32[11,6,2,384]{3,2,1,0:T(2,128)S(1)} %get-tuple-element.44), channel_id=1, source_target_pairs={{4,8},{8,4},{5,9},{9,5},{6,10},{10,6},{7,11},{11,7},{20,24},{24,20... | collective-permute-start | bytes 608264 | tf_op jit(solution)/shard_map/ppermute | solution.py:50
  27.6 6.1 %forcing0.1.refs_6_.refs_0_ = f32[4,3,15,8,384]{4,3,2,1,0:T(8,128)S(1)} custom-call(bf16[42,16,3072]{2,1,0:T(8,128)(2,1)S(1)} %get-tuple-element.45.refs_0_, bf16[384,3072]{1,0:T(8,128)(2,1)S(1)} %get-tuple-element.46.refs_1_, f32[8,3072]{1,0:T(8,128)S(1)} %get-tuple-element.47.refs_2_), custom_call_target="tpu_custom_call" | custom-call | flops 6341787648 | bytes 1048576 | tf_op jit(solution)/shard_map/forcing0/pallas_call | solution.py:574
  33.8 3.0 %round0.1 = (f32[3,17,8,384]{3,2,1,0:T(8,128)S(1)}, f32[6,17,8,384]{3,2,1,0:T(8,128)S(1)}, f32[3,8,384]{2,1,0:T(8,128)S(1)}, f32[5,12,2,384]{3,2,1,0:T(2,128)S(1)}, f32[5,12,2,384]{3,2,1,0:T(2,128)S(1)}) custom-call(f32[8,9,4,384]{3,2,1,0:T(4,128)S(1)} %get-tuple-element.33.refs_0_, f32[11,9,2,384]{3,2,1,0:T(2,128)S(1)} %collective-permute-done.3.refs_1_, ...), custom_call_target="tpu_custom_call" | custom-call | bytes 1048576 | tf_op jit(solution)/shard_map/round0/pallas_call | solution.py:596
  36.8 3.6 %collective-permute-start.12 = (f32[5,12,2,384]{3,2,1,0:T(2,128)S(1)}, f32[5,12,2,384]{3,2,1,0:T(2,128)S(1)}, u32[]{:S(2)}, u32[]{:S(2)}) collective-permute-start(f32[5,12,2,384]{3,2,1,0:T(2,128)S(1)} %get-tuple-element.50), channel_id=1, source_target_pairs={{0,4},{4,0},{8,12},{12,8},{1,5},{5,1},{9,13},{13,9},{2,6},{6,2},{1... | collective-permute-start | bytes 552968 | tf_op jit(solution)/shard_map/ppermute | solution.py:50
  40.4 0.8 %collective-permute-start.13 = (f32[5,12,2,384]{3,2,1,0:T(2,128)S(1)}, f32[5,12,2,384]{3,2,1,0:T(2,128)S(1)}, u32[]{:S(2)}, u32[]{:S(2)}) collective-permute-start(f32[5,12,2,384]{3,2,1,0:T(2,128)S(1)} %get-tuple-element.51), channel_id=1, source_target_pairs={{4,8},{8,4},{5,9},{9,5},{6,10},{10,6},{7,11},{11,7},{20,24},{24,20... | collective-permute-start | bytes 552968 | tf_op jit(solution)/shard_map/ppermute | solution.py:50
  41.2 3.4 %forcing3.1.refs_1_ = f32[2,3,15,8,384]{4,3,2,1,0:T(8,128)S(1)} custom-call(bf16[42,16,3072]{2,1,0:T(8,128)(2,1)S(1)} %get-tuple-element.45.refs_0_, bf16[384,3072]{1,0:T(8,128)(2,1)S(1)} %get-tuple-element.46.refs_1_, f32[8,3072]{1,0:T(8,128)S(1)} %get-tuple-element.47.refs_2_), custom_call_target="tpu_custom_call" | custom-call | flops 3170893824 | bytes 1048576 | tf_op jit(solution)/shard_map/forcing3/pallas_call | solution.py:574
  44.6 2.6 %round1.1 = (f32[3,9,4,360]{3,2,1,0:T(4,128)}, f32[3,2,360]{2,1,0:T(2,128)S(1)}, f32[3,2,360]{2,1,0:T(2,128)S(1)}) custom-call(f32[3,17,8,384]{3,2,1,0:T(8,128)S(1)} %get-tuple-element.48.state, f32[6,17,8,384]{3,2,1,0:T(8,128)S(1)} %get-tuple-element.49.coef, f32[5,12,2,384]{3,2,1,0:T(2,128)S(1)} %collective-permute-done.12.first, ...), custom_call_target="tpu_custom_call" | custom-call | bytes 1048576 | tf_op jit(solution)/shard_map/round1/pallas_call | solution.py:615
  47.2 0.5 %collective-permute-start.14 = (f32[3,2,360]{2,1,0:T(2,128)S(1)}, f32[3,2,360]{2,1,0:T(2,128)S(1)}, u32[]{:S(2)}, u32[]{:S(2)}) collective-permute-start(f32[3,2,360]{2,1,0:T(2,128)S(1)} %get-tuple-element.55), channel_id=1, source_target_pairs={{0,2},{2,0},{1,3},{3,1},{4,6},{6,4},{5,7},{7,5},{8,10},{10,8},{9,1... | collective-permute-start | bytes 25928 | tf_op jit(solution)/shard_map/ppermute | solution.py:628
  47.7 3.1 %collective-permute-done.14 = f32[3,2,360]{2,1,0:T(2,128)S(1)} collective-permute-done((f32[3,2,360]{2,1,0:T(2,128)S(1)}, f32[3,2,360]{2,1,0:T(2,128)S(1)}, u32[]{:S(2)}, u32[]{:S(2)}) %collective-permute-start.14) | collective-permute-done | bytes 8672 | tf_op jit(solution)/shard_map/ppermute | solution.py:628
  50.9 0.6 %add.3 = f32[3,2,360]{2,1,0:T(2,128)} add(f32[3,2,360]{2,1,0:T(2,128)S(1)} %get-tuple-element.54, f32[3,2,360]{2,1,0:T(2,128)S(1)} %collective-permute-done.14) | non-fusion elementwise | flops 2160 | bytes 25920 | tf_op jit(solution)/shard_map/add | solution.py:628
  (22 shorter events, 1.5 us)
Async XLA Ops:
  2.8 5.5 %collective-permute-start = (f32[8,9,4,128]{3,2,1,0:T(4,128)}, f32[8,9,4,128]{3,2,1,0:T(4,128)S(1)}, u32[]{:S(2)}, u32[]{:S(2)}) collective-permute-start(f32[8,9,4,128]{3,2,1,0:T(4,128)} %get-tuple-element.30), channel_id=1, source_target_pairs={{0,1},{1,0},{2,3},{3,2},{4,5},{5,4},{6,7},{7,6},{8,9},{9,8},{10,11... | collective-permute-start | bytes 442376 | tf_op jit(solution)/shard_map/ppermute | solution.py:502
  3.3 5.0 %collective-permute-start.2 = (f32[24,384]{1,0:T(8,128)}, f32[24,384]{1,0:T(8,128)S(1)}, u32[]{:S(2)}, u32[]{:S(2)}) collective-permute-start(f32[24,384]{1,0:T(8,128)} %get-tuple-element.31.refs_0_), channel_id=1, source_target_pairs={{0,1},{1,0},{2,3},{3,2},{4,5},{5,4},{6,7},{7,6},{8,9},{9,8},{10,11... | collective-permute-start | bytes 110600 | tf_op jit(solution)/shard_map/ppermute | solution.py:503
  3.4 4.9 %collective-permute-start.1 = (f32[9,384]{1,0:T(8,128)}, f32[9,384]{1,0:T(8,128)S(1)}, u32[]{:S(2)}, u32[]{:S(2)}) collective-permute-start(f32[9,384]{1,0:T(8,128)} %refs_6_.1), channel_id=1, source_target_pairs={{0,2},{2,0},{1,3},{3,1},{4,6},{6,4},{5,7},{7,5},{8,10},{10,8},{9,1... | collective-permute-start | bytes 41480 | tf_op jit(solution)/shard_map/ppermute | solution.py:486
  8.3 1.0 %copy-start = (f32[8,9,4,384]{3,2,1,0:T(4,128)S(1)}, f32[8,9,4,384]{3,2,1,0:T(4,128)}, u32[]{:S(2)}) copy-start(f32[8,9,4,384]{3,2,1,0:T(4,128)} %get-tuple-element.29.own) | copy-start | bytes 1327108
  9.6 16.8 %collective-permute-start.5 = (f32[8,6,4,384]{3,2,1,0:T(4,128)S(1)}, f32[8,6,4,384]{3,2,1,0:T(4,128)S(1)}, u32[]{:S(2)}, u32[]{:S(2)}) collective-permute-start(f32[8,6,4,384]{3,2,1,0:T(4,128)S(1)} %get-tuple-element.36), channel_id=1, source_target_pairs={{0,2},{2,0},{1,3},{3,1},{4,6},{6,4},{5,7},{7,5},{8,10},{10,8},{9,1... | collective-permute-start | bytes 884744 | tf_op jit(solution)/shard_map/ppermute | solution.py:517
  11.7 1.2 %collective-permute-start.6 = (f32[9,384]{1,0:T(8,128)S(1)}, f32[9,384]{1,0:T(8,128)S(1)}, u32[]{:S(2)}, u32[]{:S(2)}) collective-permute-start(f32[9,384]{1,0:T(8,128)S(1)} %collective-permute-done.1.refs_1_), channel_id=1, source_target_pairs={{0,1},{1,0},{2,3},{3,2},{4,5},{5,4},{6,7},{7,6},{8,9},{9,8},{10,11... | collective-permute-start | bytes 41480 | tf_op jit(solution)/shard_map/ppermute | solution.py:505
  12.9 0.8 %copy-start.1 = (f32[24,384]{1,0:T(8,128)S(1)}, f32[24,384]{1,0:T(8,128)}, u32[]{:S(2)}) copy-start(f32[24,384]{1,0:T(8,128)} %get-tuple-element.31.refs_0_) | copy-start | bytes 110596
  13.7 5.1 %collective-permute-start.7 = (f32[2,5,4,384]{3,2,1,0:T(4,128)S(1)}, f32[2,5,4,384]{3,2,1,0:T(4,128)S(1)}, u32[]{:S(2)}, u32[]{:S(2)}) collective-permute-start(f32[2,5,4,384]{3,2,1,0:T(4,128)S(1)} %payload.1.refs_0_), channel_id=1, source_target_pairs={{0,4},{4,0},{8,12},{12,8},{1,5},{5,1},{9,13},{13,9},{2,6},{6,2},{1... | collective-permute-start | bytes 184328 | tf_op jit(solution)/shard_map/ppermute | solution.py:528
  15.3 6.7 %collective-permute-start.8 = (f32[2,5,4,384]{3,2,1,0:T(4,128)S(1)}, f32[2,5,4,384]{3,2,1,0:T(4,128)S(1)}, u32[]{:S(2)}, u32[]{:S(2)}) collective-permute-start(f32[2,5,4,384]{3,2,1,0:T(4,128)S(1)} %payload.1.refs_0_), channel_id=1, source_target_pairs={{0,8},{4,12},{8,0},{12,4},{1,9},{5,13},{9,1},{13,5},{2,10},{6,14},... | collective-permute-start | bytes 184328 | tf_op jit(solution)/shard_map/ppermute | solution.py:528
  17.9 6.7 %collective-permute-start.9 = (f32[2,5,4,384]{3,2,1,0:T(4,128)S(1)}, f32[2,5,4,384]{3,2,1,0:T(4,128)S(1)}, u32[]{:S(2)}, u32[]{:S(2)}) collective-permute-start(f32[2,5,4,384]{3,2,1,0:T(4,128)S(1)} %payload.1.refs_0_), channel_id=1, source_target_pairs={{0,12},{4,8},{8,4},{12,0},{1,13},{5,9},{9,5},{13,1},{2,14},{6,10},... | collective-permute-start | bytes 184328 | tf_op jit(solution)/shard_map/ppermute | solution.py:528
  18.2 15.5 %collective-permute-start.3 = (f32[11,9,2,384]{3,2,1,0:T(2,128)S(1)}, f32[11,9,2,384]{3,2,1,0:T(2,128)S(1)}, u32[]{:S(2)}, u32[]{:S(2)}) collective-permute-start(f32[11,9,2,384]{3,2,1,0:T(2,128)S(1)} %get-tuple-element.34), channel_id=1, source_target_pairs={{0,4},{4,0},{8,12},{12,8},{1,5},{5,1},{9,13},{13,9},{2,6},{6,2},{1... | collective-permute-start | bytes 912392 | tf_op jit(solution)/shard_map/ppermute | solution.py:50
  18.8 14.9 %collective-permute-start.4 = (f32[11,9,2,384]{3,2,1,0:T(2,128)S(1)}, f32[11,9,2,384]{3,2,1,0:T(2,128)S(1)}, u32[]{:S(2)}, u32[]{:S(2)}) collective-permute-start(f32[11,9,2,384]{3,2,1,0:T(2,128)S(1)} %get-tuple-element.35), channel_id=1, source_target_pairs={{4,8},{8,4},{5,9},{9,5},{6,10},{10,6},{7,11},{11,7},{20,24},{24,20... | collective-permute-start | bytes 912392 | tf_op jit(solution)/shard_map/ppermute | solution.py:50
  26.6 7.2 %collective-permute-start.10 = (f32[11,6,2,384]{3,2,1,0:T(2,128)S(1)}, f32[11,6,2,384]{3,2,1,0:T(2,128)S(1)}, u32[]{:S(2)}, u32[]{:S(2)}) collective-permute-start(f32[11,6,2,384]{3,2,1,0:T(2,128)S(1)} %get-tuple-element.43), channel_id=1, source_target_pairs={{0,4},{4,0},{8,12},{12,8},{1,5},{5,1},{9,13},{13,9},{2,6},{6,2},{1... | collective-permute-start | bytes 608264 | tf_op jit(solution)/shard_map/ppermute | solution.py:50
  26.8 7.0 %copy-start.2 = (f32[9]{0:T(128)S(1)}, f32[9]{0:T(128)}, u32[]{:S(2)}) copy-start(f32[9]{0:T(128)} %refs_2_.3) | copy-start | bytes 112
  26.8 6.9 %collective-permute-start.11 = (f32[11,6,2,384]{3,2,1,0:T(2,128)S(1)}, f32[11,6,2,384]{3,2,1,0:T(2,128)S(1)}, u32[]{:S(2)}, u32[]{:S(2)}) collective-permute-start(f32[11,6,2,384]{3,2,1,0:T(2,128)S(1)} %get-tuple-element.44), channel_id=1, source_target_pairs={{4,8},{8,4},{5,9},{9,5},{6,10},{10,6},{7,11},{11,7},{20,24},{24,20... | collective-permute-start | bytes 608264 | tf_op jit(solution)/shard_map/ppermute | solution.py:50
  36.8 7.8 %collective-permute-start.12 = (f32[5,12,2,384]{3,2,1,0:T(2,128)S(1)}, f32[5,12,2,384]{3,2,1,0:T(2,128)S(1)}, u32[]{:S(2)}, u32[]{:S(2)}) collective-permute-start(f32[5,12,2,384]{3,2,1,0:T(2,128)S(1)} %get-tuple-element.50), channel_id=1, source_target_pairs={{0,4},{4,0},{8,12},{12,8},{1,5},{5,1},{9,13},{13,9},{2,6},{6,2},{1... | collective-permute-start | bytes 552968 | tf_op jit(solution)/shard_map/ppermute | solution.py:50
  40.4 4.2 %collective-permute-start.13 = (f32[5,12,2,384]{3,2,1,0:T(2,128)S(1)}, f32[5,12,2,384]{3,2,1,0:T(2,128)S(1)}, u32[]{:S(2)}, u32[]{:S(2)}) collective-permute-start(f32[5,12,2,384]{3,2,1,0:T(2,128)S(1)} %get-tuple-element.51), channel_id=1, source_target_pairs={{4,8},{8,4},{5,9},{9,5},{6,10},{10,6},{7,11},{11,7},{20,24},{24,20... | collective-permute-start | bytes 552968 | tf_op jit(solution)/shard_map/ppermute | solution.py:50
  47.2 3.7 %collective-permute-start.14 = (f32[3,2,360]{2,1,0:T(2,128)S(1)}, f32[3,2,360]{2,1,0:T(2,128)S(1)}, u32[]{:S(2)}, u32[]{:S(2)}) collective-permute-start(f32[3,2,360]{2,1,0:T(2,128)S(1)} %get-tuple-element.55), channel_id=1, source_target_pairs={{0,2},{2,0},{1,3},{3,1},{4,6},{6,4},{5,7},{7,5},{8,10},{10,8},{9,1... | collective-permute-start | bytes 25928 | tf_op jit(solution)/shard_map/ppermute | solution.py:628

commit v7 on v6

--- a/solution.py
+++ b/solution.py
@@ -212,20 +212,23 @@
         east, west, north, south = (coef[c, at + 1] for c in range(1, 5))
         if outer is not None:
             up_outer, down_outer = coef[5, at + 1], coef[5, at]
+            stay_outer = 1.0 - up_outer - down_outer
+        stay = 1.0 - up - down
+        keep = 1.0 - east - west - north - south
         own_id = at - own
         inside = (own_id >= 0) & (own_id < levels)
         weight = jnp.where(inside, profile[jnp.clip(own_id, 0, levels - 1)], 0.0)
         for t in range(tracers):
             a = src[t, at + 1]
-            b = a + up * (src[t, at + 2] - a) + down * (src[t, at] - a)
-            moved = b + east * (pltpu.roll(b, lanes - 1, 1) - b) + west * (pltpu.roll(b, 1, 1) - b)
+            b = stay * a + up * src[t, at + 2] + down * src[t, at]
+            moved = keep * b + east * pltpu.roll(b, lanes - 1, 1) + west * pltpu.roll(b, 1, 1)
             above, below = pltpu.roll(b, 7, 0), pltpu.roll(b, 1, 0)
             if outer is not None:
                 a = outer[t, at + 1]
-                b_outer = a + up_outer * (outer[t, at + 2] - a) + down_outer * (outer[t, at] - a)
+                b_outer = stay_outer * a + up_outer * outer[t, at + 2] + down_outer * outer[t, at]
                 above = jnp.where(ids == 5, b_outer, above)
                 below = jnp.where(ids == 6, b_outer, below)
-            moved = moved + north * (above - b) + south * (below - b)
+            moved = moved + north * above + south * below
             new = moved + force[index, t, at]
             dst[t, at + 1] = new
             total[t] = total[t] + weight * new
@@ -475,7 +478,7 @@
     def call(body, limit, flops=0, **kwargs):
         return pl.pallas_call(
             body,
-            compiler_params=pltpu.CompilerParams(vmem_limit_bytes=limit * MIB),
+            compiler_params=pltpu.CompilerParams(vmem_limit_bytes=int(limit * MIB)),
             cost_estimate=pl.CostEstimate(flops=flops, bytes_accessed=MIB, transcendentals=0),
             **kwargs,
         )

time: 52 us -> 51.9 us (level)
  no operation moved by 1% of the time
where the time goes in v7:
time: 51.9 us; the launch traced here: 51.4 us
  Pallas kernels  19.3 us (37%)
  starting transfers between devices  17.3 us (33%)
  waiting for transfers between devices  11.5 us (22%)
  local copies, waits for them, and re-layouts  1.78 us (3%)
  between operations  0.78 us (2%)
  other arithmetic  0.6 us (1%)
    pallas_call x2, Pallas kernels, forcing_of(): call(functools.partial(forcing_kernel, steps, *sizes), limit, flops=2 * l...  9.47 us
    ppermute x6, starting transfers between devices, swap_tiles(): return lax.ppermute(value, 'tiles', pairs)  6.75 us
    ppermute x3, waiting for transfers between devices, per_device(): lax.ppermute(both, 'tiles', [(i, i ^ k) for i in range(tiles)])  5.15 us
    ppermute x3, starting transfers between devices, per_device(): lax.ppermute(both, 'tiles', [(i, i ^ k) for i in range(tiles)])  4.45 us
    ppermute x1, waiting for transfers between devices, per_device(): flux_gradient = keep + lax.ppermute(give, 'levels', [(0, 1), (1, 0)])  3.14 us
    pallas_call x1, Pallas kernels, per_device(): call(functools.partial(first_kernel, moves, levels), 16, out_shape=[shape...  3 us
    ppermute x1, starting transfers between devices, per_device(): lax.ppermute(averaging_kernel, 'levels', pairs)  2.92 us
    pallas_call x1, Pallas kernels, per_device(): call(functools.partial(next_kernel, round_id, levels, rows), 16, out_shap...  2.53 us
  transfers between devices with their start and end apart: 15, of which 5 were waited for; matrix products, arithmetic and copies ran while one was open for 0% of the time, Pallas kernels for 22%

profile of v7, /device:TPU:0, one launch (start us, length us, event | category | flops | bytes accessed | tf_op | source)
XLA Modules:
  0.0 51.4 jit_solution(7145357502538276653)
XLA Ops:
  0.6 2.1 %edges.1 = (f32[8,9,4,384]{3,2,1,0:T(4,128)}, f32[8,9,4,128]{3,2,1,0:T(4,128)}, f32[24,384]{1,0:T(8,128)}) custom-call(f32[3,9,4,360]{3,2,1,0:T(4,128)} %refs_0_.1, f32[9,4,360]{2,1,0:T(4,128)} %refs_1_.1, f32[9,4,360]{2,1,0:T(4,128)} %refs_2_.2, s32[2,9,4,360]{3,2,1,0:T(4,128)} %refs_3_.1, f32[9,4,360]{2,1,0:T(4,128)} %refs_4_.1, f32[3,384]{1,0:T(4,128)} %refs_5_.1, ...), custom_call_target="tpu_custom_call" | custom-call | bytes 1048576 | tf_op jit(solution)/shard_map/edges/pallas_call | solution.py:494
  2.8 0.5 %collective-permute-start = (f32[8,9,4,128]{3,2,1,0:T(4,128)}, f32[8,9,4,128]{3,2,1,0:T(4,128)S(1)}, u32[]{:S(2)}, u32[]{:S(2)}) collective-permute-start(f32[8,9,4,128]{3,2,1,0:T(4,128)} %get-tuple-element.30), channel_id=1, source_target_pairs={{0,1},{1,0},{2,3},{3,2},{4,5},{5,4},{6,7},{7,6},{8,9},{9,8},{10,11... | collective-permute-start | bytes 442376 | tf_op jit(solution)/shard_map/ppermute | solution.py:505
  3.4 2.9 %collective-permute-start.1 = (f32[9,384]{1,0:T(8,128)}, f32[9,384]{1,0:T(8,128)S(1)}, u32[]{:S(2)}, u32[]{:S(2)}) collective-permute-start(f32[9,384]{1,0:T(8,128)} %refs_6_.1), channel_id=1, source_target_pairs={{0,2},{2,0},{1,3},{3,1},{4,6},{6,4},{5,7},{7,5},{8,10},{10,8},{9,1... | collective-permute-start | bytes 41480 | tf_op jit(solution)/shard_map/ppermute | solution.py:489
  6.3 2.0 %collective-permute-done.1.refs_1_ = f32[9,384]{1,0:T(8,128)S(1)} collective-permute-done((f32[9,384]{1,0:T(8,128)}, f32[9,384]{1,0:T(8,128)S(1)}, u32[]{:S(2)}, u32[]{:S(2)}) %collective-permute-start.1) | collective-permute-done | bytes 13856 | tf_op jit(solution)/shard_map/ppermute | solution.py:489
  8.3 1.0 %copy-done = f32[8,9,4,384]{3,2,1,0:T(4,128)S(1)} copy-done((f32[8,9,4,384]{3,2,1,0:T(4,128)S(1)}, f32[8,9,4,384]{3,2,1,0:T(4,128)}, u32[]{:S(2)}) %copy-start) | copy-done | bytes 442392
  9.6 2.1 %collective-permute-start.5 = (f32[8,6,4,384]{3,2,1,0:T(4,128)S(1)}, f32[8,6,4,384]{3,2,1,0:T(4,128)S(1)}, u32[]{:S(2)}, u32[]{:S(2)}) collective-permute-start(f32[8,6,4,384]{3,2,1,0:T(4,128)S(1)} %get-tuple-element.36), channel_id=1, source_target_pairs={{0,2},{2,0},{1,3},{3,1},{4,6},{6,4},{5,7},{7,5},{8,10},{10,8},{9,1... | collective-permute-start | bytes 884744 | tf_op jit(solution)/shard_map/ppermute | solution.py:520
  11.7 1.2 %collective-permute-done.6.refs_3_ = f32[9,384]{1,0:T(8,128)S(1)} collective-permute-done((f32[9,384]{1,0:T(8,128)S(1)}, f32[9,384]{1,0:T(8,128)S(1)}, u32[]{:S(2)}, u32[]{:S(2)}) %collective-permute-start.6) | collective-permute-done | bytes 13856 | tf_op jit(solution)/shard_map/ppermute | solution.py:508
  12.9 0.8 %copy-done.1 = f32[24,384]{1,0:T(8,128)S(1)} copy-done((f32[24,384]{1,0:T(8,128)S(1)}, f32[24,384]{1,0:T(8,128)}, u32[]{:S(2)}) %copy-start.1) | copy-done | bytes 36888
  13.7 1.6 %collective-permute-start.7 = (f32[2,5,4,384]{3,2,1,0:T(4,128)S(1)}, f32[2,5,4,384]{3,2,1,0:T(4,128)S(1)}, u32[]{:S(2)}, u32[]{:S(2)}) collective-permute-start(f32[2,5,4,384]{3,2,1,0:T(4,128)S(1)} %payload.1.refs_0_), channel_id=1, source_target_pairs={{0,4},{4,0},{8,12},{12,8},{1,5},{5,1},{9,13},{13,9},{2,6},{6,2},{1... | collective-permute-start | bytes 184328 | tf_op jit(solution)/shard_map/ppermute | solution.py:531
  15.3 2.6 %collective-permute-start.8 = (f32[2,5,4,384]{3,2,1,0:T(4,128)S(1)}, f32[2,5,4,384]{3,2,1,0:T(4,128)S(1)}, u32[]{:S(2)}, u32[]{:S(2)}) collective-permute-start(f32[2,5,4,384]{3,2,1,0:T(4,128)S(1)} %payload.1.refs_0_), channel_id=1, source_target_pairs={{0,8},{4,12},{8,0},{12,4},{1,9},{5,13},{9,1},{13,5},{2,10},{6,14},... | collective-permute-start | bytes 184328 | tf_op jit(solution)/shard_map/ppermute | solution.py:531
  18.2 0.7 %collective-permute-start.3 = (f32[11,9,2,384]{3,2,1,0:T(2,128)S(1)}, f32[11,9,2,384]{3,2,1,0:T(2,128)S(1)}, u32[]{:S(2)}, u32[]{:S(2)}) collective-permute-start(f32[11,9,2,384]{3,2,1,0:T(2,128)S(1)} %get-tuple-element.34), channel_id=1, source_target_pairs={{0,4},{4,0},{8,12},{12,8},{1,5},{5,1},{9,13},{13,9},{2,6},{6,2},{1... | collective-permute-start | bytes 912392 | tf_op jit(solution)/shard_map/ppermute | solution.py:50
  18.8 0.7 %collective-permute-start.4 = (f32[11,9,2,384]{3,2,1,0:T(2,128)S(1)}, f32[11,9,2,384]{3,2,1,0:T(2,128)S(1)}, u32[]{:S(2)}, u32[]{:S(2)}) collective-permute-start(f32[11,9,2,384]{3,2,1,0:T(2,128)S(1)} %get-tuple-element.35), channel_id=1, source_target_pairs={{4,8},{8,4},{5,9},{9,5},{6,10},{10,6},{7,11},{11,7},{20,24},{24,20... | collective-permute-start | bytes 912392 | tf_op jit(solution)/shard_map/ppermute | solution.py:50
  19.5 2.6 %collective-permute-done.8.refs_2_ = f32[2,5,4,384]{3,2,1,0:T(4,128)S(1)} collective-permute-done((f32[2,5,4,384]{3,2,1,0:T(4,128)S(1)}, f32[2,5,4,384]{3,2,1,0:T(4,128)S(1)}, u32[]{:S(2)}, u32[]{:S(2)}) %collective-permute-start.8) | collective-permute-done | bytes 61472 | tf_op jit(solution)/shard_map/ppermute | solution.py:531
  22.1 2.6 %collective-permute-done.9.refs_3_ = f32[2,5,4,384]{3,2,1,0:T(4,128)S(1)} collective-permute-done((f32[2,5,4,384]{3,2,1,0:T(4,128)S(1)}, f32[2,5,4,384]{3,2,1,0:T(4,128)S(1)}, u32[]{:S(2)}, u32[]{:S(2)}) %collective-permute-start.9) | collective-permute-done | bytes 61472 | tf_op jit(solution)/shard_map/ppermute | solution.py:531
  24.7 1.7 %prepare.1 = (bf16[42,16,3072]{2,1,0:T(8,128)(2,1)S(1)}, bf16[384,3072]{1,0:T(8,128)(2,1)S(1)}, f32[8,3072]{1,0:T(8,128)S(1)}) custom-call(f32[2,5,4,384]{3,2,1,0:T(4,128)S(1)} %payload.1.refs_0_, f32[2,5,4,384]{3,2,1,0:T(4,128)S(1)} %collective-permute-done.7.refs_1_, f32[2,5,4,384]{3,2,1,0:T(4,128)S(1)} %collective-permute-done.8.refs_2_, ...), custom_call_target="tpu_custom_call" | custom-call | bytes 1048576 | tf_op jit(solution)/shard_map/prepare/pallas_call | solution.py:545
  26.8 0.8 %collective-permute-start.11 = (f32[11,6,2,384]{3,2,1,0:T(2,128)S(1)}, f32[11,6,2,384]{3,2,1,0:T(2,128)S(1)}, u32[]{:S(2)}, u32[]{:S(2)}) collective-permute-start(f32[11,6,2,384]{3,2,1,0:T(2,128)S(1)} %get-tuple-element.44), channel_id=1, source_target_pairs={{4,8},{8,4},{5,9},{9,5},{6,10},{10,6},{7,11},{11,7},{20,24},{24,20... | collective-permute-start | bytes 608264 | tf_op jit(solution)/shard_map/ppermute | solution.py:50
  27.6 6.1 %forcing0.1.refs_6_.refs_0_ = f32[4,3,15,8,384]{4,3,2,1,0:T(8,128)S(1)} custom-call(bf16[42,16,3072]{2,1,0:T(8,128)(2,1)S(1)} %get-tuple-element.45.refs_0_, bf16[384,3072]{1,0:T(8,128)(2,1)S(1)} %get-tuple-element.46.refs_1_, f32[8,3072]{1,0:T(8,128)S(1)} %get-tuple-element.47.refs_2_), custom_call_target="tpu_custom_call" | custom-call | flops 6341787648 | bytes 1048576 | tf_op jit(solution)/shard_map/forcing0/pallas_call | solution.py:577
  33.8 3.0 %round0.1 = (f32[3,17,8,384]{3,2,1,0:T(8,128)S(1)}, f32[6,17,8,384]{3,2,1,0:T(8,128)S(1)}, f32[3,8,384]{2,1,0:T(8,128)S(1)}, f32[5,12,2,384]{3,2,1,0:T(2,128)S(1)}, f32[5,12,2,384]{3,2,1,0:T(2,128)S(1)}) custom-call(f32[8,9,4,384]{3,2,1,0:T(4,128)S(1)} %get-tuple-element.33.refs_0_, f32[11,9,2,384]{3,2,1,0:T(2,128)S(1)} %collective-permute-done.3.refs_1_, ...), custom_call_target="tpu_custom_call" | custom-call | bytes 1048576 | tf_op jit(solution)/shard_map/round0/pallas_call | solution.py:599
  36.8 3.6 %collective-permute-start.12 = (f32[5,12,2,384]{3,2,1,0:T(2,128)S(1)}, f32[5,12,2,384]{3,2,1,0:T(2,128)S(1)}, u32[]{:S(2)}, u32[]{:S(2)}) collective-permute-start(f32[5,12,2,384]{3,2,1,0:T(2,128)S(1)} %get-tuple-element.50), channel_id=1, source_target_pairs={{0,4},{4,0},{8,12},{12,8},{1,5},{5,1},{9,13},{13,9},{2,6},{6,2},{1... | collective-permute-start | bytes 552968 | tf_op jit(solution)/shard_map/ppermute | solution.py:50
  40.3 0.8 %collective-permute-start.13 = (f32[5,12,2,384]{3,2,1,0:T(2,128)S(1)}, f32[5,12,2,384]{3,2,1,0:T(2,128)S(1)}, u32[]{:S(2)}, u32[]{:S(2)}) collective-permute-start(f32[5,12,2,384]{3,2,1,0:T(2,128)S(1)} %get-tuple-element.51), channel_id=1, source_target_pairs={{4,8},{8,4},{5,9},{9,5},{6,10},{10,6},{7,11},{11,7},{20,24},{24,20... | collective-permute-start | bytes 552968 | tf_op jit(solution)/shard_map/ppermute | solution.py:50
  41.2 3.4 %forcing3.1.refs_1_ = f32[2,3,15,8,384]{4,3,2,1,0:T(8,128)S(1)} custom-call(bf16[42,16,3072]{2,1,0:T(8,128)(2,1)S(1)} %get-tuple-element.45.refs_0_, bf16[384,3072]{1,0:T(8,128)(2,1)S(1)} %get-tuple-element.46.refs_1_, f32[8,3072]{1,0:T(8,128)S(1)} %get-tuple-element.47.refs_2_), custom_call_target="tpu_custom_call" | custom-call | flops 3170893824 | bytes 1048576 | tf_op jit(solution)/shard_map/forcing3/pallas_call | solution.py:577
  44.6 2.5 %round1.1 = (f32[3,9,4,360]{3,2,1,0:T(4,128)}, f32[3,2,360]{2,1,0:T(2,128)S(1)}, f32[3,2,360]{2,1,0:T(2,128)S(1)}) custom-call(f32[3,17,8,384]{3,2,1,0:T(8,128)S(1)} %get-tuple-element.48.state, f32[6,17,8,384]{3,2,1,0:T(8,128)S(1)} %get-tuple-element.49.coef, f32[5,12,2,384]{3,2,1,0:T(2,128)S(1)} %collective-permute-done.12.first, ...), custom_call_target="tpu_custom_call" | custom-call | bytes 1048576 | tf_op jit(solution)/shard_map/round1/pallas_call | solution.py:618
  47.6 3.1 %collective-permute-done.14 = f32[3,2,360]{2,1,0:T(2,128)S(1)} collective-permute-done((f32[3,2,360]{2,1,0:T(2,128)S(1)}, f32[3,2,360]{2,1,0:T(2,128)S(1)}, u32[]{:S(2)}, u32[]{:S(2)}) %collective-permute-start.14) | collective-permute-done | bytes 8672 | tf_op jit(solution)/shard_map/ppermute | solution.py:631
  50.7 0.6 %add.3 = f32[3,2,360]{2,1,0:T(2,128)} add(f32[3,2,360]{2,1,0:T(2,128)S(1)} %get-tuple-element.54, f32[3,2,360]{2,1,0:T(2,128)S(1)} %collective-permute-done.14) | non-fusion elementwise | flops 2160 | bytes 25920 | tf_op jit(solution)/shard_map/add | solution.py:631
  (22 shorter events, 1.5 us)
Async XLA Ops:
  2.8 5.5 %collective-permute-start = (f32[8,9,4,128]{3,2,1,0:T(4,128)}, f32[8,9,4,128]{3,2,1,0:T(4,128)S(1)}, u32[]{:S(2)}, u32[]{:S(2)}) collective-permute-start(f32[8,9,4,128]{3,2,1,0:T(4,128)} %get-tuple-element.30), channel_id=1, source_target_pairs={{0,1},{1,0},{2,3},{3,2},{4,5},{5,4},{6,7},{7,6},{8,9},{9,8},{10,11... | collective-permute-start | bytes 442376 | tf_op jit(solution)/shard_map/ppermute | solution.py:505
  3.3 5.0 %collective-permute-start.2 = (f32[24,384]{1,0:T(8,128)}, f32[24,384]{1,0:T(8,128)S(1)}, u32[]{:S(2)}, u32[]{:S(2)}) collective-permute-start(f32[24,384]{1,0:T(8,128)} %get-tuple-element.31.refs_0_), channel_id=1, source_target_pairs={{0,1},{1,0},{2,3},{3,2},{4,5},{5,4},{6,7},{7,6},{8,9},{9,8},{10,11... | collective-permute-start | bytes 110600 | tf_op jit(solution)/shard_map/ppermute | solution.py:506
  3.4 4.9 %collective-permute-start.1 = (f32[9,384]{1,0:T(8,128)}, f32[9,384]{1,0:T(8,128)S(1)}, u32[]{:S(2)}, u32[]{:S(2)}) collective-permute-start(f32[9,384]{1,0:T(8,128)} %refs_6_.1), channel_id=1, source_target_pairs={{0,2},{2,0},{1,3},{3,1},{4,6},{6,4},{5,7},{7,5},{8,10},{10,8},{9,1... | collective-permute-start | bytes 41480 | tf_op jit(solution)/shard_map/ppermute | solution.py:489
  8.3 1.0 %copy-start = (f32[8,9,4,384]{3,2,1,0:T(4,128)S(1)}, f32[8,9,4,384]{3,2,1,0:T(4,128)}, u32[]{:S(2)}) copy-start(f32[8,9,4,384]{3,2,1,0:T(4,128)} %get-tuple-element.29.own) | copy-start | bytes 1327108
  9.6 16.8 %collective-permute-start.5 = (f32[8,6,4,384]{3,2,1,0:T(4,128)S(1)}, f32[8,6,4,384]{3,2,1,0:T(4,128)S(1)}, u32[]{:S(2)}, u32[]{:S(2)}) collective-permute-start(f32[8,6,4,384]{3,2,1,0:T(4,128)S(1)} %get-tuple-element.36), channel_id=1, source_target_pairs={{0,2},{2,0},{1,3},{3,1},{4,6},{6,4},{5,7},{7,5},{8,10},{10,8},{9,1... | collective-permute-start | bytes 884744 | tf_op jit(solution)/shard_map/ppermute | solution.py:520
  11.7 1.2 %collective-permute-start.6 = (f32[9,384]{1,0:T(8,128)S(1)}, f32[9,384]{1,0:T(8,128)S(1)}, u32[]{:S(2)}, u32[]{:S(2)}) collective-permute-start(f32[9,384]{1,0:T(8,128)S(1)} %collective-permute-done.1.refs_1_), channel_id=1, source_target_pairs={{0,1},{1,0},{2,3},{3,2},{4,5},{5,4},{6,7},{7,6},{8,9},{9,8},{10,11... | collective-permute-start | bytes 41480 | tf_op jit(solution)/shard_map/ppermute | solution.py:508
  12.9 0.8 %copy-start.1 = (f32[24,384]{1,0:T(8,128)S(1)}, f32[24,384]{1,0:T(8,128)}, u32[]{:S(2)}) copy-start(f32[24,384]{1,0:T(8,128)} %get-tuple-element.31.refs_0_) | copy-start | bytes 110596
  13.7 5.1 %collective-permute-start.7 = (f32[2,5,4,384]{3,2,1,0:T(4,128)S(1)}, f32[2,5,4,384]{3,2,1,0:T(4,128)S(1)}, u32[]{:S(2)}, u32[]{:S(2)}) collective-permute-start(f32[2,5,4,384]{3,2,1,0:T(4,128)S(1)} %payload.1.refs_0_), channel_id=1, source_target_pairs={{0,4},{4,0},{8,12},{12,8},{1,5},{5,1},{9,13},{13,9},{2,6},{6,2},{1... | collective-permute-start | bytes 184328 | tf_op jit(solution)/shard_map/ppermute | solution.py:531
  15.3 6.7 %collective-permute-start.8 = (f32[2,5,4,384]{3,2,1,0:T(4,128)S(1)}, f32[2,5,4,384]{3,2,1,0:T(4,128)S(1)}, u32[]{:S(2)}, u32[]{:S(2)}) collective-permute-start(f32[2,5,4,384]{3,2,1,0:T(4,128)S(1)} %payload.1.refs_0_), channel_id=1, source_target_pairs={{0,8},{4,12},{8,0},{12,4},{1,9},{5,13},{9,1},{13,5},{2,10},{6,14},... | collective-permute-start | bytes 184328 | tf_op jit(solution)/shard_map/ppermute | solution.py:531
  17.9 6.7 %collective-permute-start.9 = (f32[2,5,4,384]{3,2,1,0:T(4,128)S(1)}, f32[2,5,4,384]{3,2,1,0:T(4,128)S(1)}, u32[]{:S(2)}, u32[]{:S(2)}) collective-permute-start(f32[2,5,4,384]{3,2,1,0:T(4,128)S(1)} %payload.1.refs_0_), channel_id=1, source_target_pairs={{0,12},{4,8},{8,4},{12,0},{1,13},{5,9},{9,5},{13,1},{2,14},{6,10},... | collective-permute-start | bytes 184328 | tf_op jit(solution)/shard_map/ppermute | solution.py:531
  18.2 15.5 %collective-permute-start.3 = (f32[11,9,2,384]{3,2,1,0:T(2,128)S(1)}, f32[11,9,2,384]{3,2,1,0:T(2,128)S(1)}, u32[]{:S(2)}, u32[]{:S(2)}) collective-permute-start(f32[11,9,2,384]{3,2,1,0:T(2,128)S(1)} %get-tuple-element.34), channel_id=1, source_target_pairs={{0,4},{4,0},{8,12},{12,8},{1,5},{5,1},{9,13},{13,9},{2,6},{6,2},{1... | collective-permute-start | bytes 912392 | tf_op jit(solution)/shard_map/ppermute | solution.py:50
  18.8 14.9 %collective-permute-start.4 = (f32[11,9,2,384]{3,2,1,0:T(2,128)S(1)}, f32[11,9,2,384]{3,2,1,0:T(2,128)S(1)}, u32[]{:S(2)}, u32[]{:S(2)}) collective-permute-start(f32[11,9,2,384]{3,2,1,0:T(2,128)S(1)} %get-tuple-element.35), channel_id=1, source_target_pairs={{4,8},{8,4},{5,9},{9,5},{6,10},{10,6},{7,11},{11,7},{20,24},{24,20... | collective-permute-start | bytes 912392 | tf_op jit(solution)/shard_map/ppermute | solution.py:50
  26.6 7.2 %collective-permute-start.10 = (f32[11,6,2,384]{3,2,1,0:T(2,128)S(1)}, f32[11,6,2,384]{3,2,1,0:T(2,128)S(1)}, u32[]{:S(2)}, u32[]{:S(2)}) collective-permute-start(f32[11,6,2,384]{3,2,1,0:T(2,128)S(1)} %get-tuple-element.43), channel_id=1, source_target_pairs={{0,4},{4,0},{8,12},{12,8},{1,5},{5,1},{9,13},{13,9},{2,6},{6,2},{1... | collective-permute-start | bytes 608264 | tf_op jit(solution)/shard_map/ppermute | solution.py:50
  26.8 7.0 %copy-start.2 = (f32[9]{0:T(128)S(1)}, f32[9]{0:T(128)}, u32[]{:S(2)}) copy-start(f32[9]{0:T(128)} %refs_2_.3) | copy-start | bytes 112
  26.8 6.9 %collective-permute-start.11 = (f32[11,6,2,384]{3,2,1,0:T(2,128)S(1)}, f32[11,6,2,384]{3,2,1,0:T(2,128)S(1)}, u32[]{:S(2)}, u32[]{:S(2)}) collective-permute-start(f32[11,6,2,384]{3,2,1,0:T(2,128)S(1)} %get-tuple-element.44), channel_id=1, source_target_pairs={{4,8},{8,4},{5,9},{9,5},{6,10},{10,6},{7,11},{11,7},{20,24},{24,20... | collective-permute-start | bytes 608264 | tf_op jit(solution)/shard_map/ppermute | solution.py:50
  36.8 7.8 %collective-permute-start.12 = (f32[5,12,2,384]{3,2,1,0:T(2,128)S(1)}, f32[5,12,2,384]{3,2,1,0:T(2,128)S(1)}, u32[]{:S(2)}, u32[]{:S(2)}) collective-permute-start(f32[5,12,2,384]{3,2,1,0:T(2,128)S(1)} %get-tuple-element.50), channel_id=1, source_target_pairs={{0,4},{4,0},{8,12},{12,8},{1,5},{5,1},{9,13},{13,9},{2,6},{6,2},{1... | collective-permute-start | bytes 552968 | tf_op jit(solution)/shard_map/ppermute | solution.py:50
  40.3 4.2 %collective-permute-start.13 = (f32[5,12,2,384]{3,2,1,0:T(2,128)S(1)}, f32[5,12,2,384]{3,2,1,0:T(2,128)S(1)}, u32[]{:S(2)}, u32[]{:S(2)}) collective-permute-start(f32[5,12,2,384]{3,2,1,0:T(2,128)S(1)} %get-tuple-element.51), channel_id=1, source_target_pairs={{4,8},{8,4},{5,9},{9,5},{6,10},{10,6},{7,11},{11,7},{20,24},{24,20... | collective-permute-start | bytes 552968 | tf_op jit(solution)/shard_map/ppermute | solution.py:50
  47.1 3.7 %collective-permute-start.14 = (f32[3,2,360]{2,1,0:T(2,128)S(1)}, f32[3,2,360]{2,1,0:T(2,128)S(1)}, u32[]{:S(2)}, u32[]{:S(2)}) collective-permute-start(f32[3,2,360]{2,1,0:T(2,128)S(1)} %get-tuple-element.55), channel_id=1, source_target_pairs={{0,2},{2,0},{1,3},{3,1},{4,6},{6,4},{5,7},{7,5},{8,10},{10,8},{9,1... | collective-permute-start | bytes 25928 | tf_op jit(solution)/shard_map/ppermute | solution.py:631

commit v8 on v7

--- a/solution.py
+++ b/solution.py
@@ -191,6 +191,11 @@
     for out, (_, start, _) in zip(outs, moves()):
         out[...] = body[:, pl.ds(start, STEPS)]
     tile_messages(body, first_out, second_out)
+
+
+def stage_kernel(own, payload, own_out, payload_out):
+    own_out[...] = own[...]
+    payload_out[...] = payload[...]
 
 
 def far_kernel(number, *refs):
@@ -504,7 +509,16 @@
     )(*fields)
     edge = lax.ppermute(edge, "sub", sub_pairs)
     swapped = lax.ppermute(payload, "sub", sub_pairs)
-    edge, beside, swapped = lax.optimization_barrier((edge, beside, swapped))
+    own, payload = call(
+        stage_kernel,
+        8,
+        flops=10**9,
+        out_shape=[shape(*own.shape), shape(*payload.shape)],
+        in_specs=[VMEM] * 2,
+        out_specs=[VMEM] * 2,
+        name="stage",
+    )(own, payload)
+    edge, beside, swapped, own, payload = lax.optimization_barrier((edge, beside, swapped, own, payload))
     crossed = [lax.ppermute(part, "sub", sub_pairs) for part in beside]
     depth = tracers + 5 + (tracers + 3) // 2
     body, first, second, *parts = call(

time: 51.9 us -> 49.7 us (0.958)
  waiting for transfers between devices: 11.5 us -> 9.54 us
    ppermute x1, waiting for transfers between devices: 2.01 us -> 0.03 us  [per_device(): lax.ppermute(averaging_kernel, 'levels', pairs)]
  transfers between devices with their start and end apart: 15 -> 15, of which waited for: 5 -> 4; matrix products, arithmetic and copies ran while one was open for 0% -> 0% of each run, Pallas kernels for 22% -> 23%
where the time goes in v8:
time: 49.7 us; the launch traced here: 49.1 us
  Pallas kernels  19.4 us (39%)
  starting transfers between devices  17 us (34%)
  waiting for transfers between devices  9.54 us (19%)
  local copies, waits for them, and re-layouts  1.78 us (4%)
  between operations  0.78 us (2%)
  other arithmetic  0.6 us (1%)
    pallas_call x2, Pallas kernels, forcing_of(): call(functools.partial(forcing_kernel, steps, *sizes), limit, flops=2 * l...  9.47 us
    ppermute x6, starting transfers between devices, swap_tiles(): return lax.ppermute(value, 'tiles', pairs)  6.75 us
    ppermute x3, waiting for transfers between devices, per_device(): lax.ppermute(both, 'tiles', [(i, i ^ k) for i in range(tiles)])  5.15 us
    ppermute x3, starting transfers between devices, per_device(): lax.ppermute(both, 'tiles', [(i, i ^ k) for i in range(tiles)])  4.45 us
    ppermute x1, waiting for transfers between devices, per_device(): flux_gradient = keep + lax.ppermute(give, 'levels', [(0, 1), (1, 0)])  3.15 us
    pallas_call x1, Pallas kernels, per_device(): call(functools.partial(first_kernel, moves, levels), 16, out_shape=[shape...  3 us
    ppermute x1, starting transfers between devices, per_device(): lax.ppermute(averaging_kernel, 'levels', pairs)  2.56 us
    pallas_call x1, Pallas kernels, per_device(): call(functools.partial(next_kernel, round_id, levels, rows), 16, out_shap...  2.53 us
  transfers between devices with their start and end apart: 15, of which 4 were waited for; matrix products, arithmetic and copies ran while one was open for 0% of the time, Pallas kernels for 23%

profile of v8, /device:TPU:0, one launch (start us, length us, event | category | flops | bytes accessed | tf_op | source)
XLA Modules:
  0.0 49.1 jit_solution(3138884747530028208)
XLA Ops:
  0.6 2.1 %edges.1 = (f32[8,9,4,384]{3,2,1,0:T(4,128)}, f32[8,9,4,128]{3,2,1,0:T(4,128)}, f32[24,384]{1,0:T(8,128)}) custom-call(f32[3,9,4,360]{3,2,1,0:T(4,128)} %refs_0_.1, f32[9,4,360]{2,1,0:T(4,128)} %refs_1_.1, f32[9,4,360]{2,1,0:T(4,128)} %refs_2_.2, s32[2,9,4,360]{3,2,1,0:T(4,128)} %refs_3_.1, f32[9,4,360]{2,1,0:T(4,128)} %refs_4_.1, f32[3,384]{1,0:T(4,128)} %refs_5_.1, ...), custom_call_target="tpu_custom_call" | custom-call | bytes 1048576 | tf_op jit(solution)/shard_map/edges/pallas_call | solution.py:499
  2.8 0.5 %collective-permute-start = (f32[8,9,4,128]{3,2,1,0:T(4,128)}, f32[8,9,4,128]{3,2,1,0:T(4,128)S(1)}, u32[]{:S(2)}, u32[]{:S(2)}) collective-permute-start(f32[8,9,4,128]{3,2,1,0:T(4,128)} %get-tuple-element.33), channel_id=1, source_target_pairs={{0,1},{1,0},{2,3},{3,2},{4,5},{5,4},{6,7},{7,6},{8,9},{9,8},{10,11... | collective-permute-start | bytes 442376 | tf_op jit(solution)/shard_map/ppermute | solution.py:510
  3.3 2.6 %collective-permute-start.1 = (f32[9,384]{1,0:T(8,128)}, f32[9,384]{1,0:T(8,128)S(1)}, u32[]{:S(2)}, u32[]{:S(2)}) collective-permute-start(f32[9,384]{1,0:T(8,128)} %refs_6_.1), channel_id=1, source_target_pairs={{0,2},{2,0},{1,3},{3,1},{4,6},{6,4},{5,7},{7,5},{8,10},{10,8},{9,1... | collective-permute-start | bytes 41480 | tf_op jit(solution)/shard_map/ppermute | solution.py:494
  6.0 1.0 %copy-done.1 = f32[8,9,4,384]{3,2,1,0:T(4,128)S(1)} copy-done((f32[8,9,4,384]{3,2,1,0:T(4,128)S(1)}, f32[8,9,4,384]{3,2,1,0:T(4,128)}, u32[]{:S(2)}) %copy-start.1) | copy-done | bytes 442392
  7.0 0.8 %copy-done.2 = f32[24,384]{1,0:T(8,128)S(1)} copy-done((f32[24,384]{1,0:T(8,128)S(1)}, f32[24,384]{1,0:T(8,128)}, u32[]{:S(2)}) %copy-start.2) | copy-done | bytes 36888
  8.2 2.1 %collective-permute-start.5 = (f32[8,6,4,384]{3,2,1,0:T(4,128)S(1)}, f32[8,6,4,384]{3,2,1,0:T(4,128)S(1)}, u32[]{:S(2)}, u32[]{:S(2)}) collective-permute-start(f32[8,6,4,384]{3,2,1,0:T(4,128)S(1)} %get-tuple-element.43), channel_id=1, source_target_pairs={{0,2},{2,0},{1,3},{3,1},{4,6},{6,4},{5,7},{7,5},{8,10},{10,8},{9,1... | collective-permute-start | bytes 884744 | tf_op jit(solution)/shard_map/ppermute | solution.py:534
  10.3 1.2 %collective-permute-done.6.refs_3_ = f32[9,384]{1,0:T(8,128)S(1)} collective-permute-done((f32[9,384]{1,0:T(8,128)S(1)}, f32[9,384]{1,0:T(8,128)S(1)}, u32[]{:S(2)}, u32[]{:S(2)}) %collective-permute-start.6) | collective-permute-done | bytes 13856 | tf_op jit(solution)/shard_map/ppermute | solution.py:522
  11.5 1.6 %collective-permute-start.7 = (f32[2,5,4,384]{3,2,1,0:T(4,128)S(1)}, f32[2,5,4,384]{3,2,1,0:T(4,128)S(1)}, u32[]{:S(2)}, u32[]{:S(2)}) collective-permute-start(f32[2,5,4,384]{3,2,1,0:T(4,128)S(1)} %payload.1.refs_0_), channel_id=1, source_target_pairs={{0,4},{4,0},{8,12},{12,8},{1,5},{5,1},{9,13},{13,9},{2,6},{6,2},{1... | collective-permute-start | bytes 184328 | tf_op jit(solution)/shard_map/ppermute | solution.py:545
  13.1 2.6 %collective-permute-start.8 = (f32[2,5,4,384]{3,2,1,0:T(4,128)S(1)}, f32[2,5,4,384]{3,2,1,0:T(4,128)S(1)}, u32[]{:S(2)}, u32[]{:S(2)}) collective-permute-start(f32[2,5,4,384]{3,2,1,0:T(4,128)S(1)} %payload.1.refs_0_), channel_id=1, source_target_pairs={{0,8},{4,12},{8,0},{12,4},{1,9},{5,13},{9,1},{13,5},{2,10},{6,14},... | collective-permute-start | bytes 184328 | tf_op jit(solution)/shard_map/ppermute | solution.py:545
  15.9 0.7 %collective-permute-start.3 = (f32[11,9,2,384]{3,2,1,0:T(2,128)S(1)}, f32[11,9,2,384]{3,2,1,0:T(2,128)S(1)}, u32[]{:S(2)}, u32[]{:S(2)}) collective-permute-start(f32[11,9,2,384]{3,2,1,0:T(2,128)S(1)} %get-tuple-element.41), channel_id=1, source_target_pairs={{0,4},{4,0},{8,12},{12,8},{1,5},{5,1},{9,13},{13,9},{2,6},{6,2},{1... | collective-permute-start | bytes 912392 | tf_op jit(solution)/shard_map/ppermute | solution.py:50
  16.6 0.7 %collective-permute-start.4 = (f32[11,9,2,384]{3,2,1,0:T(2,128)S(1)}, f32[11,9,2,384]{3,2,1,0:T(2,128)S(1)}, u32[]{:S(2)}, u32[]{:S(2)}) collective-permute-start(f32[11,9,2,384]{3,2,1,0:T(2,128)S(1)} %get-tuple-element.42), channel_id=1, source_target_pairs={{4,8},{8,4},{5,9},{9,5},{6,10},{10,6},{7,11},{11,7},{20,24},{24,20... | collective-permute-start | bytes 912392 | tf_op jit(solution)/shard_map/ppermute | solution.py:50
  17.3 2.6 %collective-permute-done.8.refs_2_ = f32[2,5,4,384]{3,2,1,0:T(4,128)S(1)} collective-permute-done((f32[2,5,4,384]{3,2,1,0:T(4,128)S(1)}, f32[2,5,4,384]{3,2,1,0:T(4,128)S(1)}, u32[]{:S(2)}, u32[]{:S(2)}) %collective-permute-start.8) | collective-permute-done | bytes 61472 | tf_op jit(solution)/shard_map/ppermute | solution.py:545
  19.8 2.6 %collective-permute-done.9.refs_3_ = f32[2,5,4,384]{3,2,1,0:T(4,128)S(1)} collective-permute-done((f32[2,5,4,384]{3,2,1,0:T(4,128)S(1)}, f32[2,5,4,384]{3,2,1,0:T(4,128)S(1)}, u32[]{:S(2)}, u32[]{:S(2)}) %collective-permute-start.9) | collective-permute-done | bytes 61472 | tf_op jit(solution)/shard_map/ppermute | solution.py:545
  22.4 1.7 %prepare.1 = (bf16[42,16,3072]{2,1,0:T(8,128)(2,1)S(1)}, bf16[384,3072]{1,0:T(8,128)(2,1)S(1)}, f32[8,3072]{1,0:T(8,128)S(1)}) custom-call(f32[2,5,4,384]{3,2,1,0:T(4,128)S(1)} %payload.1.refs_0_, f32[2,5,4,384]{3,2,1,0:T(4,128)S(1)} %collective-permute-done.7.refs_1_, f32[2,5,4,384]{3,2,1,0:T(4,128)S(1)} %collective-permute-done.8.refs_2_, ...), custom_call_target="tpu_custom_call" | custom-call | bytes 1048576 | tf_op jit(solution)/shard_map/prepare/pallas_call | solution.py:559
  24.6 0.8 %collective-permute-start.11 = (f32[11,6,2,384]{3,2,1,0:T(2,128)S(1)}, f32[11,6,2,384]{3,2,1,0:T(2,128)S(1)}, u32[]{:S(2)}, u32[]{:S(2)}) collective-permute-start(f32[11,6,2,384]{3,2,1,0:T(2,128)S(1)} %get-tuple-element.52), channel_id=1, source_target_pairs={{4,8},{8,4},{5,9},{9,5},{6,10},{10,6},{7,11},{11,7},{20,24},{24,20... | collective-permute-start | bytes 608264 | tf_op jit(solution)/shard_map/ppermute | solution.py:50
  25.4 6.1 %forcing0.1.refs_6_.refs_0_ = f32[4,3,15,8,384]{4,3,2,1,0:T(8,128)S(1)} custom-call(bf16[42,16,3072]{2,1,0:T(8,128)(2,1)S(1)} %get-tuple-element.53.refs_0_, bf16[384,3072]{1,0:T(8,128)(2,1)S(1)} %get-tuple-element.54.refs_1_, f32[8,3072]{1,0:T(8,128)S(1)} %get-tuple-element.55.refs_2_), custom_call_target="tpu_custom_call" | custom-call | flops 6341787648 | bytes 1048576 | tf_op jit(solution)/shard_map/forcing0/pallas_call | solution.py:591
  31.5 3.0 %round0.1 = (f32[3,17,8,384]{3,2,1,0:T(8,128)S(1)}, f32[6,17,8,384]{3,2,1,0:T(8,128)S(1)}, f32[3,8,384]{2,1,0:T(8,128)S(1)}, f32[5,12,2,384]{3,2,1,0:T(2,128)S(1)}, f32[5,12,2,384]{3,2,1,0:T(2,128)S(1)}) custom-call(f32[8,9,4,384]{3,2,1,0:T(4,128)S(1)} %get-tuple-element.40.refs_0_, f32[11,9,2,384]{3,2,1,0:T(2,128)S(1)} %collective-permute-done.3.refs_1_, ...), custom_call_target="tpu_custom_call" | custom-call | bytes 1048576 | tf_op jit(solution)/shard_map/round0/pallas_call | solution.py:613
  34.5 3.6 %collective-permute-start.12 = (f32[5,12,2,384]{3,2,1,0:T(2,128)S(1)}, f32[5,12,2,384]{3,2,1,0:T(2,128)S(1)}, u32[]{:S(2)}, u32[]{:S(2)}) collective-permute-start(f32[5,12,2,384]{3,2,1,0:T(2,128)S(1)} %get-tuple-element.58), channel_id=1, source_target_pairs={{0,4},{4,0},{8,12},{12,8},{1,5},{5,1},{9,13},{13,9},{2,6},{6,2},{1... | collective-permute-start | bytes 552968 | tf_op jit(solution)/shard_map/ppermute | solution.py:50
  38.1 0.8 %collective-permute-start.13 = (f32[5,12,2,384]{3,2,1,0:T(2,128)S(1)}, f32[5,12,2,384]{3,2,1,0:T(2,128)S(1)}, u32[]{:S(2)}, u32[]{:S(2)}) collective-permute-start(f32[5,12,2,384]{3,2,1,0:T(2,128)S(1)} %get-tuple-element.59), channel_id=1, source_target_pairs={{4,8},{8,4},{5,9},{9,5},{6,10},{10,6},{7,11},{11,7},{20,24},{24,20... | collective-permute-start | bytes 552968 | tf_op jit(solution)/shard_map/ppermute | solution.py:50
  38.9 3.4 %forcing3.1.refs_1_ = f32[2,3,15,8,384]{4,3,2,1,0:T(8,128)S(1)} custom-call(bf16[42,16,3072]{2,1,0:T(8,128)(2,1)S(1)} %get-tuple-element.53.refs_0_, bf16[384,3072]{1,0:T(8,128)(2,1)S(1)} %get-tuple-element.54.refs_1_, f32[8,3072]{1,0:T(8,128)S(1)} %get-tuple-element.55.refs_2_), custom_call_target="tpu_custom_call" | custom-call | flops 3170893824 | bytes 1048576 | tf_op jit(solution)/shard_map/forcing3/pallas_call | solution.py:591
  42.3 2.5 %round1.1 = (f32[3,9,4,360]{3,2,1,0:T(4,128)}, f32[3,2,360]{2,1,0:T(2,128)S(1)}, f32[3,2,360]{2,1,0:T(2,128)S(1)}) custom-call(f32[3,17,8,384]{3,2,1,0:T(8,128)S(1)} %get-tuple-element.56.state, f32[6,17,8,384]{3,2,1,0:T(8,128)S(1)} %get-tuple-element.57.coef, f32[5,12,2,384]{3,2,1,0:T(2,128)S(1)} %collective-permute-done.12.first, ...), custom_call_target="tpu_custom_call" | custom-call | bytes 1048576 | tf_op jit(solution)/shard_map/round1/pallas_call | solution.py:632
  44.9 0.5 %collective-permute-start.14 = (f32[3,2,360]{2,1,0:T(2,128)S(1)}, f32[3,2,360]{2,1,0:T(2,128)S(1)}, u32[]{:S(2)}, u32[]{:S(2)}) collective-permute-start(f32[3,2,360]{2,1,0:T(2,128)S(1)} %get-tuple-element.63), channel_id=1, source_target_pairs={{0,2},{2,0},{1,3},{3,1},{4,6},{6,4},{5,7},{7,5},{8,10},{10,8},{9,1... | collective-permute-start | bytes 25928 | tf_op jit(solution)/shard_map/ppermute | solution.py:645
  45.4 3.1 %collective-permute-done.14 = f32[3,2,360]{2,1,0:T(2,128)S(1)} collective-permute-done((f32[3,2,360]{2,1,0:T(2,128)S(1)}, f32[3,2,360]{2,1,0:T(2,128)S(1)}, u32[]{:S(2)}, u32[]{:S(2)}) %collective-permute-start.14) | collective-permute-done | bytes 8672 | tf_op jit(solution)/shard_map/ppermute | solution.py:645
  48.5 0.6 %add.3 = f32[3,2,360]{2,1,0:T(2,128)} add(f32[3,2,360]{2,1,0:T(2,128)S(1)} %get-tuple-element.62, f32[3,2,360]{2,1,0:T(2,128)S(1)} %collective-permute-done.14) | non-fusion elementwise | flops 2160 | bytes 25920 | tf_op jit(solution)/shard_map/add | solution.py:645
  (23 shorter events, 1.2 us)
Async XLA Ops:
  2.8 5.1 %collective-permute-start = (f32[8,9,4,128]{3,2,1,0:T(4,128)}, f32[8,9,4,128]{3,2,1,0:T(4,128)S(1)}, u32[]{:S(2)}, u32[]{:S(2)}) collective-permute-start(f32[8,9,4,128]{3,2,1,0:T(4,128)} %get-tuple-element.33), channel_id=1, source_target_pairs={{0,1},{1,0},{2,3},{3,2},{4,5},{5,4},{6,7},{7,6},{8,9},{9,8},{10,11... | collective-permute-start | bytes 442376 | tf_op jit(solution)/shard_map/ppermute | solution.py:510
  3.3 4.6 %collective-permute-start.1 = (f32[9,384]{1,0:T(8,128)}, f32[9,384]{1,0:T(8,128)S(1)}, u32[]{:S(2)}, u32[]{:S(2)}) collective-permute-start(f32[9,384]{1,0:T(8,128)} %refs_6_.1), channel_id=1, source_target_pairs={{0,2},{2,0},{1,3},{3,1},{4,6},{6,4},{5,7},{7,5},{8,10},{10,8},{9,1... | collective-permute-start | bytes 41480 | tf_op jit(solution)/shard_map/ppermute | solution.py:494
  5.9 2.0 %collective-permute-start.2 = (f32[24,384]{1,0:T(8,128)}, f32[24,384]{1,0:T(8,128)S(1)}, u32[]{:S(2)}, u32[]{:S(2)}) collective-permute-start(f32[24,384]{1,0:T(8,128)} %get-tuple-element.34.payload), channel_id=1, source_target_pairs={{0,1},{1,0},{2,3},{3,2},{4,5},{5,4},{6,7},{7,6},{8,9},{9,8},{10,11... | collective-permute-start | bytes 110600 | tf_op jit(solution)/shard_map/ppermute | solution.py:511
  6.0 1.0 %copy-start.1 = (f32[8,9,4,384]{3,2,1,0:T(4,128)S(1)}, f32[8,9,4,384]{3,2,1,0:T(4,128)}, u32[]{:S(2)}) copy-start(f32[8,9,4,384]{3,2,1,0:T(4,128)} %get-tuple-element.35.own) | copy-start | bytes 1327108
  7.0 0.8 %copy-start.2 = (f32[24,384]{1,0:T(8,128)S(1)}, f32[24,384]{1,0:T(8,128)}, u32[]{:S(2)}) copy-start(f32[24,384]{1,0:T(8,128)} %get-tuple-element.34.payload) | copy-start | bytes 110596
  8.2 16.0 %collective-permute-start.5 = (f32[8,6,4,384]{3,2,1,0:T(4,128)S(1)}, f32[8,6,4,384]{3,2,1,0:T(4,128)S(1)}, u32[]{:S(2)}, u32[]{:S(2)}) collective-permute-start(f32[8,6,4,384]{3,2,1,0:T(4,128)S(1)} %get-tuple-element.43), channel_id=1, source_target_pairs={{0,2},{2,0},{1,3},{3,1},{4,6},{6,4},{5,7},{7,5},{8,10},{10,8},{9,1... | collective-permute-start | bytes 884744 | tf_op jit(solution)/shard_map/ppermute | solution.py:534
  10.3 1.2 %collective-permute-start.6 = (f32[9,384]{1,0:T(8,128)S(1)}, f32[9,384]{1,0:T(8,128)S(1)}, u32[]{:S(2)}, u32[]{:S(2)}) collective-permute-start(f32[9,384]{1,0:T(8,128)S(1)} %collective-permute-done.1.refs_1_), channel_id=1, source_target_pairs={{0,1},{1,0},{2,3},{3,2},{4,5},{5,4},{6,7},{7,6},{8,9},{9,8},{10,11... | collective-permute-start | bytes 41480 | tf_op jit(solution)/shard_map/ppermute | solution.py:522
  11.5 5.1 %collective-permute-start.7 = (f32[2,5,4,384]{3,2,1,0:T(4,128)S(1)}, f32[2,5,4,384]{3,2,1,0:T(4,128)S(1)}, u32[]{:S(2)}, u32[]{:S(2)}) collective-permute-start(f32[2,5,4,384]{3,2,1,0:T(4,128)S(1)} %payload.1.refs_0_), channel_id=1, source_target_pairs={{0,4},{4,0},{8,12},{12,8},{1,5},{5,1},{9,13},{13,9},{2,6},{6,2},{1... | collective-permute-start | bytes 184328 | tf_op jit(solution)/shard_map/ppermute | solution.py:545
  13.1 6.7 %collective-permute-start.8 = (f32[2,5,4,384]{3,2,1,0:T(4,128)S(1)}, f32[2,5,4,384]{3,2,1,0:T(4,128)S(1)}, u32[]{:S(2)}, u32[]{:S(2)}) collective-permute-start(f32[2,5,4,384]{3,2,1,0:T(4,128)S(1)} %payload.1.refs_0_), channel_id=1, source_target_pairs={{0,8},{4,12},{8,0},{12,4},{1,9},{5,13},{9,1},{13,5},{2,10},{6,14},... | collective-permute-start | bytes 184328 | tf_op jit(solution)/shard_map/ppermute | solution.py:545
  15.7 6.7 %collective-permute-start.9 = (f32[2,5,4,384]{3,2,1,0:T(4,128)S(1)}, f32[2,5,4,384]{3,2,1,0:T(4,128)S(1)}, u32[]{:S(2)}, u32[]{:S(2)}) collective-permute-start(f32[2,5,4,384]{3,2,1,0:T(4,128)S(1)} %payload.1.refs_0_), channel_id=1, source_target_pairs={{0,12},{4,8},{8,4},{12,0},{1,13},{5,9},{9,5},{13,1},{2,14},{6,10},... | collective-permute-start | bytes 184328 | tf_op jit(solution)/shard_map/ppermute | solution.py:545
  15.9 15.5 %collective-permute-start.3 = (f32[11,9,2,384]{3,2,1,0:T(2,128)S(1)}, f32[11,9,2,384]{3,2,1,0:T(2,128)S(1)}, u32[]{:S(2)}, u32[]{:S(2)}) collective-permute-start(f32[11,9,2,384]{3,2,1,0:T(2,128)S(1)} %get-tuple-element.41), channel_id=1, source_target_pairs={{0,4},{4,0},{8,12},{12,8},{1,5},{5,1},{9,13},{13,9},{2,6},{6,2},{1... | collective-permute-start | bytes 912392 | tf_op jit(solution)/shard_map/ppermute | solution.py:50
  16.6 14.9 %collective-permute-start.4 = (f32[11,9,2,384]{3,2,1,0:T(2,128)S(1)}, f32[11,9,2,384]{3,2,1,0:T(2,128)S(1)}, u32[]{:S(2)}, u32[]{:S(2)}) collective-permute-start(f32[11,9,2,384]{3,2,1,0:T(2,128)S(1)} %get-tuple-element.42), channel_id=1, source_target_pairs={{4,8},{8,4},{5,9},{9,5},{6,10},{10,6},{7,11},{11,7},{20,24},{24,20... | collective-permute-start | bytes 912392 | tf_op jit(solution)/shard_map/ppermute | solution.py:50
  24.4 7.2 %collective-permute-start.10 = (f32[11,6,2,384]{3,2,1,0:T(2,128)S(1)}, f32[11,6,2,384]{3,2,1,0:T(2,128)S(1)}, u32[]{:S(2)}, u32[]{:S(2)}) collective-permute-start(f32[11,6,2,384]{3,2,1,0:T(2,128)S(1)} %get-tuple-element.51), channel_id=1, source_target_pairs={{0,4},{4,0},{8,12},{12,8},{1,5},{5,1},{9,13},{13,9},{2,6},{6,2},{1... | collective-permute-start | bytes 608264 | tf_op jit(solution)/shard_map/ppermute | solution.py:50
  24.6 7.0 %copy-start = (f32[9]{0:T(128)S(1)}, f32[9]{0:T(128)}, u32[]{:S(2)}) copy-start(f32[9]{0:T(128)} %refs_2_.3) | copy-start | bytes 112
  24.6 6.9 %collective-permute-start.11 = (f32[11,6,2,384]{3,2,1,0:T(2,128)S(1)}, f32[11,6,2,384]{3,2,1,0:T(2,128)S(1)}, u32[]{:S(2)}, u32[]{:S(2)}) collective-permute-start(f32[11,6,2,384]{3,2,1,0:T(2,128)S(1)} %get-tuple-element.52), channel_id=1, source_target_pairs={{4,8},{8,4},{5,9},{9,5},{6,10},{10,6},{7,11},{11,7},{20,24},{24,20... | collective-permute-start | bytes 608264 | tf_op jit(solution)/shard_map/ppermute | solution.py:50
  34.5 7.8 %collective-permute-start.12 = (f32[5,12,2,384]{3,2,1,0:T(2,128)S(1)}, f32[5,12,2,384]{3,2,1,0:T(2,128)S(1)}, u32[]{:S(2)}, u32[]{:S(2)}) collective-permute-start(f32[5,12,2,384]{3,2,1,0:T(2,128)S(1)} %get-tuple-element.58), channel_id=1, source_target_pairs={{0,4},{4,0},{8,12},{12,8},{1,5},{5,1},{9,13},{13,9},{2,6},{6,2},{1... | collective-permute-start | bytes 552968 | tf_op jit(solution)/shard_map/ppermute | solution.py:50
  38.1 4.2 %collective-permute-start.13 = (f32[5,12,2,384]{3,2,1,0:T(2,128)S(1)}, f32[5,12,2,384]{3,2,1,0:T(2,128)S(1)}, u32[]{:S(2)}, u32[]{:S(2)}) collective-permute-start(f32[5,12,2,384]{3,2,1,0:T(2,128)S(1)} %get-tuple-element.59), channel_id=1, source_target_pairs={{4,8},{8,4},{5,9},{9,5},{6,10},{10,6},{7,11},{11,7},{20,24},{24,20... | collective-permute-start | bytes 552968 | tf_op jit(solution)/shard_map/ppermute | solution.py:50
  44.9 3.7 %collective-permute-start.14 = (f32[3,2,360]{2,1,0:T(2,128)S(1)}, f32[3,2,360]{2,1,0:T(2,128)S(1)}, u32[]{:S(2)}, u32[]{:S(2)}) collective-permute-start(f32[3,2,360]{2,1,0:T(2,128)S(1)} %get-tuple-element.63), channel_id=1, source_target_pairs={{0,2},{2,0},{1,3},{3,1},{4,6},{6,4},{5,7},{7,5},{8,10},{10,8},{9,1... | collective-permute-start | bytes 25928 | tf_op jit(solution)/shard_map/ppermute | solution.py:645

commit v9 on v8

--- a/solution.py
+++ b/solution.py
@@ -292,14 +292,14 @@
     refs = refs[3 * (1 + number) :]
     count = len(forced_in(0))
     forcings, profile = refs[:count], refs[count]
-    state_out, coef_out, flux, first_out, second_out, work, other, outer, raw = refs[count + 1 :]
+    state_out, coef_out, flux, first_out, second_out, work, outer, raw = refs[count + 1 :]
     planes, _, rows, lanes = groups[0][0].shape
     tracers = planes - 5
     mixing, east, west, north, south = range(tracers, planes)
     raw[...] = jnp.zeros_like(raw)
     flux[...] = jnp.zeros_like(flux)
     clear_pads(work)
-    clear_pads(other)
+    clear_pads(state_out)
     clear_pads(outer)
     even = is_even()
     starts = [window(0, levels)[0]] + [slot for _, _, slot in moves()]
@@ -325,8 +325,7 @@
     for l in range(raw.shape[1]):
         coef_out[2, l] = pltpu.roll(raw[2, l], 1, 1)
         coef_out[4, l] = jnp.where(ids == 6, raw[6, l], pltpu.roll(raw[4, l], 1, 0))
-    last = run_steps(0, work, other, outer, coef_out, forcings, profile, flux, levels)
-    state_out[...] = last[...]
+    run_steps(0, work, state_out, outer, coef_out, forcings, profile, flux, levels)
     send_rows(0, state_out, first_out, second_out, rows, levels)
 
 
@@ -616,7 +615,7 @@
         out_shape=[shape(*state_shape), shape(*coef_shape), shape(*flux_shape), *messages(1)],
         in_specs=[VMEM] * (len(blocks) + len(forced_in(0))) + [SMEM],
         out_specs=[VMEM] * 5,
-        scratch_shapes=scratch + [pltpu.VMEM((7, wide + 2, 8, lanes), F32)],
+        scratch_shapes=scratch[:2] + [pltpu.VMEM((7, wide + 2, 8, lanes), F32)],
         name="round0",
     )(*blocks, *[forcings[i] for i in forced_in(0)], level_profile)
     half = rows // 2 if bands == 2 else rows

time: 49.7 us -> 49.6 us (level)
  no operation moved by 1% of the time
where the time goes in v9:
time: 49.6 us; the launch traced here: 49.1 us
  Pallas kernels  19.3 us (39%)
  starting transfers between devices  17.1 us (34%)
  waiting for transfers between devices  9.51 us (19%)
  local copies, waits for them, and re-layouts  1.78 us (4%)
  between operations  0.78 us (2%)
  other arithmetic  0.6 us (1%)
    pallas_call x2, Pallas kernels, forcing_of(): call(functools.partial(forcing_kernel, steps, *sizes), limit, flops=2 * l...  9.46 us
    ppermute x6, starting transfers between devices, swap_tiles(): return lax.ppermute(value, 'tiles', pairs)  6.75 us
    ppermute x3, waiting for transfers between devices, per_device(): lax.ppermute(both, 'tiles', [(i, i ^ k) for i in range(tiles)])  5.15 us
    ppermute x3, starting transfers between devices, per_device(): lax.ppermute(both, 'tiles', [(i, i ^ k) for i in range(tiles)])  4.45 us
    ppermute x1, waiting for transfers between devices, per_device(): flux_gradient = keep + lax.ppermute(give, 'levels', [(0, 1), (1, 0)])  3.11 us
    pallas_call x1, Pallas kernels, per_device(): call(functools.partial(first_kernel, moves, levels), 16, out_shape=[shape...  2.92 us
    ppermute x1, starting transfers between devices, per_device(): lax.ppermute(averaging_kernel, 'levels', pairs)  2.56 us
    pallas_call x1, Pallas kernels, per_device(): call(functools.partial(next_kernel, round_id, levels, rows), 16, out_shap...  2.53 us
  transfers between devices with their start and end apart: 15, of which 4 were waited for; matrix products, arithmetic and copies ran while one was open for 0% of the time, Pallas kernels for 23%

profile of v9, /device:TPU:0, one launch (start us, length us, event | category | flops | bytes accessed | tf_op | source)
XLA Modules:
  0.0 49.1 jit_solution(15327353889598070907)
XLA Ops:
  0.6 2.1 %edges.1 = (f32[8,9,4,384]{3,2,1,0:T(4,128)}, f32[8,9,4,128]{3,2,1,0:T(4,128)}, f32[24,384]{1,0:T(8,128)}) custom-call(f32[3,9,4,360]{3,2,1,0:T(4,128)} %refs_0_.1, f32[9,4,360]{2,1,0:T(4,128)} %refs_1_.1, f32[9,4,360]{2,1,0:T(4,128)} %refs_2_.2, s32[2,9,4,360]{3,2,1,0:T(4,128)} %refs_3_.1, f32[9,4,360]{2,1,0:T(4,128)} %refs_4_.1, f32[3,384]{1,0:T(4,128)} %refs_5_.1, ...), custom_call_target="tpu_custom_call" | custom-call | bytes 1048576 | tf_op jit(solution)/shard_map/edges/pallas_call | solution.py:498
  2.8 0.5 %collective-permute-start = (f32[8,9,4,128]{3,2,1,0:T(4,128)}, f32[8,9,4,128]{3,2,1,0:T(4,128)S(1)}, u32[]{:S(2)}, u32[]{:S(2)}) collective-permute-start(f32[8,9,4,128]{3,2,1,0:T(4,128)} %get-tuple-element.33), channel_id=1, source_target_pairs={{0,1},{1,0},{2,3},{3,2},{4,5},{5,4},{6,7},{7,6},{8,9},{9,8},{10,11... | collective-permute-start | bytes 442376 | tf_op jit(solution)/shard_map/ppermute | solution.py:509
  3.3 2.6 %collective-permute-start.1 = (f32[9,384]{1,0:T(8,128)}, f32[9,384]{1,0:T(8,128)S(1)}, u32[]{:S(2)}, u32[]{:S(2)}) collective-permute-start(f32[9,384]{1,0:T(8,128)} %refs_6_.1), channel_id=1, source_target_pairs={{0,2},{2,0},{1,3},{3,1},{4,6},{6,4},{5,7},{7,5},{8,10},{10,8},{9,1... | collective-permute-start | bytes 41480 | tf_op jit(solution)/shard_map/ppermute | solution.py:493
  6.0 1.0 %copy-done.1 = f32[8,9,4,384]{3,2,1,0:T(4,128)S(1)} copy-done((f32[8,9,4,384]{3,2,1,0:T(4,128)S(1)}, f32[8,9,4,384]{3,2,1,0:T(4,128)}, u32[]{:S(2)}) %copy-start.1) | copy-done | bytes 442392
  7.0 0.8 %copy-done.2 = f32[24,384]{1,0:T(8,128)S(1)} copy-done((f32[24,384]{1,0:T(8,128)S(1)}, f32[24,384]{1,0:T(8,128)}, u32[]{:S(2)}) %copy-start.2) | copy-done | bytes 36888
  8.2 2.1 %collective-permute-start.5 = (f32[8,6,4,384]{3,2,1,0:T(4,128)S(1)}, f32[8,6,4,384]{3,2,1,0:T(4,128)S(1)}, u32[]{:S(2)}, u32[]{:S(2)}) collective-permute-start(f32[8,6,4,384]{3,2,1,0:T(4,128)S(1)} %get-tuple-element.43), channel_id=1, source_target_pairs={{0,2},{2,0},{1,3},{3,1},{4,6},{6,4},{5,7},{7,5},{8,10},{10,8},{9,1... | collective-permute-start | bytes 884744 | tf_op jit(solution)/shard_map/ppermute | solution.py:533
  10.3 1.2 %collective-permute-done.6.refs_3_ = f32[9,384]{1,0:T(8,128)S(1)} collective-permute-done((f32[9,384]{1,0:T(8,128)S(1)}, f32[9,384]{1,0:T(8,128)S(1)}, u32[]{:S(2)}, u32[]{:S(2)}) %collective-permute-start.6) | collective-permute-done | bytes 13856 | tf_op jit(solution)/shard_map/ppermute | solution.py:521
  11.5 1.6 %collective-permute-start.7 = (f32[2,5,4,384]{3,2,1,0:T(4,128)S(1)}, f32[2,5,4,384]{3,2,1,0:T(4,128)S(1)}, u32[]{:S(2)}, u32[]{:S(2)}) collective-permute-start(f32[2,5,4,384]{3,2,1,0:T(4,128)S(1)} %payload.1.refs_0_), channel_id=1, source_target_pairs={{0,4},{4,0},{8,12},{12,8},{1,5},{5,1},{9,13},{13,9},{2,6},{6,2},{1... | collective-permute-start | bytes 184328 | tf_op jit(solution)/shard_map/ppermute | solution.py:544
  13.1 2.6 %collective-permute-start.8 = (f32[2,5,4,384]{3,2,1,0:T(4,128)S(1)}, f32[2,5,4,384]{3,2,1,0:T(4,128)S(1)}, u32[]{:S(2)}, u32[]{:S(2)}) collective-permute-start(f32[2,5,4,384]{3,2,1,0:T(4,128)S(1)} %payload.1.refs_0_), channel_id=1, source_target_pairs={{0,8},{4,12},{8,0},{12,4},{1,9},{5,13},{9,1},{13,5},{2,10},{6,14},... | collective-permute-start | bytes 184328 | tf_op jit(solution)/shard_map/ppermute | solution.py:544
  15.9 0.7 %collective-permute-start.3 = (f32[11,9,2,384]{3,2,1,0:T(2,128)S(1)}, f32[11,9,2,384]{3,2,1,0:T(2,128)S(1)}, u32[]{:S(2)}, u32[]{:S(2)}) collective-permute-start(f32[11,9,2,384]{3,2,1,0:T(2,128)S(1)} %get-tuple-element.41), channel_id=1, source_target_pairs={{0,4},{4,0},{8,12},{12,8},{1,5},{5,1},{9,13},{13,9},{2,6},{6,2},{1... | collective-permute-start | bytes 912392 | tf_op jit(solution)/shard_map/ppermute | solution.py:50
  16.6 0.7 %collective-permute-start.4 = (f32[11,9,2,384]{3,2,1,0:T(2,128)S(1)}, f32[11,9,2,384]{3,2,1,0:T(2,128)S(1)}, u32[]{:S(2)}, u32[]{:S(2)}) collective-permute-start(f32[11,9,2,384]{3,2,1,0:T(2,128)S(1)} %get-tuple-element.42), channel_id=1, source_target_pairs={{4,8},{8,4},{5,9},{9,5},{6,10},{10,6},{7,11},{11,7},{20,24},{24,20... | collective-permute-start | bytes 912392 | tf_op jit(solution)/shard_map/ppermute | solution.py:50
  17.3 2.6 %collective-permute-done.8.refs_2_ = f32[2,5,4,384]{3,2,1,0:T(4,128)S(1)} collective-permute-done((f32[2,5,4,384]{3,2,1,0:T(4,128)S(1)}, f32[2,5,4,384]{3,2,1,0:T(4,128)S(1)}, u32[]{:S(2)}, u32[]{:S(2)}) %collective-permute-start.8) | collective-permute-done | bytes 61472 | tf_op jit(solution)/shard_map/ppermute | solution.py:544
  19.8 2.6 %collective-permute-done.9.refs_3_ = f32[2,5,4,384]{3,2,1,0:T(4,128)S(1)} collective-permute-done((f32[2,5,4,384]{3,2,1,0:T(4,128)S(1)}, f32[2,5,4,384]{3,2,1,0:T(4,128)S(1)}, u32[]{:S(2)}, u32[]{:S(2)}) %collective-permute-start.9) | collective-permute-done | bytes 61472 | tf_op jit(solution)/shard_map/ppermute | solution.py:544
  22.4 1.7 %prepare.1 = (bf16[42,16,3072]{2,1,0:T(8,128)(2,1)S(1)}, bf16[384,3072]{1,0:T(8,128)(2,1)S(1)}, f32[8,3072]{1,0:T(8,128)S(1)}) custom-call(f32[2,5,4,384]{3,2,1,0:T(4,128)S(1)} %payload.1.refs_0_, f32[2,5,4,384]{3,2,1,0:T(4,128)S(1)} %collective-permute-done.7.refs_1_, f32[2,5,4,384]{3,2,1,0:T(4,128)S(1)} %collective-permute-done.8.refs_2_, ...), custom_call_target="tpu_custom_call" | custom-call | bytes 1048576 | tf_op jit(solution)/shard_map/prepare/pallas_call | solution.py:558
  24.6 0.8 %collective-permute-start.11 = (f32[11,6,2,384]{3,2,1,0:T(2,128)S(1)}, f32[11,6,2,384]{3,2,1,0:T(2,128)S(1)}, u32[]{:S(2)}, u32[]{:S(2)}) collective-permute-start(f32[11,6,2,384]{3,2,1,0:T(2,128)S(1)} %get-tuple-element.52), channel_id=1, source_target_pairs={{4,8},{8,4},{5,9},{9,5},{6,10},{10,6},{7,11},{11,7},{20,24},{24,20... | collective-permute-start | bytes 608264 | tf_op jit(solution)/shard_map/ppermute | solution.py:50
  25.4 6.1 %forcing0.1.refs_6_.refs_0_ = f32[4,3,15,8,384]{4,3,2,1,0:T(8,128)S(1)} custom-call(bf16[42,16,3072]{2,1,0:T(8,128)(2,1)S(1)} %get-tuple-element.53.refs_0_, bf16[384,3072]{1,0:T(8,128)(2,1)S(1)} %get-tuple-element.54.refs_1_, f32[8,3072]{1,0:T(8,128)S(1)} %get-tuple-element.55.refs_2_), custom_call_target="tpu_custom_call" | custom-call | flops 6341787648 | bytes 1048576 | tf_op jit(solution)/shard_map/forcing0/pallas_call | solution.py:590
  31.5 2.9 %round0.1 = (f32[3,17,8,384]{3,2,1,0:T(8,128)S(1)}, f32[6,17,8,384]{3,2,1,0:T(8,128)S(1)}, f32[3,8,384]{2,1,0:T(8,128)S(1)}, f32[5,12,2,384]{3,2,1,0:T(2,128)S(1)}, f32[5,12,2,384]{3,2,1,0:T(2,128)S(1)}) custom-call(f32[8,9,4,384]{3,2,1,0:T(4,128)S(1)} %get-tuple-element.40.refs_0_, f32[11,9,2,384]{3,2,1,0:T(2,128)S(1)} %collective-permute-done.3.refs_1_, ...), custom_call_target="tpu_custom_call" | custom-call | bytes 1048576 | tf_op jit(solution)/shard_map/round0/pallas_call | solution.py:612
  34.5 3.6 %collective-permute-start.12 = (f32[5,12,2,384]{3,2,1,0:T(2,128)S(1)}, f32[5,12,2,384]{3,2,1,0:T(2,128)S(1)}, u32[]{:S(2)}, u32[]{:S(2)}) collective-permute-start(f32[5,12,2,384]{3,2,1,0:T(2,128)S(1)} %get-tuple-element.58), channel_id=1, source_target_pairs={{0,4},{4,0},{8,12},{12,8},{1,5},{5,1},{9,13},{13,9},{2,6},{6,2},{1... | collective-permute-start | bytes 552968 | tf_op jit(solution)/shard_map/ppermute | solution.py:50
  38.0 0.8 %collective-permute-start.13 = (f32[5,12,2,384]{3,2,1,0:T(2,128)S(1)}, f32[5,12,2,384]{3,2,1,0:T(2,128)S(1)}, u32[]{:S(2)}, u32[]{:S(2)}) collective-permute-start(f32[5,12,2,384]{3,2,1,0:T(2,128)S(1)} %get-tuple-element.59), channel_id=1, source_target_pairs={{4,8},{8,4},{5,9},{9,5},{6,10},{10,6},{7,11},{11,7},{20,24},{24,20... | collective-permute-start | bytes 552968 | tf_op jit(solution)/shard_map/ppermute | solution.py:50
  38.9 3.4 %forcing3.1.refs_1_ = f32[2,3,15,8,384]{4,3,2,1,0:T(8,128)S(1)} custom-call(bf16[42,16,3072]{2,1,0:T(8,128)(2,1)S(1)} %get-tuple-element.53.refs_0_, bf16[384,3072]{1,0:T(8,128)(2,1)S(1)} %get-tuple-element.54.refs_1_, f32[8,3072]{1,0:T(8,128)S(1)} %get-tuple-element.55.refs_2_), custom_call_target="tpu_custom_call" | custom-call | flops 3170893824 | bytes 1048576 | tf_op jit(solution)/shard_map/forcing3/pallas_call | solution.py:590
  42.3 2.5 %round1.1 = (f32[3,9,4,360]{3,2,1,0:T(4,128)}, f32[3,2,360]{2,1,0:T(2,128)S(1)}, f32[3,2,360]{2,1,0:T(2,128)S(1)}) custom-call(f32[3,17,8,384]{3,2,1,0:T(8,128)S(1)} %get-tuple-element.56.state, f32[6,17,8,384]{3,2,1,0:T(8,128)S(1)} %get-tuple-element.57.coef, f32[5,12,2,384]{3,2,1,0:T(2,128)S(1)} %collective-permute-done.12.first, ...), custom_call_target="tpu_custom_call" | custom-call | bytes 1048576 | tf_op jit(solution)/shard_map/round1/pallas_call | solution.py:631
  44.8 0.5 %collective-permute-start.14 = (f32[3,2,360]{2,1,0:T(2,128)S(1)}, f32[3,2,360]{2,1,0:T(2,128)S(1)}, u32[]{:S(2)}, u32[]{:S(2)}) collective-permute-start(f32[3,2,360]{2,1,0:T(2,128)S(1)} %get-tuple-element.63), channel_id=1, source_target_pairs={{0,2},{2,0},{1,3},{3,1},{4,6},{6,4},{5,7},{7,5},{8,10},{10,8},{9,1... | collective-permute-start | bytes 25928 | tf_op jit(solution)/shard_map/ppermute | solution.py:644
  45.3 3.1 %collective-permute-done.14 = f32[3,2,360]{2,1,0:T(2,128)S(1)} collective-permute-done((f32[3,2,360]{2,1,0:T(2,128)S(1)}, f32[3,2,360]{2,1,0:T(2,128)S(1)}, u32[]{:S(2)}, u32[]{:S(2)}) %collective-permute-start.14) | collective-permute-done | bytes 8672 | tf_op jit(solution)/shard_map/ppermute | solution.py:644
  48.5 0.6 %add.3 = f32[3,2,360]{2,1,0:T(2,128)} add(f32[3,2,360]{2,1,0:T(2,128)S(1)} %get-tuple-element.62, f32[3,2,360]{2,1,0:T(2,128)S(1)} %collective-permute-done.14) | non-fusion elementwise | flops 2160 | bytes 25920 | tf_op jit(solution)/shard_map/add | solution.py:644
  (23 shorter events, 1.2 us)
Async XLA Ops:
  2.8 5.1 %collective-permute-start = (f32[8,9,4,128]{3,2,1,0:T(4,128)}, f32[8,9,4,128]{3,2,1,0:T(4,128)S(1)}, u32[]{:S(2)}, u32[]{:S(2)}) collective-permute-start(f32[8,9,4,128]{3,2,1,0:T(4,128)} %get-tuple-element.33), channel_id=1, source_target_pairs={{0,1},{1,0},{2,3},{3,2},{4,5},{5,4},{6,7},{7,6},{8,9},{9,8},{10,11... | collective-permute-start | bytes 442376 | tf_op jit(solution)/shard_map/ppermute | solution.py:509
  3.3 4.6 %collective-permute-start.1 = (f32[9,384]{1,0:T(8,128)}, f32[9,384]{1,0:T(8,128)S(1)}, u32[]{:S(2)}, u32[]{:S(2)}) collective-permute-start(f32[9,384]{1,0:T(8,128)} %refs_6_.1), channel_id=1, source_target_pairs={{0,2},{2,0},{1,3},{3,1},{4,6},{6,4},{5,7},{7,5},{8,10},{10,8},{9,1... | collective-permute-start | bytes 41480 | tf_op jit(solution)/shard_map/ppermute | solution.py:493
  5.9 2.0 %collective-permute-start.2 = (f32[24,384]{1,0:T(8,128)}, f32[24,384]{1,0:T(8,128)S(1)}, u32[]{:S(2)}, u32[]{:S(2)}) collective-permute-start(f32[24,384]{1,0:T(8,128)} %get-tuple-element.34.payload), channel_id=1, source_target_pairs={{0,1},{1,0},{2,3},{3,2},{4,5},{5,4},{6,7},{7,6},{8,9},{9,8},{10,11... | collective-permute-start | bytes 110600 | tf_op jit(solution)/shard_map/ppermute | solution.py:510
  6.0 1.0 %copy-start.1 = (f32[8,9,4,384]{3,2,1,0:T(4,128)S(1)}, f32[8,9,4,384]{3,2,1,0:T(4,128)}, u32[]{:S(2)}) copy-start(f32[8,9,4,384]{3,2,1,0:T(4,128)} %get-tuple-element.35.own) | copy-start | bytes 1327108
  7.0 0.8 %copy-start.2 = (f32[24,384]{1,0:T(8,128)S(1)}, f32[24,384]{1,0:T(8,128)}, u32[]{:S(2)}) copy-start(f32[24,384]{1,0:T(8,128)} %get-tuple-element.34.payload) | copy-start | bytes 110596
  8.2 16.0 %collective-permute-start.5 = (f32[8,6,4,384]{3,2,1,0:T(4,128)S(1)}, f32[8,6,4,384]{3,2,1,0:T(4,128)S(1)}, u32[]{:S(2)}, u32[]{:S(2)}) collective-permute-start(f32[8,6,4,384]{3,2,1,0:T(4,128)S(1)} %get-tuple-element.43), channel_id=1, source_target_pairs={{0,2},{2,0},{1,3},{3,1},{4,6},{6,4},{5,7},{7,5},{8,10},{10,8},{9,1... | collective-permute-start | bytes 884744 | tf_op jit(solution)/shard_map/ppermute | solution.py:533
  10.3 1.2 %collective-permute-start.6 = (f32[9,384]{1,0:T(8,128)S(1)}, f32[9,384]{1,0:T(8,128)S(1)}, u32[]{:S(2)}, u32[]{:S(2)}) collective-permute-start(f32[9,384]{1,0:T(8,128)S(1)} %collective-permute-done.1.refs_1_), channel_id=1, source_target_pairs={{0,1},{1,0},{2,3},{3,2},{4,5},{5,4},{6,7},{7,6},{8,9},{9,8},{10,11... | collective-permute-start | bytes 41480 | tf_op jit(solution)/shard_map/ppermute | solution.py:521
  11.5 5.1 %collective-permute-start.7 = (f32[2,5,4,384]{3,2,1,0:T(4,128)S(1)}, f32[2,5,4,384]{3,2,1,0:T(4,128)S(1)}, u32[]{:S(2)}, u32[]{:S(2)}) collective-permute-start(f32[2,5,4,384]{3,2,1,0:T(4,128)S(1)} %payload.1.refs_0_), channel_id=1, source_target_pairs={{0,4},{4,0},{8,12},{12,8},{1,5},{5,1},{9,13},{13,9},{2,6},{6,2},{1... | collective-permute-start | bytes 184328 | tf_op jit(solution)/shard_map/ppermute | solution.py:544
  13.1 6.7 %collective-permute-start.8 = (f32[2,5,4,384]{3,2,1,0:T(4,128)S(1)}, f32[2,5,4,384]{3,2,1,0:T(4,128)S(1)}, u32[]{:S(2)}, u32[]{:S(2)}) collective-permute-start(f32[2,5,4,384]{3,2,1,0:T(4,128)S(1)} %payload.1.refs_0_), channel_id=1, source_target_pairs={{0,8},{4,12},{8,0},{12,4},{1,9},{5,13},{9,1},{13,5},{2,10},{6,14},... | collective-permute-start | bytes 184328 | tf_op jit(solution)/shard_map/ppermute | solution.py:544
  15.7 6.7 %collective-permute-start.9 = (f32[2,5,4,384]{3,2,1,0:T(4,128)S(1)}, f32[2,5,4,384]{3,2,1,0:T(4,128)S(1)}, u32[]{:S(2)}, u32[]{:S(2)}) collective-permute-start(f32[2,5,4,384]{3,2,1,0:T(4,128)S(1)} %payload.1.refs_0_), channel_id=1, source_target_pairs={{0,12},{4,8},{8,4},{12,0},{1,13},{5,9},{9,5},{13,1},{2,14},{6,10},... | collective-permute-start | bytes 184328 | tf_op jit(solution)/shard_map/ppermute | solution.py:544
  15.9 15.5 %collective-permute-start.3 = (f32[11,9,2,384]{3,2,1,0:T(2,128)S(1)}, f32[11,9,2,384]{3,2,1,0:T(2,128)S(1)}, u32[]{:S(2)}, u32[]{:S(2)}) collective-permute-start(f32[11,9,2,384]{3,2,1,0:T(2,128)S(1)} %get-tuple-element.41), channel_id=1, source_target_pairs={{0,4},{4,0},{8,12},{12,8},{1,5},{5,1},{9,13},{13,9},{2,6},{6,2},{1... | collective-permute-start | bytes 912392 | tf_op jit(solution)/shard_map/ppermute | solution.py:50
  16.6 14.9 %collective-permute-start.4 = (f32[11,9,2,384]{3,2,1,0:T(2,128)S(1)}, f32[11,9,2,384]{3,2,1,0:T(2,128)S(1)}, u32[]{:S(2)}, u32[]{:S(2)}) collective-permute-start(f32[11,9,2,384]{3,2,1,0:T(2,128)S(1)} %get-tuple-element.42), channel_id=1, source_target_pairs={{4,8},{8,4},{5,9},{9,5},{6,10},{10,6},{7,11},{11,7},{20,24},{24,20... | collective-permute-start | bytes 912392 | tf_op jit(solution)/shard_map/ppermute | solution.py:50
  24.4 7.2 %collective-permute-start.10 = (f32[11,6,2,384]{3,2,1,0:T(2,128)S(1)}, f32[11,6,2,384]{3,2,1,0:T(2,128)S(1)}, u32[]{:S(2)}, u32[]{:S(2)}) collective-permute-start(f32[11,6,2,384]{3,2,1,0:T(2,128)S(1)} %get-tuple-element.51), channel_id=1, source_target_pairs={{0,4},{4,0},{8,12},{12,8},{1,5},{5,1},{9,13},{13,9},{2,6},{6,2},{1... | collective-permute-start | bytes 608264 | tf_op jit(solution)/shard_map/ppermute | solution.py:50
  24.6 7.0 %copy-start = (f32[9]{0:T(128)S(1)}, f32[9]{0:T(128)}, u32[]{:S(2)}) copy-start(f32[9]{0:T(128)} %refs_2_.3) | copy-start | bytes 112
  24.6 6.9 %collective-permute-start.11 = (f32[11,6,2,384]{3,2,1,0:T(2,128)S(1)}, f32[11,6,2,384]{3,2,1,0:T(2,128)S(1)}, u32[]{:S(2)}, u32[]{:S(2)}) collective-permute-start(f32[11,6,2,384]{3,2,1,0:T(2,128)S(1)} %get-tuple-element.52), channel_id=1, source_target_pairs={{4,8},{8,4},{5,9},{9,5},{6,10},{10,6},{7,11},{11,7},{20,24},{24,20... | collective-permute-start | bytes 608264 | tf_op jit(solution)/shard_map/ppermute | solution.py:50
  34.5 7.8 %collective-permute-start.12 = (f32[5,12,2,384]{3,2,1,0:T(2,128)S(1)}, f32[5,12,2,384]{3,2,1,0:T(2,128)S(1)}, u32[]{:S(2)}, u32[]{:S(2)}) collective-permute-start(f32[5,12,2,384]{3,2,1,0:T(2,128)S(1)} %get-tuple-element.58), channel_id=1, source_target_pairs={{0,4},{4,0},{8,12},{12,8},{1,5},{5,1},{9,13},{13,9},{2,6},{6,2},{1... | collective-permute-start | bytes 552968 | tf_op jit(solution)/shard_map/ppermute | solution.py:50
  38.0 4.2 %collective-permute-start.13 = (f32[5,12,2,384]{3,2,1,0:T(2,128)S(1)}, f32[5,12,2,384]{3,2,1,0:T(2,128)S(1)}, u32[]{:S(2)}, u32[]{:S(2)}) collective-permute-start(f32[5,12,2,384]{3,2,1,0:T(2,128)S(1)} %get-tuple-element.59), channel_id=1, source_target_pairs={{4,8},{8,4},{5,9},{9,5},{6,10},{10,6},{7,11},{11,7},{20,24},{24,20... | collective-permute-start | bytes 552968 | tf_op jit(solution)/shard_map/ppermute | solution.py:50
  44.8 3.7 %collective-permute-start.14 = (f32[3,2,360]{2,1,0:T(2,128)S(1)}, f32[3,2,360]{2,1,0:T(2,128)S(1)}, u32[]{:S(2)}, u32[]{:S(2)}) collective-permute-start(f32[3,2,360]{2,1,0:T(2,128)S(1)} %get-tuple-element.63), channel_id=1, source_target_pairs={{0,2},{2,0},{1,3},{3,1},{4,6},{6,4},{5,7},{7,5},{8,10},{10,8},{9,1... | collective-permute-start | bytes 25928 | tf_op jit(solution)/shard_map/ppermute | solution.py:644
